TPU v7x, 256 devices: a whole 4x4x8 slice. The times are simulated.
256 devices in a mesh: agent: 16 (over y, x), tensor: 16 (over z, core).
Axes of the slice: x: 4, y: 4, z: 8, core: 2. Of those that a mesh axis runs over, the one named last changes fastest.
Arguments:
- tokens: bfloat16 [8192, 4096], P('agent', 'tensor'), may hold values from -6 to 6
- valid: int32 [8192], P('agent'), may hold values from 0 to 1, as said below
- latents: bfloat16 [512, 4096], P(None, 'tensor'), may hold values from -6 to 6
- w_query: bfloat16 [4096, 4096], P('agent', 'tensor'), may hold values from -5.625 to 5.625
- w_key: bfloat16 [4096, 4096], P('agent', 'tensor'), may hold values from -0.09375 to 0.09375
- w_value: bfloat16 [4096, 4096], P('agent', 'tensor'), may hold values from -0.09375 to 0.09375
- w_out: bfloat16 [4096, 4096], P('agent', 'tensor'), may hold values from -0.09375 to 0.09375
- gain: float32 [4096], P('tensor'), may hold values from 0.25 to 1.75
Outputs:
- updated: bfloat16 [512, 4096], P(None, 'tensor')
- normed: bfloat16 [512, 4096], P(None, 'tensor')
Inputs may be any that keep to these rules, and one draw needn't show every extreme that they name: Each block of 512 agents has its own share of valid agents, from an eighth to all.
All inputs are finite; a program needn't handle non-finite values.
Results may differ from a plain program's by a relative error of at most 0.0034.
The roundings to bfloat16 on the way count: a program that leaves them out, or rounds other values in their place, can miss the bound.
Values may be sent and summed in bfloat16 or wider, within the bound.
No kernel may reach another device: no remote copies, remote signals or barrier semaphores. Data moves between devices by JAX's collectives and lax.ppermute only.
A program may use at most 64 MiB of HBM per device.

v0:
```python
import jax
import jax.numpy as jnp
from jax import lax
from jax.sharding import PartitionSpec as P

HEAD_DIM = 128


def add_rows(left, piece):
    return jnp.dot(left, piece, preferred_element_type=jnp.float32)


def body(tokens, valid, latents, w_query, w_key, w_value, w_out, gain):
    features = lax.all_gather(tokens, "tensor", axis=1, tiled=True)
    latent_all = lax.all_gather(latents, "tensor", axis=1, tiled=True)
    width = w_key.shape[1]
    agent_rows = features.shape[0]
    lat_rows = latent_all.shape[0]
    head_count = width // HEAD_DIM
    query = add_rows(latent_all, lax.all_gather(w_query, "agent", axis=0, tiled=True))
    keys = add_rows(features, lax.all_gather(w_key, "agent", axis=0, tiled=True))
    values = add_rows(features, lax.all_gather(w_value, "agent", axis=0, tiled=True))
    query = query.astype(jnp.bfloat16).reshape(lat_rows, head_count, HEAD_DIM)
    keys = keys.astype(jnp.bfloat16).reshape(agent_rows, head_count, HEAD_DIM)
    values = values.astype(jnp.bfloat16).reshape(agent_rows, head_count, HEAD_DIM)
    scale = 1.0 / HEAD_DIM**0.5
    scores = jnp.einsum("lhd,ahd->hla", query, keys, preferred_element_type=jnp.float32) * scale
    scores = jnp.where((valid > 0)[None, None, :], scores, jnp.float32(-1000000000.0))
    local_top = jnp.max(scores, axis=2)
    expo = jnp.exp(scores - local_top[..., None])
    local_total = jnp.sum(expo, axis=2)
    local_sums = jnp.einsum(
        "hla,ahd->hld", expo, values.astype(jnp.float32), precision=lax.Precision.HIGHEST
    )
    top = lax.pmax(local_top, "agent")
    factor = jnp.exp(local_top - top)
    total, summed = lax.psum((local_total * factor, local_sums * factor[..., None]), "agent")
    attended = summed / total[..., None]
    attended = attended.transpose(1, 0, 2).reshape(lat_rows, width).astype(jnp.bfloat16)
    attended_all = lax.all_gather(attended, "tensor", axis=1, tiled=True)
    projected = add_rows(attended_all, lax.all_gather(w_out, "agent", axis=0, tiled=True))
    upd = latents.astype(jnp.float32) + projected
    square_total = lax.psum(jnp.sum(upd * upd, axis=1), "tensor")
    mean_sq = square_total / (width * lax.axis_size("tensor"))
    normed = gain[None, :] * upd * lax.rsqrt(mean_sq + 1e-05)[:, None]
    return (upd.astype(jnp.bfloat16), normed.astype(jnp.bfloat16))


def solution(mesh):
    return jax.shard_map(
        body,
        mesh=mesh,
        in_specs=(
            P("agent", "tensor"),
            P("agent"),
            P(None, "tensor"),
            P("agent", "tensor"),
            P("agent", "tensor"),
            P("agent", "tensor"),
            P("agent", "tensor"),
            P("tensor"),
        ),
        out_specs=(P(None, "tensor"), P(None, "tensor")),
        check_vma=False,
    )
```

profile of v0, /device:TPU:1, one launch (start us, length us, event | category | flops | bytes accessed | tf_op | source)
XLA Modules:
  0.0 501.5 jit_solution(1042139625767640476)
XLA Ops:
  7.2 0.0 all-gather.14.cloned.1.call-start
  7.2 0.7 all-gather.14.cloned.1.call-update
  7.9 0.0 all-gather.12.cloned.1.call-start
  7.9 0.7 all-gather.12.cloned.1.call-update
  8.6 0.0 all-gather.10.cloned.1.call-start
  8.7 0.7 all-gather.10.cloned.1.call-update
  9.4 0.0 all-gather.8.cloned.1.call-start
  9.4 0.5 all-gather.8.cloned.1.call-update
  10.0 0.0 all-gather.16.cloned.1.call-start
  10.0 0.5 all-gather.16.cloned.1.call-update
  10.5 0.0 all-reduce.2.cloned.1.call-start
  10.6 0.7 broadcast_compare_fusion
  11.3 52.1 %all-gather.14.cloned.1.call-done = bf16[4096,256]{1,0:T(8,128)(2,1)} async-done(((bf16[256,256]{1,0:T(8,128)(2,1)}), bf16[4096,256]{1,0:T(8,128)(2,1)}) %all-gather.14.cloned.1.call-update) | async-done | bytes 2097168 | tf_op jit(solution)/shard_map/all_gather | solution.py:21
  63.4 51.8 %all-gather.12.cloned.1.call-done = bf16[512,4096]{1,0:T(8,128)(2,1)} async-done(((bf16[512,256]{1,0:T(8,128)(2,1)}), bf16[512,4096]{1,0:T(8,128)(2,1)}) %all-gather.12.cloned.1.call-update) | async-done | bytes 4194320 | tf_op jit(solution)/shard_map/all_gather | solution.py:14
  115.2 4.2 convolution_convert_fusion.1
  119.4 45.5 %all-gather.10.cloned.1.call-done = bf16[4096,256]{1,0:T(8,128)(2,1)} async-done(((bf16[256,256]{1,0:T(8,128)(2,1)}), bf16[4096,256]{1,0:T(8,128)(2,1)}) %all-gather.10.cloned.1.call-update) | async-done | bytes 2097168 | tf_op jit(solution)/shard_map/all_gather | solution.py:20
  164.9 51.7 %all-gather.8.cloned.1.call-done = bf16[512,4096]{1,0:T(8,128)(2,1)} async-done(((bf16[512,256]{1,0:T(8,128)(2,1)}), bf16[512,4096]{1,0:T(8,128)(2,1)}) %all-gather.8.cloned.1.call-update) | async-done | bytes 4194320 | tf_op jit(solution)/shard_map/all_gather | solution.py:15
  216.6 4.2 convolution_convert_fusion.2
  220.7 0.5 fusion
  221.3 32.3 %pmax.7 = f32[2,512]{1,0:T(2,128)S(1)} all-reduce(f32[2,512]{1,0:T(2,128)S(1)} %get-tuple-element.10), channel_id=1, replica_groups=mesh['agent'=16,'tensor'=16] {'agent'}, use_global_device_ids=true, to_apply=%region_1.2 | all-reduce | flops 1024 | bytes 8192 | tf_op jit(solution)/shard_map/pmax | solution.py:35
  253.6 0.5 fusion.1
  254.1 11.9 %all-gather.16.cloned.1.call-done = bf16[4096,256]{1,0:T(8,128)(2,1)} async-done(((bf16[256,256]{1,0:T(8,128)(2,1)}), bf16[4096,256]{1,0:T(8,128)(2,1)}) %all-gather.16.cloned.1.call-update) | async-done | bytes 2097168 | tf_op jit(solution)/shard_map/all_gather | solution.py:22
  266.1 4.2 convolution_convert_fusion
  270.2 0.0 copy-start
  270.2 2.9 fusion.3
  273.1 0.0 all-reduce.2.cloned.1.call-update
  273.1 0.0 all-gather.20.cloned.1.call-start
  273.2 0.7 all-gather.20.cloned.1.call-update
  273.9 0.0 all-gather.18.cloned.1.call-start
  273.9 30.9 %psum.22 = f32[2,512]{1,0:T(2,128)S(1)} all-reduce(f32[2,512]{1,0:T(2,128)S(1)} %get-tuple-element.6), channel_id=1, replica_groups=mesh['agent'=16,'tensor'=16] {'agent'}, use_global_device_ids=true, to_apply=%region_4.5 | all-reduce | flops 1024 | bytes 8192 | tf_op jit(solution)/shard_map/psum | solution.py:37
  304.8 62.7 %all-reduce.2.cloned.1.call-done = f32[2,512,128]{2,1,0:T(8,128)} async-done(((f32[2,512,128]{2,1,0:T(8,128)}), f32[2,512,128]{2,1,0:T(8,128)}) %all-reduce.2.cloned.1.call-update) | async-done | bytes 524304 | tf_op jit(solution)/shard_map/psum | solution.py:37
  367.5 1.2 fusion.8
  368.8 0.9 copy.22
  369.6 0.0 all-gather.18.cloned.1.call-update
  369.7 0.0 copy-done
  369.7 0.1 copy.17
  369.8 0.0 copy-start.1
  369.8 50.3 %all-gather.20.cloned.1.call-done = bf16[4096,256]{1,0:T(8,128)(2,1)} async-done(((bf16[256,256]{1,0:T(8,128)(2,1)}), bf16[4096,256]{1,0:T(8,128)(2,1)}) %all-gather.20.cloned.1.call-update) | async-done | bytes 2097168 | tf_op jit(solution)/shard_map/all_gather | solution.py:41
  420.1 45.4 %all-gather.18.cloned.1.call-done = bf16[512,4096]{0,1:T(8,128)(2,1)} async-done(((bf16[512,256]{0,1:T(8,128)(2,1)}), bf16[512,4096]{0,1:T(8,128)(2,1)}) %all-gather.18.cloned.1.call-update) | async-done | bytes 4194320 | tf_op jit(solution)/shard_map/all_gather | solution.py:40
  465.5 4.2 multiply_reduce_fusion
  469.7 23.2 %psum.23 = f32[512]{0:T(512)S(1)} all-reduce(f32[512]{0:T(512)S(1)} %get-tuple-element.12), channel_id=1, replica_groups=mesh['agent'=16,'tensor'=16] {'tensor'}, use_global_device_ids=true, to_apply=%region_6.7 | all-reduce | flops 512 | bytes 4096 | tf_op jit(solution)/shard_map/psum | solution.py:43
  492.8 0.0 copy-done.1
  492.8 0.1 multiply_convert_fusion
  492.9 0.8 copy.24
  493.8 0.8 copy.23
  (2 shorter events, 0.0 us)
Async XLA Ops:
  7.2 56.2 %all-gather.14.cloned.1.call-start = ((), (), s32[]{:S(2)}) async-start(), calls=%async_computation.3 | async-start | bytes 2228224 | tf_op jit(solution)/shard_map/all_gather | solution.py:21
  7.9 107.3 %all-gather.12.cloned.1.call-start = ((), (), s32[]{:S(2)}) async-start(), calls=%async_computation.2 | async-start | bytes 4456448 | tf_op jit(solution)/shard_map/all_gather | solution.py:14
  8.6 156.2 %all-gather.10.cloned.1.call-start = ((), (), s32[]{:S(2)}) async-start(), calls=%async_computation.1 | async-start | bytes 2228224 | tf_op jit(solution)/shard_map/all_gather | solution.py:20
  9.4 207.2 %all-gather.8.cloned.1.call-start = ((), (), s32[]{:S(2)}) async-start(), calls=%async_computation | async-start | bytes 4456448 | tf_op jit(solution)/shard_map/all_gather | solution.py:15
  10.0 256.1 %all-gather.16.cloned.1.call-start = ((), (), s32[]{:S(2)}) async-start(), calls=%async_computation.4 | async-start | bytes 2228224 | tf_op jit(solution)/shard_map/all_gather | solution.py:22
  10.5 357.0 %all-reduce.2.cloned.1.call-start = ((), (), s32[]{:S(2)}) async-start(), calls=%async_computation.5 | async-start | bytes 1048576 | tf_op jit(solution)/shard_map/psum | solution.py:37
  270.2 99.4 %copy-start = (bf16[512,256]{1,0:T(8,128)(2,1)S(1)}, bf16[512,256]{1,0:T(8,128)(2,1)}, u32[]{:S(2)}) copy-start(bf16[512,256]{1,0:T(8,128)(2,1)} %param.10) | copy-start | bytes 786436
  273.1 147.0 %all-gather.20.cloned.1.call-start = ((), (), s32[]{:S(2)}) async-start(), calls=%async_computation.7 | async-start | bytes 2228224 | tf_op jit(solution)/shard_map/all_gather | solution.py:41
  273.9 191.6 %all-gather.18.cloned.1.call-start = ((), (), s32[]{:S(2)}) async-start(), calls=%async_computation.6 | async-start | bytes 4456448 | tf_op jit(solution)/shard_map/all_gather | solution.py:40
  369.8 123.0 %copy-start.1 = (f32[256]{0:T(256)S(1)}, f32[256]{0:T(256)}, u32[]{:S(2)}) copy-start(f32[256]{0:T(256)} %param.15) | copy-start | bytes 3076
Sparse Core Ops, SparseCore 0:
  10.4 52.8 all-gather.13
  65.1 50.0 all-gather.11
  117.6 47.1 all-gather.9
  166.5 50.0 all-gather.7
  218.8 47.1 all-gather.15
  273.3 94.2 all-reduce.1
  370.2 49.8 all-gather.19
  422.7 42.7 all-gather.17
where the time goes:
time: 503 us; the launch traced here: 501 us
  waiting for transfers between devices  375 us (75%)
  blocking collectives  86.4 us (17%)
  matrix products  20.1 us (4%)
  between operations  14.2 us (3%)
    psum x1, waiting for transfers between devices, body(): lax.psum((local_total * factor, local_sums * factor[..., None]), 'agent')  62.7 us
    all_gather x1, waiting for transfers between devices, body(): lax.all_gather(w_key, 'agent', axis=0, tiled=True)  52.1 us
    all_gather x1, waiting for transfers between devices, body(): features = lax.all_gather(tokens, 'tensor', axis=1, tiled=True)  51.8 us
    all_gather x1, waiting for transfers between devices, body(): latent_all = lax.all_gather(latents, 'tensor', axis=1, tiled=True)  51.7 us
    all_gather x1, waiting for transfers between devices, body(): lax.all_gather(w_out, 'agent', axis=0, tiled=True)  50.3 us
    all_gather x1, waiting for transfers between devices, body(): lax.all_gather(w_query, 'agent', axis=0, tiled=True)  45.5 us
    all_gather x1, waiting for transfers between devices, body(): attended_all = lax.all_gather(attended, 'tensor', axis=1, tiled=True)  45.4 us
    pmax x1, blocking collectives, body(): top = lax.pmax(local_top, 'agent')  32.3 us
  transfers between devices with their start and end apart: 8, of which 8 were waited for; matrix products, arithmetic and copies ran while one was open for 2% of the time, Pallas kernels for 0%

commit v1 on v0

v1 whole, which is shorter than its diff:
```python
import jax
import jax.numpy as jnp
from jax import lax
from jax.experimental import pallas as pl
from jax.experimental.pallas import tpu as pltpu
from jax.sharding import PartitionSpec as P

HEAD_DIM = 128
SIDE = 4
GROUP = 16
STEPS = (0, -1, 1, 2)
BF16 = jnp.bfloat16
F32 = jnp.float32


def hop_x(array, by):
    pairs = [(a, a // SIDE * SIDE + (a + by) % SIDE) for a in range(GROUP)]
    return lax.ppermute(array, "agent", pairs)


def hop_y(array, by):
    pairs = [(a, (a + by * SIDE) % GROUP) for a in range(GROUP)]
    return lax.ppermute(array, "agent", pairs)


def ring(block, hop):
    half = block.shape[0] // 2
    low = hop(block, 1)
    high = hop(block, -1)
    far_top = hop(low[:half], 1)
    far_bottom = hop(high[half:], -1)
    return block, low, high, far_top, far_bottom


def gather_weights(first, second, hop_one, hop_two):
    pair = jnp.concatenate([first, second], axis=0)
    line = jnp.concatenate(ring(pair, hop_one), axis=0)
    return ring(line, hop_two)


def attend_kernel(block_ids, feats, qk0, qk1, qk2, qk3, qk4, vo0, vo1, vo2, vo3, vo4, valid,
                  out, x_all, qk_all, v_all, stat, x_sem, qk_sem, v_sem):
    rows = feats.shape[1] // 2
    depth = feats.shape[2]
    x_copies = []
    for slot in range(GROUP):
        copy = pltpu.make_async_copy(feats.at[block_ids[slot]], x_all.at[slot], x_sem.at[slot])
        x_copies.append(copy)
    qk_parts = ((qk0, 0, 4), (qk1, 4, 4), (qk2, 8, 4), (qk3, 12, 2), (qk4, 14, 2))
    vo_parts = ((vo0, 0, 4), (vo1, 4, 4), (vo2, 8, 4), (vo3, 12, 2), (vo4, 14, 2))
    qk_copies, v_copies = [], []
    for n, (ref, start, count) in enumerate(qk_parts):
        qk_copies.append(pltpu.make_async_copy(
            ref, qk_all.at[pl.ds(start, count)], qk_sem.at[n]))
    for n, (ref, start, count) in enumerate(vo_parts):
        v_copies.append(pltpu.make_async_copy(
            ref.at[:, 0], v_all.at[pl.ds(start, count)], v_sem.at[n]))
    for part in range(SIDE):
        for copy in x_copies[part * SIDE:(part + 1) * SIDE]:
            copy.start()
        if part < 3:
            qk_copies[part].start()
        else:
            qk_copies[3].start()
            qk_copies[4].start()
    for copy in v_copies:
        copy.start()

    def columns(first, top):
        return jnp.concatenate(
            [x_all[first + j, pl.ds(top, rows), :] for j in range(SIDE)], axis=1)

    query = keys = values = None
    for part in range(SIDE):
        for copy in x_copies[part * SIDE:(part + 1) * SIDE]:
            copy.wait()
        if part < 3:
            qk_copies[part].wait()
        else:
            qk_copies[3].wait()
            qk_copies[4].wait()
        w_q = qk_all[pl.ds(part * SIDE, SIDE), 0].reshape(SIDE * depth, -1)
        w_k = qk_all[pl.ds(part * SIDE, SIDE), 1].reshape(SIDE * depth, -1)
        more_q = jnp.dot(columns(part * SIDE, rows), w_q, preferred_element_type=F32)
        more_k = jnp.dot(columns(part * SIDE, 0), w_k, preferred_element_type=F32)
        query = more_q if query is None else query + more_q
        keys = more_k if keys is None else keys + more_k
    for copy in v_copies:
        copy.wait()
    for part in range(SIDE):
        w_v = jnp.concatenate([v_all[j * SIDE + part] for j in range(SIDE)], axis=0)
        more_v = jnp.dot(columns(part * SIDE, 0), w_v, preferred_element_type=F32)
        values = more_v if values is None else values + more_v
    query = query.astype(BF16)
    keys = keys.astype(BF16)
    values = values.astype(BF16)
    scale = 1.0 / HEAD_DIM**0.5
    keep = valid[...] > 0
    lane = lax.broadcasted_iota(jnp.int32, (rows, HEAD_DIM), 1)
    tile = lax.broadcasted_iota(jnp.int32, (rows, HEAD_DIM), 0) // 8 % 4
    packed = jnp.zeros((rows, HEAD_DIM), F32)
    chunk = rows // GROUP
    for head in range(2):
        cols = slice(head * HEAD_DIM, (head + 1) * HEAD_DIM)
        scores = lax.dot_general(query[:, cols], keys[:, cols], (((1,), (1,)), ((), ())),
                                 preferred_element_type=F32) * scale
        scores = jnp.where(keep, scores, jnp.float32(-1000000000.0))
        top = jnp.max(scores, axis=1, keepdims=True)
        expo = jnp.exp(scores - top)
        total = jnp.sum(expo, axis=1, keepdims=True)
        coarse = expo.astype(BF16)
        fine = (expo - coarse.astype(F32)).astype(BF16)
        summed = jnp.dot(coarse, values[:, cols], preferred_element_type=F32)
        summed += jnp.dot(fine, values[:, cols], preferred_element_type=F32)
        out[:, pl.ds(head * chunk, chunk), :] = summed.reshape(GROUP, chunk, HEAD_DIM)
        packed = jnp.where(lane == 4 * tile + 2 * head, top, packed)
        packed = jnp.where(lane == 4 * tile + 2 * head + 1, total, packed)
    stat[...] = packed.reshape(GROUP, chunk // 8, 8, HEAD_DIM)
    out[:, pl.ds(2 * chunk, 8), :] = stat[:, 0] + stat[:, 1] + stat[:, 2] + stat[:, 3]


def combine_kernel(parts, out):
    chunk = out.shape[1]
    for tile in range(chunk // 8):
        for head in range(2):
            at = 4 * tile + 2 * head
            rows = pl.ds(2 * chunk, 8)
            tops = parts[:, rows, at:at + 1]
            totals = parts[:, rows, at + 1:at + 2]
            top = jnp.max(tops, axis=0, keepdims=True)
            factor = jnp.exp(tops - top)
            total = jnp.sum(totals * factor, axis=0)
            summed = jnp.sum(parts[:, pl.ds(head * chunk + 8 * tile, 8), :] * factor, axis=0)
            out_tile = (summed / total).astype(BF16)
            for t in range(GROUP):
                out[t, pl.ds(8 * tile, 8), head * HEAD_DIM:(head + 1) * HEAD_DIM] = out_tile


def project_kernel(block_ids, attended, vo0, vo1, vo2, vo3, vo4, latents, upd, squares):
    refs = ((vo0, 0, 4), (vo1, 4, 4), (vo2, 8, 4), (vo3, 12, 2), (vo4, 14, 2))
    total = latents[...].astype(F32)
    chunk = latents.shape[0]
    for ref, start, count in refs:
        for at in range(count):
            slot = start + at
            block = block_ids[slot % SIDE * SIDE + slot // SIDE]
            total += jnp.dot(attended[block], ref[at, 1], preferred_element_type=F32)
    upd[...] = total
    square = jnp.sum(total * total, axis=1, keepdims=True)
    lane = lax.broadcasted_iota(jnp.int32, (8, HEAD_DIM), 1)
    packed = jnp.zeros((8, HEAD_DIM), F32)
    for tile in range(chunk // 8):
        packed = jnp.where(lane == tile, square[8 * tile:8 * tile + 8], packed)
    for t in range(GROUP):
        squares[t] = packed


def finish_kernel(width, squares, upd, gain, out):
    total = jnp.sum(squares[...], axis=0)
    chunk = upd.shape[0]
    for tile in range(chunk // 8):
        rows = pl.ds(8 * tile, 8)
        mean_sq = total[:, tile:tile + 1] / width
        u = upd[rows, :]
        normed = gain[...] * u * lax.rsqrt(mean_sq + 1e-05)
        for a in range(GROUP):
            out[a, 0, rows, :] = u.astype(BF16)
            out[a, 1, rows, :] = normed.astype(BF16)


def whole(count):
    return [pl.BlockSpec(memory_space=pltpu.VMEM)] * count


def body(tokens, valid, latents, w_query, w_key, w_value, w_out, gain):
    me = lax.axis_index("agent")
    rows, depth = tokens.shape
    chunk = latents.shape[0] // GROUP
    width = depth * lax.axis_size("tensor")
    both = jnp.concatenate([tokens, latents], axis=0)
    feats = lax.all_gather(both, "tensor", axis=0, tiled=False)
    qk = gather_weights(w_query, w_key, hop_x, hop_y)
    vo = gather_weights(w_value, w_out, hop_y, hop_x)
    qk = [part.reshape(-1, 2, depth, depth) for part in qk]
    vo = [part.reshape(-1, 2, depth, depth) for part in vo]
    y, x = me // SIDE, me % SIDE
    block_ids = jnp.stack(
        [(y + i + SIDE) % SIDE * SIDE + (x + j + SIDE) % SIDE for i in STEPS for j in STEPS]
    ).astype(jnp.int32)
    smem = pl.BlockSpec(memory_space=pltpu.SMEM)
    anywhere = pl.BlockSpec(memory_space=pl.ANY)
    partial = pl.pallas_call(
        attend_kernel,
        out_shape=jax.ShapeDtypeStruct((GROUP, 2 * chunk + 8, HEAD_DIM), F32),
        in_specs=[smem] + [anywhere] * 11 + whole(1),
        out_specs=whole(1)[0],
        scratch_shapes=[
            pltpu.VMEM((GROUP, 2 * rows, depth), BF16),
            pltpu.VMEM((GROUP, 2, depth, depth), BF16),
            pltpu.VMEM((GROUP, depth, depth), BF16),
            pltpu.VMEM((GROUP, chunk // 8, 8, HEAD_DIM), F32),
            pltpu.SemaphoreType.DMA((GROUP,)),
            pltpu.SemaphoreType.DMA((5,)),
            pltpu.SemaphoreType.DMA((5,)),
        ],
        compiler_params=pltpu.CompilerParams(vmem_limit_bytes=40 * 2**20),
        name="attend",
    )(block_ids, feats, *qk, *vo, valid.reshape(1, rows))
    partial = lax.all_to_all(partial, "agent", 0, 0)
    attended = pl.pallas_call(
        combine_kernel,
        out_shape=jax.ShapeDtypeStruct((GROUP, chunk, depth), BF16),
        in_specs=whole(1),
        out_specs=whole(1)[0],
        name="combine",
    )(partial)
    attended = lax.all_to_all(attended, "tensor", 0, 0)
    mine = lax.dynamic_slice_in_dim(latents, me * chunk, chunk, axis=0)
    upd, squares = pl.pallas_call(
        project_kernel,
        out_shape=(jax.ShapeDtypeStruct((chunk, depth), F32),
                   jax.ShapeDtypeStruct((GROUP, 8, HEAD_DIM), F32)),
        in_specs=[smem] + whole(7),
        out_specs=tuple(whole(2)),
        compiler_params=pltpu.CompilerParams(vmem_limit_bytes=40 * 2**20),
        name="project",
    )(block_ids, attended, *vo, mine)
    squares = lax.all_to_all(squares, "tensor", 0, 0)
    out = pl.pallas_call(
        lambda *refs: finish_kernel(width, *refs),
        out_shape=jax.ShapeDtypeStruct((GROUP, 2, chunk, depth), BF16),
        in_specs=whole(3),
        out_specs=whole(1)[0],
        name="finish",
    )(squares, upd, gain.reshape(1, depth))
    out = lax.all_to_all(out, "agent", 0, 0)
    return out[:, 0].reshape(-1, depth), out[:, 1].reshape(-1, depth)


def solution(mesh):
    return jax.shard_map(
        body,
        mesh=mesh,
        in_specs=(
            P("agent", "tensor"),
            P("agent"),
            P(None, "tensor"),
            P("agent", "tensor"),
            P("agent", "tensor"),
            P("agent", "tensor"),
            P("agent", "tensor"),
            P("tensor"),
        ),
        out_specs=(P(None, "tensor"), P(None, "tensor")),
        check_vma=False,
    )
```

time: 503 us -> 164 us (0.33)
  waiting for transfers between devices: 375 us -> 40.1 us
  blocking collectives: 86.4 us -> 39.8 us
  starting transfers between devices: 0.31 us -> 37.7 us
  matrix products: 20.1 us -> 0 us
  Pallas kernels: 0 us -> 15.5 us
  local copies, waits for them, and re-layouts: 2.69 us -> 14.5 us
    all_gather x7 -> x1, waiting for transfers between devices: 309 us -> 0.01 us  [body(): feats = lax.all_gather(both, 'tensor', axis=0, tiled=False)]
    psum x1 -> x0, waiting for transfers between devices: 62.7 us -> none  [body(): lax.psum((local_total * factor, local_sums * factor[..., None]), 'agent')]
    psum x2 -> x0, blocking collectives: 54.1 us -> none  [the longest x1 30.9 us: body(): lax.psum((local_total * factor, local_sums * factor[..., None]), 'agent')]
    all_to_all x0 -> x3, blocking collectives: none -> 39.8 us  [the longest x1 14.7 us: body(): out = lax.all_to_all(out, 'agent', 0, 0)]
    pmax x1 -> x0, blocking collectives: 32.3 us -> none  [body(): top = lax.pmax(local_top, 'agent')]
    ppermute x0 -> x16, waiting for transfers between devices: none -> 29.1 us  [the longest x8 22 us: hop_x(): return lax.ppermute(array, 'agent', pairs)]
    ppermute x0 -> x16, starting transfers between devices: none -> 23.5 us  [the longest x8 12.1 us: hop_y(): return lax.ppermute(array, 'agent', pairs)]
    dot_general x6 -> x0, matrix products: 20.1 us -> none  [the longest x4 16.6 us: add_rows(): return jnp.dot(left, piece, preferred_element_type=jnp.float32)]
  transfers between devices with their start and end apart: 8 -> 18, of which waited for: 8 -> 7; matrix products, arithmetic and copies ran while one was open for 2% -> 5% of each run, Pallas kernels for 0% -> 0%
where the time goes in v1:
time: 164 us
  waiting for transfers between devices  40.1 us (24%)
  blocking collectives  39.8 us (24%)
  starting transfers between devices  37.7 us (23%)
  Pallas kernels  15.5 us (9%)
  local copies, waits for them, and re-layouts  14.5 us (9%)
  between operations  14.2 us (9%)
  other arithmetic  1.9 us (1%)
    ppermute x8, waiting for transfers between devices, hop_x(): return lax.ppermute(array, 'agent', pairs)  22 us
    all_to_all x1, blocking collectives, body(): out = lax.all_to_all(out, 'agent', 0, 0)  14.7 us
    all_to_all x1, blocking collectives, body(): partial = lax.all_to_all(partial, 'agent', 0, 0)  14.6 us
    all_to_all x1, starting transfers between devices, body(): attended = lax.all_to_all(attended, 'tensor', 0, 0)  14.1 us
    ppermute x8, starting transfers between devices, hop_y(): return lax.ppermute(array, 'agent', pairs)  12.1 us
    ppermute x8, starting transfers between devices, hop_x(): return lax.ppermute(array, 'agent', pairs)  11.4 us
    all_to_all x1, waiting for transfers between devices, body(): attended = lax.all_to_all(attended, 'tensor', 0, 0)  11 us
    all_to_all x1, blocking collectives, body(): squares = lax.all_to_all(squares, 'tensor', 0, 0)  10.5 us
  transfers between devices with their start and end apart: 18, of which 7 were waited for; matrix products, arithmetic and copies ran while one was open for 5% of the time, Pallas kernels for 0%

profile of v1, /device:TPU:1, one launch (start us, length us, event | category | flops | bytes accessed | tf_op | source)
XLA Modules:
  0.0 163.8 jit_solution(7028827350900473214)
XLA Ops:
  7.2 0.0 copy-start.7
  7.2 0.0 all-gather.3.cloned.1.call-start
  7.2 1.9 %pad_maximum_fusion = bf16[1024,256]{1,0:T(8,128)(2,1)} fusion(bf16[512,256]{1,0:T(8,128)(2,1)} %param.10, bf16[512,256]{1,0:T(8,128)(2,1)} %param.8), kind=kLoop, calls=%fused_computation | loop fusion | flops 1048576 | bytes 1048576 | tf_op jit(solution)/shard_map/concatenate | solution.py:180
  9.1 0.0 all-gather.3.cloned.1.call-update
  9.1 0.9 constant_dynamic-update-slice_fusion.9
  10.1 0.9 constant_dynamic-update-slice_fusion.8
  11.0 2.2 %collective-permute-start.8 = (bf16[512,256]{1,0:T(8,128)(2,1)S(1)}, bf16[512,256]{1,0:T(8,128)(2,1)S(1)}, u32[]{:S(2)}, u32[]{:S(2)}) collective-permute-start(bf16[512,256]{1,0:T(8,128)(2,1)S(1)} %get-tuple-element.8), channel_id=1, source_target_pairs={{0,64},{16,80},{32,96},{48,112},{64,128},{80,144},{96,160},{112,17... | collective-permute-start | bytes 786440 | tf_op jit(solution)/shard_map/ppermute | solution.py:23
  13.2 1.5 collective-permute-start.9
  14.7 0.9 constant_dynamic-update-slice_fusion.1
  15.7 0.9 constant_dynamic-update-slice_fusion
  16.6 1.3 collective-permute-start
  17.9 1.5 collective-permute-start.1
  19.3 0.0 collective-permute-done.8
  19.4 0.9 collective-permute-start.10
  20.3 0.0 collective-permute-done.9
  20.3 1.9 %collective-permute-start.11 = (bf16[256,256]{1,0:T(8,128)(2,1)S(1)}, bf16[256,256]{1,0:T(8,128)(2,1)S(1)}, u32[]{:S(2)}, u32[]{:S(2)}) collective-permute-start(bf16[256,256]{1,0:T(8,128)(2,1)S(1)} %slice.45), channel_id=1, source_target_pairs={{0,192},{16,208},{32,224},{48,240},{64,0},{80,16},{96,32},{112,48}... | collective-permute-start | bytes 393224 | tf_op jit(solution)/shard_map/ppermute | solution.py:23
  22.2 0.9 collective-permute-done
  23.1 1.5 collective-permute-start.2
  24.6 0.0 collective-permute-done.1
  24.6 1.5 collective-permute-start.3
  26.2 0.0 collective-permute-done.10
  26.2 0.0 collective-permute-done.11
  26.2 0.7 collective-permute-start.12
  26.9 2.1 %collective-permute-start.13 = (bf16[2048,256]{1,0:T(8,128)(2,1)S(1)}, bf16[2048,256]{1,0:T(8,128)(2,1)S(1)}, u32[]{:S(2)}, u32[]{:S(2)}) collective-permute-start(bf16[2048,256]{1,0:T(8,128)(2,1)S(1)} %constant_dynamic-update-slice_fusion.10), channel_id=1, source_target_pairs={{0,48},{16,0},{32,16},{48,32},{64,112},{80,64},{96,80},{112,96},{1... | collective-permute-start | bytes 3145736 | tf_op jit(solution)/shard_map/ppermute | solution.py:18
  29.0 0.0 collective-permute-done.2
  29.0 0.0 collective-permute-done.3
  29.0 1.0 collective-permute-start.4
  30.0 1.8 %collective-permute-start.5 = (bf16[2048,256]{1,0:T(8,128)(2,1)S(1)}, bf16[2048,256]{1,0:T(8,128)(2,1)S(1)}, u32[]{:S(2)}, u32[]{:S(2)}) collective-permute-start(bf16[2048,256]{1,0:T(8,128)(2,1)S(1)} %constant_dynamic-update-slice_fusion.2), channel_id=1, source_target_pairs={{0,192},{16,208},{32,224},{48,240},{64,0},{80,16},{96,32},{112,48}... | collective-permute-start | bytes 3145736 | tf_op jit(solution)/shard_map/ppermute | solution.py:23
  31.8 18.8 %collective-permute-done.12 = bf16[2048,256]{1,0:T(8,128)(2,1)S(1)} collective-permute-done((bf16[2048,256]{1,0:T(8,128)(2,1)S(1)}, bf16[2048,256]{1,0:T(8,128)(2,1)S(1)}, u32[]{:S(2)}, u32[]{:S(2)}) %collective-permute-start.12) | collective-permute-done | bytes 1048608 | tf_op jit(solution)/shard_map/ppermute | solution.py:18
  50.7 0.9 slice.46
  51.5 0.2 collective-permute-start.14
  51.7 0.0 collective-permute-done.13
  51.7 0.9 slice.47
  52.6 2.8 %collective-permute-start.15 = (bf16[1024,256]{1,0:T(8,128)(2,1)}, bf16[1024,256]{1,0:T(8,128)(2,1)}, u32[]{:S(2)}, u32[]{:S(2)}) collective-permute-start(bf16[1024,256]{1,0:T(8,128)(2,1)} %slice.47), channel_id=1, source_target_pairs={{0,48},{16,0},{32,16},{48,32},{64,112},{80,64},{96,80},{112,96},{1... | collective-permute-start | bytes 1572872 | tf_op jit(solution)/shard_map/ppermute | solution.py:18
  55.3 0.0 collective-permute-done.4
  55.3 0.8 slice.42
  56.2 1.0 copy-done
  57.2 1.8 %collective-permute-start.6 = (bf16[1024,256]{1,0:T(8,128)(2,1)}, bf16[1024,256]{1,0:T(8,128)(2,1)}, u32[]{:S(2)}, u32[]{:S(2)}) collective-permute-start(bf16[1024,256]{1,0:T(8,128)(2,1)} %slice.42), channel_id=1, source_target_pairs={{0,64},{16,80},{32,96},{48,112},{64,128},{80,144},{96,160},{112,17... | collective-permute-start | bytes 1572872 | tf_op jit(solution)/shard_map/ppermute | solution.py:23
  59.0 0.0 collective-permute-done.5
  59.0 0.9 slice.43
  59.8 1.0 copy-done.2
  60.8 0.9 collective-permute-start.7
  61.7 0.1 stack.67.block_ids
  61.8 1.4 collective-permute-done.14
  63.2 0.9 collective-permute-done.15
  64.1 4.0 %collective-permute-done.6 = bf16[1024,256]{1,0:T(8,128)(2,1)} collective-permute-done((bf16[1024,256]{1,0:T(8,128)(2,1)}, bf16[1024,256]{1,0:T(8,128)(2,1)}, u32[]{:S(2)}, u32[]{:S(2)}) %collective-permute-start.6) | collective-permute-done | bytes 524320 | tf_op jit(solution)/shard_map/ppermute | solution.py:23
  68.1 3.1 %collective-permute-done.7 = bf16[1024,256]{1,0:T(8,128)(2,1)} collective-permute-done((bf16[1024,256]{1,0:T(8,128)(2,1)}, bf16[1024,256]{1,0:T(8,128)(2,1)}, u32[]{:S(2)}, u32[]{:S(2)}) %collective-permute-start.7) | collective-permute-done | bytes 524320 | tf_op jit(solution)/shard_map/ppermute | solution.py:23
  71.2 0.0 copy-done.7
  71.2 1.2 copy-done.1
  72.4 1.2 copy-done.3
  73.6 1.2 copy-done.5
  74.9 9.6 %attend.1 = f32[16,72,128]{2,1,0:T(8,128)S(1)} custom-call(s32[16]{0:T(128)S(1)} %stack.67.block_ids, bf16[16,1024,256]{2,1,0:T(8,128)(2,1)} %bitcast.41, bf16[4,2,256,256]{3,2,1,0:T(8,128)(2,1)S(1)} %bitcast.39, bf16[4,2,256,256]{3,2,1,0:T(8,128)(2,1)S(1)} %bitcast.37, bf16[4,2,256,256]{3,2,1,0:T(8,128)(2,1)S(1)} %bitcast.38, ...), custom_call_target="tpu_custom_call" | custom-call | tf_op jit(solution)/shard_map/attend/pallas_call | solution.py:192
  84.4 14.6 %all_to_all.20.parts = f32[16,72,128]{2,1,0:T(8,128)} all-to-all(f32[16,72,128]{2,1,0:T(8,128)S(1)} %attend.1), channel_id=1, replica_groups=mesh['agent'=16,'tensor'=16] {'agent'}, dimensions={0} | all-to-all | bytes 1179648 | tf_op jit(solution)/shard_map/all_to_all | solution.py:209
  99.1 2.4 %combine.1 = bf16[16,32,256]{2,1,0:T(8,128)(2,1)} custom-call(f32[16,72,128]{2,1,0:T(8,128)} %all_to_all.20.parts), custom_call_target="tpu_custom_call" | custom-call | tf_op jit(solution)/shard_map/combine/pallas_call | solution.py:210
  101.5 14.1 %all-to-all-start.1 = ((bf16[16,32,256]{2,1,0:T(8,128)(2,1)}), bf16[16,32,256]{2,1,0:T(8,128)(2,1)S(1)}, u32[]{:S(2)}, u32[]{:S(2)}) async-start(bf16[16,32,256]{2,1,0:T(8,128)(2,1)} %combine.1), calls=%async_computation.1 | async-start | bytes 524288 | tf_op jit(solution)/shard_map/all_to_all | solution.py:217
  115.6 0.7 constant_dynamic-slice_fusion.latents
  116.4 11.0 %all-to-all-done.1.attended = bf16[16,32,256]{2,1,0:T(8,128)(2,1)S(1)} async-done(((bf16[16,32,256]{2,1,0:T(8,128)(2,1)}), bf16[16,32,256]{2,1,0:T(8,128)(2,1)S(1)}, u32[]{:S(2)}, u32[]{:S(2)}) %all-to-all-start.1) | async-done | bytes 262176 | tf_op jit(solution)/shard_map/all_to_all | solution.py:217
  127.3 1.8 %project.1 = (f32[32,256]{1,0:T(8,128)S(1)}, f32[16,8,128]{2,1,0:T(8,128)S(1)}) custom-call(s32[16]{0:T(128)S(1)} %stack.67.block_ids, bf16[16,32,256]{2,1,0:T(8,128)(2,1)S(1)} %all-to-all-done.1.attended, bf16[4,2,256,256]{3,2,1,0:T(8,128)(2,1)S(1)} %bitcast.36, bf16[4,2,256,256]{3,2,1,0:T(8,128)(2,1)S(1)} %bitcast.32, ...), custom_call_target="tpu_custom_call" | custom-call | tf_op jit(solution)/shard_map/project/pallas_call | solution.py:219
  129.1 0.0 copy-start.6
  129.1 10.5 %all_to_all.21.refs_0_ = f32[16,8,128]{2,1,0:T(8,128)} all-to-all(f32[16,8,128]{2,1,0:T(8,128)S(1)} %get-tuple-element.4), channel_id=1, replica_groups=mesh['agent'=16,'tensor'=16] {'tensor'}, dimensions={0} | all-to-all | bytes 131072 | tf_op jit(solution)/shard_map/all_to_all | solution.py:228
  139.6 0.0 copy-done.6
  139.7 1.8 %finish.1 = bf16[16,2,32,256]{3,2,1,0:T(8,128)(2,1)} custom-call(f32[16,8,128]{2,1,0:T(8,128)} %all_to_all.21.refs_0_, f32[32,256]{1,0:T(8,128)} %copy-done.6, f32[1,256]{1,0:T(1,128)} %bitcast.44), custom_call_target="tpu_custom_call" | custom-call | tf_op jit(solution)/shard_map/finish/pallas_call | solution.py:229
  141.4 14.7 %all_to_all.22 = bf16[16,2,32,256]{3,2,1,0:T(8,128)(2,1)S(1)} all-to-all(bf16[16,2,32,256]{3,2,1,0:T(8,128)(2,1)} %finish.1), channel_id=1, replica_groups=mesh['agent'=16,'tensor'=16] {'agent'}, dimensions={0} | all-to-all | bytes 1048576 | tf_op jit(solution)/shard_map/all_to_all | solution.py:236
  156.1 0.8 fusion
  (20 shorter events, 0.2 us)
Async XLA Ops:
  7.2 64.0 %copy-start.7 = (s32[512]{0:T(512)S(1)}, s32[512]{0:T(512)}, u32[]{:S(2)}) copy-start(s32[512]{0:T(512)} %param.9) | copy-start | bytes 6148
  7.2 64.0 %all-gather.3.cloned.1.call-start = ((), (), s32[]{:S(2)}) async-start(), calls=%async_computation.4 | async-start | bytes 8912896 | tf_op jit(solution)/shard_map/all_gather | solution.py:181
  11.0 8.3 %collective-permute-start.8 = (bf16[512,256]{1,0:T(8,128)(2,1)S(1)}, bf16[512,256]{1,0:T(8,128)(2,1)S(1)}, u32[]{:S(2)}, u32[]{:S(2)}) collective-permute-start(bf16[512,256]{1,0:T(8,128)(2,1)S(1)} %get-tuple-element.8), channel_id=1, source_target_pairs={{0,64},{16,80},{32,96},{48,112},{64,128},{80,144},{96,160},{112,17... | collective-permute-start | bytes 786440 | tf_op jit(solution)/shard_map/ppermute | solution.py:23
  13.2 7.1 %collective-permute-start.9 = (bf16[512,256]{1,0:T(8,128)(2,1)S(1)}, bf16[512,256]{1,0:T(8,128)(2,1)S(1)}, u32[]{:S(2)}, u32[]{:S(2)}) collective-permute-start(bf16[512,256]{1,0:T(8,128)(2,1)S(1)} %get-tuple-element.8), channel_id=1, source_target_pairs={{0,192},{16,208},{32,224},{48,240},{64,0},{80,16},{96,32},{112,48}... | collective-permute-start | bytes 786440 | tf_op jit(solution)/shard_map/ppermute | solution.py:23
  16.6 6.5 %collective-permute-start = (bf16[512,256]{1,0:T(8,128)(2,1)S(1)}, bf16[512,256]{1,0:T(8,128)(2,1)S(1)}, u32[]{:S(2)}, u32[]{:S(2)}) collective-permute-start(bf16[512,256]{1,0:T(8,128)(2,1)S(1)} %get-tuple-element.12), channel_id=1, source_target_pairs={{0,16},{16,32},{32,48},{48,0},{64,80},{80,96},{96,112},{112,64},{1... | collective-permute-start | bytes 786440 | tf_op jit(solution)/shard_map/ppermute | solution.py:18
  17.9 6.7 %collective-permute-start.1 = (bf16[512,256]{1,0:T(8,128)(2,1)S(1)}, bf16[512,256]{1,0:T(8,128)(2,1)S(1)}, u32[]{:S(2)}, u32[]{:S(2)}) collective-permute-start(bf16[512,256]{1,0:T(8,128)(2,1)S(1)} %get-tuple-element.12), channel_id=1, source_target_pairs={{0,48},{16,0},{32,16},{48,32},{64,112},{80,64},{96,80},{112,96},{1... | collective-permute-start | bytes 786440 | tf_op jit(solution)/shard_map/ppermute | solution.py:18
  19.4 6.8 %collective-permute-start.10 = (bf16[256,256]{1,0:T(8,128)(2,1)S(1)}, bf16[256,256]{1,0:T(8,128)(2,1)S(1)}, u32[]{:S(2)}, u32[]{:S(2)}) collective-permute-start(bf16[256,256]{1,0:T(8,128)(2,1)S(1)} %slice.44), channel_id=1, source_target_pairs={{0,64},{16,80},{32,96},{48,112},{64,128},{80,144},{96,160},{112,17... | collective-permute-start | bytes 393224 | tf_op jit(solution)/shard_map/ppermute | solution.py:23
  20.3 5.9 %collective-permute-start.11 = (bf16[256,256]{1,0:T(8,128)(2,1)S(1)}, bf16[256,256]{1,0:T(8,128)(2,1)S(1)}, u32[]{:S(2)}, u32[]{:S(2)}) collective-permute-start(bf16[256,256]{1,0:T(8,128)(2,1)S(1)} %slice.45), channel_id=1, source_target_pairs={{0,192},{16,208},{32,224},{48,240},{64,0},{80,16},{96,32},{112,48}... | collective-permute-start | bytes 393224 | tf_op jit(solution)/shard_map/ppermute | solution.py:23
  23.1 5.9 %collective-permute-start.2 = (bf16[256,256]{1,0:T(8,128)(2,1)S(1)}, bf16[256,256]{1,0:T(8,128)(2,1)S(1)}, u32[]{:S(2)}, u32[]{:S(2)}) collective-permute-start(bf16[256,256]{1,0:T(8,128)(2,1)S(1)} %slice.40), channel_id=1, source_target_pairs={{0,16},{16,32},{32,48},{48,0},{64,80},{80,96},{96,112},{112,64},{1... | collective-permute-start | bytes 393224 | tf_op jit(solution)/shard_map/ppermute | solution.py:18
  24.6 4.4 %collective-permute-start.3 = (bf16[256,256]{1,0:T(8,128)(2,1)S(1)}, bf16[256,256]{1,0:T(8,128)(2,1)S(1)}, u32[]{:S(2)}, u32[]{:S(2)}) collective-permute-start(bf16[256,256]{1,0:T(8,128)(2,1)S(1)} %slice.41), channel_id=1, source_target_pairs={{0,48},{16,0},{32,16},{48,32},{64,112},{80,64},{96,80},{112,96},{1... | collective-permute-start | bytes 393224 | tf_op jit(solution)/shard_map/ppermute | solution.py:18
  26.2 24.4 %collective-permute-start.12 = (bf16[2048,256]{1,0:T(8,128)(2,1)S(1)}, bf16[2048,256]{1,0:T(8,128)(2,1)S(1)}, u32[]{:S(2)}, u32[]{:S(2)}) collective-permute-start(bf16[2048,256]{1,0:T(8,128)(2,1)S(1)} %constant_dynamic-update-slice_fusion.10), channel_id=1, source_target_pairs={{0,16},{16,32},{32,48},{48,0},{64,80},{80,96},{96,112},{112,64},{1... | collective-permute-start | bytes 3145736 | tf_op jit(solution)/shard_map/ppermute | solution.py:18
  26.9 24.8 %collective-permute-start.13 = (bf16[2048,256]{1,0:T(8,128)(2,1)S(1)}, bf16[2048,256]{1,0:T(8,128)(2,1)S(1)}, u32[]{:S(2)}, u32[]{:S(2)}) collective-permute-start(bf16[2048,256]{1,0:T(8,128)(2,1)S(1)} %constant_dynamic-update-slice_fusion.10), channel_id=1, source_target_pairs={{0,48},{16,0},{32,16},{48,32},{64,112},{80,64},{96,80},{112,96},{1... | collective-permute-start | bytes 3145736 | tf_op jit(solution)/shard_map/ppermute | solution.py:18
  29.0 30.8 %copy-start.4 = (bf16[2048,256]{1,0:T(8,128)(2,1)}, bf16[2048,256]{1,0:T(8,128)(2,1)S(1)}, u32[]{:S(2)}) copy-start(bf16[2048,256]{1,0:T(8,128)(2,1)S(1)} %constant_dynamic-update-slice_fusion.2) | copy-start | bytes 3145732
  29.0 26.3 %collective-permute-start.4 = (bf16[2048,256]{1,0:T(8,128)(2,1)S(1)}, bf16[2048,256]{1,0:T(8,128)(2,1)S(1)}, u32[]{:S(2)}, u32[]{:S(2)}) collective-permute-start(bf16[2048,256]{1,0:T(8,128)(2,1)S(1)} %constant_dynamic-update-slice_fusion.2), channel_id=1, source_target_pairs={{0,64},{16,80},{32,96},{48,112},{64,128},{80,144},{96,160},{112,17... | collective-permute-start | bytes 3145736 | tf_op jit(solution)/shard_map/ppermute | solution.py:23
  30.0 28.9 %collective-permute-start.5 = (bf16[2048,256]{1,0:T(8,128)(2,1)S(1)}, bf16[2048,256]{1,0:T(8,128)(2,1)S(1)}, u32[]{:S(2)}, u32[]{:S(2)}) collective-permute-start(bf16[2048,256]{1,0:T(8,128)(2,1)S(1)} %constant_dynamic-update-slice_fusion.2), channel_id=1, source_target_pairs={{0,192},{16,208},{32,224},{48,240},{64,0},{80,16},{96,32},{112,48}... | collective-permute-start | bytes 3145736 | tf_op jit(solution)/shard_map/ppermute | solution.py:23
  51.5 11.7 %collective-permute-start.14 = (bf16[1024,256]{1,0:T(8,128)(2,1)}, bf16[1024,256]{1,0:T(8,128)(2,1)}, u32[]{:S(2)}, u32[]{:S(2)}) collective-permute-start(bf16[1024,256]{1,0:T(8,128)(2,1)} %slice.46), channel_id=1, source_target_pairs={{0,16},{16,32},{32,48},{48,0},{64,80},{80,96},{96,112},{112,64},{1... | collective-permute-start | bytes 1572872 | tf_op jit(solution)/shard_map/ppermute | solution.py:18
  52.6 11.5 %collective-permute-start.15 = (bf16[1024,256]{1,0:T(8,128)(2,1)}, bf16[1024,256]{1,0:T(8,128)(2,1)}, u32[]{:S(2)}, u32[]{:S(2)}) collective-permute-start(bf16[1024,256]{1,0:T(8,128)(2,1)} %slice.47), channel_id=1, source_target_pairs={{0,48},{16,0},{32,16},{48,32},{64,112},{80,64},{96,80},{112,96},{1... | collective-permute-start | bytes 1572872 | tf_op jit(solution)/shard_map/ppermute | solution.py:18
  56.2 1.0 copy-start
  57.2 10.9 %collective-permute-start.6 = (bf16[1024,256]{1,0:T(8,128)(2,1)}, bf16[1024,256]{1,0:T(8,128)(2,1)}, u32[]{:S(2)}, u32[]{:S(2)}) collective-permute-start(bf16[1024,256]{1,0:T(8,128)(2,1)} %slice.42), channel_id=1, source_target_pairs={{0,64},{16,80},{32,96},{48,112},{64,128},{80,144},{96,160},{112,17... | collective-permute-start | bytes 1572872 | tf_op jit(solution)/shard_map/ppermute | solution.py:23
  59.8 1.0 copy-start.2
  60.8 10.4 %collective-permute-start.7 = (bf16[1024,256]{1,0:T(8,128)(2,1)}, bf16[1024,256]{1,0:T(8,128)(2,1)}, u32[]{:S(2)}, u32[]{:S(2)}) collective-permute-start(bf16[1024,256]{1,0:T(8,128)(2,1)} %slice.43), channel_id=1, source_target_pairs={{0,192},{16,208},{32,224},{48,240},{64,0},{80,16},{96,32},{112,48}... | collective-permute-start | bytes 1572872 | tf_op jit(solution)/shard_map/ppermute | solution.py:23
  71.2 1.2 copy-start.1
  72.4 1.2 copy-start.3
  73.6 1.2 copy-start.5
  101.5 25.9 %all-to-all-start.1 = ((bf16[16,32,256]{2,1,0:T(8,128)(2,1)}), bf16[16,32,256]{2,1,0:T(8,128)(2,1)S(1)}, u32[]{:S(2)}, u32[]{:S(2)}) async-start(bf16[16,32,256]{2,1,0:T(8,128)(2,1)} %combine.1), calls=%async_computation.1 | async-start | bytes 524288 | tf_op jit(solution)/shard_map/all_to_all | solution.py:217
  129.1 10.5 %copy-start.6 = (f32[32,256]{1,0:T(8,128)}, f32[32,256]{1,0:T(8,128)S(1)}, u32[]{:S(2)}) copy-start(f32[32,256]{1,0:T(8,128)S(1)} %get-tuple-element.5.refs_1_) | copy-start | bytes 98308
Sparse Core Ops, SparseCore 0:
  9.8 60.1 all-gather.2

commit v2 on v1

--- a/solution.py
+++ b/solution.py
@@ -23,46 +23,46 @@
     return lax.ppermute(array, "agent", pairs)
 
 
-def ring(block, hop):
+def line(block, hop):
     half = block.shape[0] // 2
     low = hop(block, 1)
     high = hop(block, -1)
     far_top = hop(low[:half], 1)
     far_bottom = hop(high[half:], -1)
-    return block, low, high, far_top, far_bottom
+    near = jnp.concatenate([block, low], axis=0)
+    rest = jnp.concatenate([high, far_top, far_bottom], axis=0)
+    return near, rest
 
 
 def gather_weights(first, second, hop_one, hop_two):
-    pair = jnp.concatenate([first, second], axis=0)
-    line = jnp.concatenate(ring(pair, hop_one), axis=0)
-    return ring(line, hop_two)
-
-
-def attend_kernel(block_ids, feats, qk0, qk1, qk2, qk3, qk4, vo0, vo1, vo2, vo3, vo4, valid,
-                  out, x_all, qk_all, v_all, stat, x_sem, qk_sem, v_sem):
+    near, rest = line(jnp.concatenate([first, second], axis=0), hop_one)
+    near_low = hop_two(near, 1)
+    near_high = hop_two(near, -1)
+    rest_low = hop_two(rest, 1)
+    rest_high = hop_two(rest, -1)
+    near_far = hop_two(near_low, 1)
+    rest_far = hop_two(rest_high, -1)
+    return near, rest, near_low, rest_low, near_high, rest_high, near_far, rest_far
+
+
+def attend_kernel(block_ids, *refs):
+    feats, qk_refs, vo_refs = refs[0], refs[1:9], refs[9:17]
+    valid, out, x_all, qk_all, v_all, stat, x_sem, qk_sem, v_sem = refs[17:]
     rows = feats.shape[1] // 2
     depth = feats.shape[2]
     x_copies = []
     for slot in range(GROUP):
         copy = pltpu.make_async_copy(feats.at[block_ids[slot]], x_all.at[slot], x_sem.at[slot])
         x_copies.append(copy)
-    qk_parts = ((qk0, 0, 4), (qk1, 4, 4), (qk2, 8, 4), (qk3, 12, 2), (qk4, 14, 2))
-    vo_parts = ((vo0, 0, 4), (vo1, 4, 4), (vo2, 8, 4), (vo3, 12, 2), (vo4, 14, 2))
     qk_copies, v_copies = [], []
-    for n, (ref, start, count) in enumerate(qk_parts):
+    for n in range(8):
         qk_copies.append(pltpu.make_async_copy(
-            ref, qk_all.at[pl.ds(start, count)], qk_sem.at[n]))
-    for n, (ref, start, count) in enumerate(vo_parts):
+            qk_refs[n], qk_all.at[pl.ds(2 * n, 2)], qk_sem.at[n]))
         v_copies.append(pltpu.make_async_copy(
-            ref.at[:, 0], v_all.at[pl.ds(start, count)], v_sem.at[n]))
+            vo_refs[n].at[:, 0], v_all.at[pl.ds(2 * n, 2)], v_sem.at[n]))
     for part in range(SIDE):
-        for copy in x_copies[part * SIDE:(part + 1) * SIDE]:
+        for copy in x_copies[part * SIDE:(part + 1) * SIDE] + qk_copies[2 * part:2 * part + 2]:
             copy.start()
-        if part < 3:
-            qk_copies[part].start()
-        else:
-            qk_copies[3].start()
-            qk_copies[4].start()
     for copy in v_copies:
         copy.start()
 
@@ -72,13 +72,8 @@
 
     query = keys = values = None
     for part in range(SIDE):
-        for copy in x_copies[part * SIDE:(part + 1) * SIDE]:
+        for copy in x_copies[part * SIDE:(part + 1) * SIDE] + qk_copies[2 * part:2 * part + 2]:
             copy.wait()
-        if part < 3:
-            qk_copies[part].wait()
-        else:
-            qk_copies[3].wait()
-            qk_copies[4].wait()
         w_q = qk_all[pl.ds(part * SIDE, SIDE), 0].reshape(SIDE * depth, -1)
         w_k = qk_all[pl.ds(part * SIDE, SIDE), 1].reshape(SIDE * depth, -1)
         more_q = jnp.dot(columns(part * SIDE, rows), w_q, preferred_element_type=F32)
@@ -136,15 +131,14 @@
                 out[t, pl.ds(8 * tile, 8), head * HEAD_DIM:(head + 1) * HEAD_DIM] = out_tile
 
 
-def project_kernel(block_ids, attended, vo0, vo1, vo2, vo3, vo4, latents, upd, squares):
-    refs = ((vo0, 0, 4), (vo1, 4, 4), (vo2, 8, 4), (vo3, 12, 2), (vo4, 14, 2))
-    total = latents[...].astype(F32)
-    chunk = latents.shape[0]
-    for ref, start, count in refs:
-        for at in range(count):
-            slot = start + at
-            block = block_ids[slot % SIDE * SIDE + slot // SIDE]
-            total += jnp.dot(attended[block], ref[at, 1], preferred_element_type=F32)
+def project_kernel(block_ids, me, attended, *refs):
+    vo_refs, (latents, upd, squares) = refs[:8], refs[8:]
+    chunk = upd.shape[0]
+    total = latents[pl.ds(pl.multiple_of(me[0] * chunk, chunk), chunk), :].astype(F32)
+    for slot in range(GROUP):
+        block = block_ids[slot % SIDE * SIDE + slot // SIDE]
+        total += jnp.dot(
+            attended[block], vo_refs[slot // 2][slot % 2, 1], preferred_element_type=F32)
     upd[...] = total
     square = jnp.sum(total * total, axis=1, keepdims=True)
     lane = lax.broadcasted_iota(jnp.int32, (8, HEAD_DIM), 1)
@@ -192,7 +186,7 @@
     partial = pl.pallas_call(
         attend_kernel,
         out_shape=jax.ShapeDtypeStruct((GROUP, 2 * chunk + 8, HEAD_DIM), F32),
-        in_specs=[smem] + [anywhere] * 11 + whole(1),
+        in_specs=[smem] + [anywhere] * 17 + whole(1),
         out_specs=whole(1)[0],
         scratch_shapes=[
             pltpu.VMEM((GROUP, 2 * rows, depth), BF16),
@@ -200,10 +194,10 @@
             pltpu.VMEM((GROUP, depth, depth), BF16),
             pltpu.VMEM((GROUP, chunk // 8, 8, HEAD_DIM), F32),
             pltpu.SemaphoreType.DMA((GROUP,)),
-            pltpu.SemaphoreType.DMA((5,)),
-            pltpu.SemaphoreType.DMA((5,)),
+            pltpu.SemaphoreType.DMA((8,)),
+            pltpu.SemaphoreType.DMA((8,)),
         ],
-        compiler_params=pltpu.CompilerParams(vmem_limit_bytes=40 * 2**20),
+        compiler_params=pltpu.CompilerParams(vmem_limit_bytes=60 * 2**20),
         name="attend",
     )(block_ids, feats, *qk, *vo, valid.reshape(1, rows))
     partial = lax.all_to_all(partial, "agent", 0, 0)
@@ -215,16 +209,15 @@
         name="combine",
     )(partial)
     attended = lax.all_to_all(attended, "tensor", 0, 0)
-    mine = lax.dynamic_slice_in_dim(latents, me * chunk, chunk, axis=0)
     upd, squares = pl.pallas_call(
         project_kernel,
         out_shape=(jax.ShapeDtypeStruct((chunk, depth), F32),
                    jax.ShapeDtypeStruct((GROUP, 8, HEAD_DIM), F32)),
-        in_specs=[smem] + whole(7),
+        in_specs=[smem, smem] + whole(10),
         out_specs=tuple(whole(2)),
         compiler_params=pltpu.CompilerParams(vmem_limit_bytes=40 * 2**20),
         name="project",
-    )(block_ids, attended, *vo, mine)
+    )(block_ids, me.astype(jnp.int32).reshape(1), attended, *vo, latents)
     squares = lax.all_to_all(squares, "tensor", 0, 0)
     out = pl.pallas_call(
         lambda *refs: finish_kernel(width, *refs),

time: 164 us -> 172 us (1.049)
  blocking collectives: 39.8 us -> 62.9 us
  starting transfers between devices: 37.7 us -> 22.8 us
  local copies, waits for them, and re-layouts: 14.5 us -> 11.7 us
  Pallas kernels: 15.5 us -> 18 us
    all_to_all x0 -> x1, blocking collectives: none -> 23.8 us  [body(): attended = lax.all_to_all(attended, 'tensor', 0, 0)]
    all_to_all x1 -> x0, starting transfers between devices: 14.1 us -> none  [body(): attended = lax.all_to_all(attended, 'tensor', 0, 0)]
    all_to_all x1 -> x0, waiting for transfers between devices: 11 us -> none  [body(): attended = lax.all_to_all(attended, 'tensor', 0, 0)]
    ppermute x8 -> x10, waiting for transfers between devices: 7.11 us -> 12.8 us  [hop_y(): return lax.ppermute(array, 'agent', pairs)]
    ppermute x8 -> x10, waiting for transfers between devices: 22 us -> 27.1 us  [hop_x(): return lax.ppermute(array, 'agent', pairs)]
    slice x8 -> x4, local copies, waits for them, and re-layouts: 3.42 us -> 0.04 us  [the longest x2 0.02 us: line(): far_bottom = hop(high[half:], -1)]
    pallas_call x1, Pallas kernels: 9.57 us -> 12.1 us  [body(): pl.pallas_call(attend_kernel, out_shape=jax.ShapeDtypeStruct((GROUP, 2 *...]
    ppermute x8 -> x10, starting transfers between devices: 11.4 us -> 10.8 us  [hop_x(): return lax.ppermute(array, 'agent', pairs)]
  transfers between devices with their start and end apart: 18 -> 21, of which waited for: 7 -> 6; matrix products, arithmetic and copies ran while one was open for 5% -> 3% of each run, Pallas kernels for 0% -> 0%
where the time goes in v2:
time: 172 us; the launch traced here: 171 us
  blocking collectives  62.9 us (37%)
  waiting for transfers between devices  39.9 us (23%)
  starting transfers between devices  22.8 us (13%)
  Pallas kernels  18 us (10%)
  between operations  14.3 us (8%)
  local copies, waits for them, and re-layouts  11.7 us (7%)
  other arithmetic  1.88 us (1%)
    ppermute x10, waiting for transfers between devices, hop_x(): return lax.ppermute(array, 'agent', pairs)  27.1 us
    all_to_all x1, blocking collectives, body(): attended = lax.all_to_all(attended, 'tensor', 0, 0)  23.8 us
    all_to_all x1, blocking collectives, body(): out = lax.all_to_all(out, 'agent', 0, 0)  14.7 us
    all_to_all x1, blocking collectives, body(): partial = lax.all_to_all(partial, 'agent', 0, 0)  14 us
    ppermute x10, waiting for transfers between devices, hop_y(): return lax.ppermute(array, 'agent', pairs)  12.8 us
    pallas_call x1, Pallas kernels, body(): pl.pallas_call(attend_kernel, out_shape=jax.ShapeDtypeStruct((GROUP, 2 *...  12.1 us
    ppermute x10, starting transfers between devices, hop_y(): return lax.ppermute(array, 'agent', pairs)  11.9 us
    ppermute x10, starting transfers between devices, hop_x(): return lax.ppermute(array, 'agent', pairs)  10.8 us
  transfers between devices with their start and end apart: 21, of which 6 were waited for; matrix products, arithmetic and copies ran while one was open for 3% of the time, Pallas kernels for 0%

profile of v2, /device:TPU:1, one launch (start us, length us, event | category | flops | bytes accessed | tf_op | source)
XLA Modules:
  0.0 171.5 jit_solution(4591227260596459702)
XLA Ops:
  7.2 0.0 all-gather.3.cloned.1.call-start
  7.2 1.9 %pad_maximum_fusion = bf16[1024,256]{1,0:T(8,128)(2,1)} fusion(bf16[512,256]{1,0:T(8,128)(2,1)} %refs_8_.1, bf16[512,256]{1,0:T(8,128)(2,1)} %param.8), kind=kLoop, calls=%fused_computation | loop fusion | flops 1048576 | bytes 1048576 | tf_op jit(solution)/shard_map/concatenate | solution.py:174
  9.1 0.0 all-gather.3.cloned.1.call-update
  9.1 0.9 constant_dynamic-update-slice_fusion.1
  10.0 0.9 constant_dynamic-update-slice_fusion
  11.0 2.1 %collective-permute-start = (bf16[512,256]{1,0:T(8,128)(2,1)S(1)}, bf16[512,256]{1,0:T(8,128)(2,1)S(1)}, u32[]{:S(2)}, u32[]{:S(2)}) collective-permute-start(bf16[512,256]{1,0:T(8,128)(2,1)S(1)} %get-tuple-element.12), channel_id=1, source_target_pairs={{0,16},{16,32},{32,48},{48,0},{64,80},{80,96},{96,112},{112,64},{1... | collective-permute-start | bytes 786440 | tf_op jit(solution)/shard_map/ppermute | solution.py:18
  13.1 1.4 collective-permute-start.1
  14.4 0.9 constant_dynamic-update-slice_fusion.9
  15.4 0.9 constant_dynamic-update-slice_fusion.8
  16.3 2.9 %collective-permute-start.11 = (bf16[512,256]{1,0:T(8,128)(2,1)S(1)}, bf16[512,256]{1,0:T(8,128)(2,1)S(1)}, u32[]{:S(2)}, u32[]{:S(2)}) collective-permute-start(bf16[512,256]{1,0:T(8,128)(2,1)S(1)} %get-tuple-element.8), channel_id=1, source_target_pairs={{0,192},{16,208},{32,224},{48,240},{64,0},{80,16},{96,32},{112,48}... | collective-permute-start | bytes 786440 | tf_op jit(solution)/shard_map/ppermute | solution.py:23
  19.2 0.0 collective-permute-start.10
  19.2 0.0 collective-permute-done
  19.3 3.8 %collective-permute-start.6 = (bf16[1024,256]{1,0:T(8,128)(2,1)S(1)}, bf16[1024,256]{1,0:T(8,128)(2,1)S(1)}, u32[]{:S(2)}, u32[]{:S(2)}) collective-permute-start(bf16[1024,256]{1,0:T(8,128)(2,1)S(1)} %constant_dynamic-update-slice_fusion.2), channel_id=1, source_target_pairs={{0,192},{16,208},{32,224},{48,240},{64,0},{80,16},{96,32},{112,48}... | collective-permute-start | bytes 1572872 | tf_op jit(solution)/shard_map/ppermute | solution.py:23
  23.1 0.0 collective-permute-start.4
  23.1 0.0 collective-permute-done.1
  23.1 1.3 collective-permute-start.3
  24.5 0.0 collective-permute-done.11
  24.5 0.3 collective-permute-start.2
  24.8 1.9 %collective-permute-done.10 = bf16[512,256]{1,0:T(8,128)(2,1)S(1)} collective-permute-done((bf16[512,256]{1,0:T(8,128)(2,1)S(1)}, bf16[512,256]{1,0:T(8,128)(2,1)S(1)}, u32[]{:S(2)}, u32[]{:S(2)}) %collective-permute-start.10) | collective-permute-done | bytes 262176 | tf_op jit(solution)/shard_map/ppermute | solution.py:23
  26.7 0.9 collective-permute-start.13
  27.6 2.4 %collective-permute-done.2 = bf16[256,256]{1,0:T(8,128)(2,1)S(1)} collective-permute-done((bf16[256,256]{1,0:T(8,128)(2,1)S(1)}, bf16[256,256]{1,0:T(8,128)(2,1)S(1)}, u32[]{:S(2)}, u32[]{:S(2)}) %collective-permute-start.2) | collective-permute-done | bytes 131104 | tf_op jit(solution)/shard_map/ppermute | solution.py:18
  30.0 0.0 collective-permute-start.12
  30.0 0.0 collective-permute-done.3
  30.1 0.3 collective-permute-start.16
  30.4 10.9 %collective-permute-done.12 = bf16[256,256]{1,0:T(8,128)(2,1)S(1)} collective-permute-done((bf16[256,256]{1,0:T(8,128)(2,1)S(1)}, bf16[256,256]{1,0:T(8,128)(2,1)S(1)}, u32[]{:S(2)}, u32[]{:S(2)}) %collective-permute-start.12) | collective-permute-done | bytes 131104 | tf_op jit(solution)/shard_map/ppermute | solution.py:23
  41.2 0.0 collective-permute-start.14
  41.3 0.0 collective-permute-done.13
  41.3 0.1 collective-permute-start.7
  41.4 0.0 collective-permute-done.6
  41.4 1.5 collective-permute-start.5
  42.9 0.0 collective-permute-done.4
  42.9 2.7 %collective-permute-start.17 = (bf16[1024,256]{1,0:T(8,128)(2,1)S(1)}, bf16[1024,256]{1,0:T(8,128)(2,1)S(1)}, u32[]{:S(2)}, u32[]{:S(2)}) collective-permute-start(bf16[1024,256]{1,0:T(8,128)(2,1)S(1)} %constant_dynamic-update-slice_fusion.13), channel_id=1, source_target_pairs={{0,48},{16,0},{32,16},{48,32},{64,112},{80,64},{96,80},{112,96},{1... | collective-permute-start | bytes 1572872 | tf_op jit(solution)/shard_map/ppermute | solution.py:18
  45.6 0.0 collective-permute-done.16
  45.6 0.0 collective-permute-start.15
  45.6 8.4 %collective-permute-done.14 = bf16[1024,256]{1,0:T(8,128)(2,1)S(1)} collective-permute-done((bf16[1024,256]{1,0:T(8,128)(2,1)S(1)}, bf16[1024,256]{1,0:T(8,128)(2,1)S(1)}, u32[]{:S(2)}, u32[]{:S(2)}) %collective-permute-start.14) | collective-permute-done | bytes 524320 | tf_op jit(solution)/shard_map/ppermute | solution.py:18
  54.0 0.0 collective-permute-start.8
  54.0 0.0 collective-permute-done.7
  54.0 0.1 collective-permute-start.18
  54.1 0.0 collective-permute-done.5
  54.1 2.7 %collective-permute-start.9 = (bf16[1024,256]{1,0:T(8,128)(2,1)}, bf16[1024,256]{1,0:T(8,128)(2,1)}, u32[]{:S(2)}, u32[]{:S(2)}) collective-permute-start(bf16[1024,256]{1,0:T(8,128)(2,1)} %collective-permute-done.7), channel_id=1, source_target_pairs={{0,192},{16,208},{32,224},{48,240},{64,0},{80,16},{96,32},{112,48}... | collective-permute-start | bytes 1572872 | tf_op jit(solution)/shard_map/ppermute | solution.py:23
  56.8 0.0 collective-permute-done.17
  56.8 2.7 %collective-permute-start.19 = (bf16[1024,256]{1,0:T(8,128)(2,1)S(1)}, bf16[1024,256]{1,0:T(8,128)(2,1)}, u32[]{:S(2)}, u32[]{:S(2)}) collective-permute-start(bf16[1024,256]{1,0:T(8,128)(2,1)S(1)} %collective-permute-done.17), channel_id=1, source_target_pairs={{0,48},{16,0},{32,16},{48,32},{64,112},{80,64},{96,80},{112,96},{1... | collective-permute-start | bytes 1572872 | tf_op jit(solution)/shard_map/ppermute | solution.py:18
  59.5 0.7 stack.67.block_ids
  60.1 5.1 %collective-permute-done.15 = bf16[1024,256]{1,0:T(8,128)(2,1)S(1)} collective-permute-done((bf16[1024,256]{1,0:T(8,128)(2,1)S(1)}, bf16[1024,256]{1,0:T(8,128)(2,1)S(1)}, u32[]{:S(2)}, u32[]{:S(2)}) %collective-permute-start.15) | collective-permute-done | bytes 524320 | tf_op jit(solution)/shard_map/ppermute | solution.py:18
  65.2 0.0 collective-permute-done.8
  65.3 11.2 %collective-permute-done.18 = bf16[1024,256]{1,0:T(8,128)(2,1)} collective-permute-done((bf16[1024,256]{1,0:T(8,128)(2,1)S(1)}, bf16[1024,256]{1,0:T(8,128)(2,1)}, u32[]{:S(2)}, u32[]{:S(2)}) %collective-permute-start.18) | collective-permute-done | bytes 524320 | tf_op jit(solution)/shard_map/ppermute | solution.py:18
  76.5 0.0 all-gather.3.cloned.1.call-done
  76.6 0.0 copy-start.12
  76.6 12.1 %attend.1 = f32[16,72,128]{2,1,0:T(8,128)} custom-call(s32[16]{0:T(128)} %stack.67.block_ids, bf16[16,1024,256]{2,1,0:T(8,128)(2,1)} %bitcast.50, bf16[2,2,256,256]{3,2,1,0:T(8,128)(2,1)} %bitcast.52, bf16[2,2,256,256]{3,2,1,0:T(8,128)(2,1)} %bitcast.51, bf16[2,2,256,256]{3,2,1,0:T(8,128)(2,1)} %bitcast.20.refs_3_, bf16[2,2,256,256]{3,2,1,0:T(8,128)(2,1)} %bitcast.54, ...), custom_call_target="tpu_custom_call" | custom-call | tf_op jit(solution)/shard_map/attend/pallas_call | solution.py:186
  88.7 14.0 %all_to_all.20.parts = f32[16,72,128]{2,1,0:T(8,128)} all-to-all(f32[16,72,128]{2,1,0:T(8,128)} %attend.1), channel_id=1, replica_groups=mesh['agent'=16,'tensor'=16] {'agent'}, dimensions={0} | all-to-all | bytes 1179648 | tf_op jit(solution)/shard_map/all_to_all | solution.py:203
  102.6 2.4 %combine.1 = bf16[16,32,256]{2,1,0:T(8,128)(2,1)} custom-call(f32[16,72,128]{2,1,0:T(8,128)} %all_to_all.20.parts), custom_call_target="tpu_custom_call" | custom-call | tf_op jit(solution)/shard_map/combine/pallas_call | solution.py:204
  105.0 23.8 %all_to_all.21.attended = bf16[16,32,256]{2,1,0:T(8,128)(2,1)S(1)} all-to-all(bf16[16,32,256]{2,1,0:T(8,128)(2,1)} %combine.1), channel_id=1, replica_groups=mesh['agent'=16,'tensor'=16] {'tensor'}, dimensions={0} | all-to-all | bytes 524288 | tf_op jit(solution)/shard_map/all_to_all | solution.py:211
  128.8 1.0 copy-done.1
  129.9 1.0 copy-done.3
  130.9 1.0 copy-done.5
  132.0 1.0 copy-done.7
  133.0 1.0 copy-done.9
  134.0 1.0 copy-done.11
  135.1 1.8 %project.1 = (f32[32,256]{1,0:T(8,128)S(1)}, f32[16,8,128]{2,1,0:T(8,128)S(1)}) custom-call(s32[16]{0:T(128)S(1)} %copy-done.14, s32[1]{0:T(128)} %bitcast.16.me, bf16[16,32,256]{2,1,0:T(8,128)(2,1)S(1)} %all_to_all.21.attended, bf16[2,2,256,256]{3,2,1,0:T(8,128)(2,1)S(1)} %bitcast.41, bf16[2,2,256,256]{3,2,1,0:T(8,128)(2,1)S(1)} %bitcast.39, ...), custom_call_target="tpu_custom_call" | custom-call | tf_op jit(solution)/shard_map/project/pallas_call | solution.py:212
  136.8 0.0 copy-start.13
  136.9 10.5 %all_to_all.22.refs_0_ = f32[16,8,128]{2,1,0:T(8,128)} all-to-all(f32[16,8,128]{2,1,0:T(8,128)S(1)} %get-tuple-element.4), channel_id=1, replica_groups=mesh['agent'=16,'tensor'=16] {'tensor'}, dimensions={0} | all-to-all | bytes 131072 | tf_op jit(solution)/shard_map/all_to_all | solution.py:221
  147.4 1.8 %finish.1 = bf16[16,2,32,256]{3,2,1,0:T(8,128)(2,1)} custom-call(f32[16,8,128]{2,1,0:T(8,128)} %all_to_all.22.refs_0_, f32[32,256]{1,0:T(8,128)} %copy-done.13, f32[1,256]{1,0:T(1,128)} %bitcast.58), custom_call_target="tpu_custom_call" | custom-call | tf_op jit(solution)/shard_map/finish/pallas_call | solution.py:222
  149.2 14.7 %all_to_all.23 = bf16[16,2,32,256]{3,2,1,0:T(8,128)(2,1)S(1)} all-to-all(bf16[16,2,32,256]{3,2,1,0:T(8,128)(2,1)} %finish.1), channel_id=1, replica_groups=mesh['agent'=16,'tensor'=16] {'agent'}, dimensions={0} | all-to-all | bytes 1048576 | tf_op jit(solution)/shard_map/all_to_all | solution.py:229
  163.8 0.8 fusion
  (44 shorter events, 0.2 us)
Async XLA Ops:
  7.2 69.3 %all-gather.3.cloned.1.call-start = ((), (), s32[]{:S(2)}) async-start(), calls=%async_computation.4 | async-start | bytes 8912896 | tf_op jit(solution)/shard_map/all_gather | solution.py:175
  11.0 8.3 %collective-permute-start = (bf16[512,256]{1,0:T(8,128)(2,1)S(1)}, bf16[512,256]{1,0:T(8,128)(2,1)S(1)}, u32[]{:S(2)}, u32[]{:S(2)}) collective-permute-start(bf16[512,256]{1,0:T(8,128)(2,1)S(1)} %get-tuple-element.12), channel_id=1, source_target_pairs={{0,16},{16,32},{32,48},{48,0},{64,80},{80,96},{96,112},{112,64},{1... | collective-permute-start | bytes 786440 | tf_op jit(solution)/shard_map/ppermute | solution.py:18
  13.1 10.0 %collective-permute-start.1 = (bf16[512,256]{1,0:T(8,128)(2,1)S(1)}, bf16[512,256]{1,0:T(8,128)(2,1)S(1)}, u32[]{:S(2)}, u32[]{:S(2)}) collective-permute-start(bf16[512,256]{1,0:T(8,128)(2,1)S(1)} %get-tuple-element.12), channel_id=1, source_target_pairs={{0,48},{16,0},{32,16},{48,32},{64,112},{80,64},{96,80},{112,96},{1... | collective-permute-start | bytes 786440 | tf_op jit(solution)/shard_map/ppermute | solution.py:18
  16.3 8.2 %collective-permute-start.11 = (bf16[512,256]{1,0:T(8,128)(2,1)S(1)}, bf16[512,256]{1,0:T(8,128)(2,1)S(1)}, u32[]{:S(2)}, u32[]{:S(2)}) collective-permute-start(bf16[512,256]{1,0:T(8,128)(2,1)S(1)} %get-tuple-element.8), channel_id=1, source_target_pairs={{0,192},{16,208},{32,224},{48,240},{64,0},{80,16},{96,32},{112,48}... | collective-permute-start | bytes 786440 | tf_op jit(solution)/shard_map/ppermute | solution.py:23
  19.2 7.5 %collective-permute-start.10 = (bf16[512,256]{1,0:T(8,128)(2,1)S(1)}, bf16[512,256]{1,0:T(8,128)(2,1)S(1)}, u32[]{:S(2)}, u32[]{:S(2)}) collective-permute-start(bf16[512,256]{1,0:T(8,128)(2,1)S(1)} %get-tuple-element.8), channel_id=1, source_target_pairs={{0,64},{16,80},{32,96},{48,112},{64,128},{80,144},{96,160},{112,17... | collective-permute-start | bytes 786440 | tf_op jit(solution)/shard_map/ppermute | solution.py:23
  19.2 23.7 %copy-start.16 = (bf16[1024,256]{1,0:T(8,128)(2,1)}, bf16[1024,256]{1,0:T(8,128)(2,1)S(1)}, u32[]{:S(2)}) copy-start(bf16[1024,256]{1,0:T(8,128)(2,1)S(1)} %constant_dynamic-update-slice_fusion.2) | copy-start | bytes 1572868
  19.3 22.1 %collective-permute-start.6 = (bf16[1024,256]{1,0:T(8,128)(2,1)S(1)}, bf16[1024,256]{1,0:T(8,128)(2,1)S(1)}, u32[]{:S(2)}, u32[]{:S(2)}) collective-permute-start(bf16[1024,256]{1,0:T(8,128)(2,1)S(1)} %constant_dynamic-update-slice_fusion.2), channel_id=1, source_target_pairs={{0,192},{16,208},{32,224},{48,240},{64,0},{80,16},{96,32},{112,48}... | collective-permute-start | bytes 1572872 | tf_op jit(solution)/shard_map/ppermute | solution.py:23
  23.1 19.8 %collective-permute-start.4 = (bf16[1024,256]{1,0:T(8,128)(2,1)S(1)}, bf16[1024,256]{1,0:T(8,128)(2,1)}, u32[]{:S(2)}, u32[]{:S(2)}) collective-permute-start(bf16[1024,256]{1,0:T(8,128)(2,1)S(1)} %constant_dynamic-update-slice_fusion.2), channel_id=1, source_target_pairs={{0,64},{16,80},{32,96},{48,112},{64,128},{80,144},{96,160},{112,17... | collective-permute-start | bytes 1572872 | tf_op jit(solution)/shard_map/ppermute | solution.py:23
  23.1 6.9 %collective-permute-start.3 = (bf16[256,256]{1,0:T(8,128)(2,1)S(1)}, bf16[256,256]{1,0:T(8,128)(2,1)S(1)}, u32[]{:S(2)}, u32[]{:S(2)}) collective-permute-start(bf16[256,256]{1,0:T(8,128)(2,1)S(1)} %slice.25), channel_id=1, source_target_pairs={{0,48},{16,0},{32,16},{48,32},{64,112},{80,64},{96,80},{112,96},{1... | collective-permute-start | bytes 393224 | tf_op jit(solution)/shard_map/ppermute | solution.py:18
  24.5 5.5 %collective-permute-start.2 = (bf16[256,256]{1,0:T(8,128)(2,1)S(1)}, bf16[256,256]{1,0:T(8,128)(2,1)S(1)}, u32[]{:S(2)}, u32[]{:S(2)}) collective-permute-start(bf16[256,256]{1,0:T(8,128)(2,1)S(1)} %slice.24), channel_id=1, source_target_pairs={{0,16},{16,32},{32,48},{48,0},{64,80},{80,96},{96,112},{112,64},{1... | collective-permute-start | bytes 393224 | tf_op jit(solution)/shard_map/ppermute | solution.py:18
  26.7 14.5 %collective-permute-start.13 = (bf16[256,256]{1,0:T(8,128)(2,1)S(1)}, bf16[256,256]{1,0:T(8,128)(2,1)S(1)}, u32[]{:S(2)}, u32[]{:S(2)}) collective-permute-start(bf16[256,256]{1,0:T(8,128)(2,1)S(1)} %slice.27), channel_id=1, source_target_pairs={{0,192},{16,208},{32,224},{48,240},{64,0},{80,16},{96,32},{112,48}... | collective-permute-start | bytes 393224 | tf_op jit(solution)/shard_map/ppermute | solution.py:23
  27.6 48.9 %copy-start.2 = (bf16[1024,256]{1,0:T(8,128)(2,1)}, bf16[1024,256]{1,0:T(8,128)(2,1)S(1)}, u32[]{:S(2)}) copy-start(bf16[1024,256]{1,0:T(8,128)(2,1)S(1)} %constant_dynamic-update-slice_fusion.10) | copy-start | bytes 1572868
  30.0 11.2 %collective-permute-start.12 = (bf16[256,256]{1,0:T(8,128)(2,1)S(1)}, bf16[256,256]{1,0:T(8,128)(2,1)S(1)}, u32[]{:S(2)}, u32[]{:S(2)}) collective-permute-start(bf16[256,256]{1,0:T(8,128)(2,1)S(1)} %slice.26), channel_id=1, source_target_pairs={{0,64},{16,80},{32,96},{48,112},{64,128},{80,144},{96,160},{112,17... | collective-permute-start | bytes 393224 | tf_op jit(solution)/shard_map/ppermute | solution.py:23
  30.1 15.6 %collective-permute-start.16 = (bf16[1024,256]{1,0:T(8,128)(2,1)S(1)}, bf16[1024,256]{1,0:T(8,128)(2,1)S(1)}, u32[]{:S(2)}, u32[]{:S(2)}) collective-permute-start(bf16[1024,256]{1,0:T(8,128)(2,1)S(1)} %constant_dynamic-update-slice_fusion.10), channel_id=1, source_target_pairs={{0,48},{16,0},{32,16},{48,32},{64,112},{80,64},{96,80},{112,96},{1... | collective-permute-start | bytes 1572872 | tf_op jit(solution)/shard_map/ppermute | solution.py:18
  30.3 26.4 %copy-start.15 = (bf16[1024,256]{1,0:T(8,128)(2,1)}, bf16[1024,256]{1,0:T(8,128)(2,1)S(1)}, u32[]{:S(2)}) copy-start(bf16[1024,256]{1,0:T(8,128)(2,1)S(1)} %constant_dynamic-update-slice_fusion.5) | copy-start | bytes 1572868
  41.2 12.8 %collective-permute-start.14 = (bf16[1024,256]{1,0:T(8,128)(2,1)S(1)}, bf16[1024,256]{1,0:T(8,128)(2,1)S(1)}, u32[]{:S(2)}, u32[]{:S(2)}) collective-permute-start(bf16[1024,256]{1,0:T(8,128)(2,1)S(1)} %constant_dynamic-update-slice_fusion.10), channel_id=1, source_target_pairs={{0,16},{16,32},{32,48},{48,0},{64,80},{80,96},{96,112},{112,64},{1... | collective-permute-start | bytes 1572872 | tf_op jit(solution)/shard_map/ppermute | solution.py:18
  41.3 12.8 %collective-permute-start.7 = (bf16[1024,256]{1,0:T(8,128)(2,1)S(1)}, bf16[1024,256]{1,0:T(8,128)(2,1)}, u32[]{:S(2)}, u32[]{:S(2)}) collective-permute-start(bf16[1024,256]{1,0:T(8,128)(2,1)S(1)} %constant_dynamic-update-slice_fusion.5), channel_id=1, source_target_pairs={{0,192},{16,208},{32,224},{48,240},{64,0},{80,16},{96,32},{112,48}... | collective-permute-start | bytes 1572872 | tf_op jit(solution)/shard_map/ppermute | solution.py:23
  41.4 35.1 %copy-start = (bf16[1024,256]{1,0:T(8,128)(2,1)}, bf16[1024,256]{1,0:T(8,128)(2,1)S(1)}, u32[]{:S(2)}) copy-start(bf16[1024,256]{1,0:T(8,128)(2,1)S(1)} %constant_dynamic-update-slice_fusion.13) | copy-start | bytes 1572868
  41.4 18.1 %copy-start.17 = (bf16[1024,256]{1,0:T(8,128)(2,1)}, bf16[1024,256]{1,0:T(8,128)(2,1)S(1)}, u32[]{:S(2)}) copy-start(bf16[1024,256]{1,0:T(8,128)(2,1)S(1)} %collective-permute-done.6) | copy-start | bytes 1572868
  41.4 12.7 %collective-permute-start.5 = (bf16[1024,256]{1,0:T(8,128)(2,1)S(1)}, bf16[1024,256]{1,0:T(8,128)(2,1)S(1)}, u32[]{:S(2)}, u32[]{:S(2)}) collective-permute-start(bf16[1024,256]{1,0:T(8,128)(2,1)S(1)} %constant_dynamic-update-slice_fusion.5), channel_id=1, source_target_pairs={{0,64},{16,80},{32,96},{48,112},{64,128},{80,144},{96,160},{112,17... | collective-permute-start | bytes 1572872 | tf_op jit(solution)/shard_map/ppermute | solution.py:23
  42.9 13.9 %collective-permute-start.17 = (bf16[1024,256]{1,0:T(8,128)(2,1)S(1)}, bf16[1024,256]{1,0:T(8,128)(2,1)S(1)}, u32[]{:S(2)}, u32[]{:S(2)}) collective-permute-start(bf16[1024,256]{1,0:T(8,128)(2,1)S(1)} %constant_dynamic-update-slice_fusion.13), channel_id=1, source_target_pairs={{0,48},{16,0},{32,16},{48,32},{64,112},{80,64},{96,80},{112,96},{1... | collective-permute-start | bytes 1572872 | tf_op jit(solution)/shard_map/ppermute | solution.py:18
  45.6 30.9 %copy-start.4 = (bf16[1024,256]{1,0:T(8,128)(2,1)}, bf16[1024,256]{1,0:T(8,128)(2,1)S(1)}, u32[]{:S(2)}) copy-start(bf16[1024,256]{1,0:T(8,128)(2,1)S(1)} %collective-permute-done.16) | copy-start | bytes 1572868
  45.6 19.6 %collective-permute-start.15 = (bf16[1024,256]{1,0:T(8,128)(2,1)S(1)}, bf16[1024,256]{1,0:T(8,128)(2,1)S(1)}, u32[]{:S(2)}, u32[]{:S(2)}) collective-permute-start(bf16[1024,256]{1,0:T(8,128)(2,1)S(1)} %constant_dynamic-update-slice_fusion.13), channel_id=1, source_target_pairs={{0,16},{16,32},{32,48},{48,0},{64,80},{80,96},{96,112},{112,64},{1... | collective-permute-start | bytes 1572872 | tf_op jit(solution)/shard_map/ppermute | solution.py:18
  54.0 22.5 %copy-start.6 = (bf16[1024,256]{1,0:T(8,128)(2,1)}, bf16[1024,256]{1,0:T(8,128)(2,1)S(1)}, u32[]{:S(2)}) copy-start(bf16[1024,256]{1,0:T(8,128)(2,1)S(1)} %collective-permute-done.14) | copy-start | bytes 1572868
  54.0 11.2 %collective-permute-start.8 = (bf16[1024,256]{1,0:T(8,128)(2,1)}, bf16[1024,256]{1,0:T(8,128)(2,1)}, u32[]{:S(2)}, u32[]{:S(2)}) collective-permute-start(bf16[1024,256]{1,0:T(8,128)(2,1)} %collective-permute-done.4), channel_id=1, source_target_pairs={{0,64},{16,80},{32,96},{48,112},{64,128},{80,144},{96,160},{112,17... | collective-permute-start | bytes 1572872 | tf_op jit(solution)/shard_map/ppermute | solution.py:23
  54.0 22.5 %collective-permute-start.18 = (bf16[1024,256]{1,0:T(8,128)(2,1)S(1)}, bf16[1024,256]{1,0:T(8,128)(2,1)}, u32[]{:S(2)}, u32[]{:S(2)}) collective-permute-start(bf16[1024,256]{1,0:T(8,128)(2,1)S(1)} %collective-permute-done.14), channel_id=1, source_target_pairs={{0,16},{16,32},{32,48},{48,0},{64,80},{80,96},{96,112},{112,64},{1... | collective-permute-start | bytes 1572872 | tf_op jit(solution)/shard_map/ppermute | solution.py:18
  54.1 5.3 %copy-start.18 = (bf16[1024,256]{1,0:T(8,128)(2,1)}, bf16[1024,256]{1,0:T(8,128)(2,1)S(1)}, u32[]{:S(2)}) copy-start(bf16[1024,256]{1,0:T(8,128)(2,1)S(1)} %collective-permute-done.5) | copy-start | bytes 1572868
  54.1 22.3 %collective-permute-start.9 = (bf16[1024,256]{1,0:T(8,128)(2,1)}, bf16[1024,256]{1,0:T(8,128)(2,1)}, u32[]{:S(2)}, u32[]{:S(2)}) collective-permute-start(bf16[1024,256]{1,0:T(8,128)(2,1)} %collective-permute-done.7), channel_id=1, source_target_pairs={{0,192},{16,208},{32,224},{48,240},{64,0},{80,16},{96,32},{112,48}... | collective-permute-start | bytes 1572872 | tf_op jit(solution)/shard_map/ppermute | solution.py:23
  56.8 19.8 %copy-start.8 = (bf16[1024,256]{1,0:T(8,128)(2,1)}, bf16[1024,256]{1,0:T(8,128)(2,1)S(1)}, u32[]{:S(2)}) copy-start(bf16[1024,256]{1,0:T(8,128)(2,1)S(1)} %collective-permute-done.17) | copy-start | bytes 1572868
  56.8 19.7 %collective-permute-start.19 = (bf16[1024,256]{1,0:T(8,128)(2,1)S(1)}, bf16[1024,256]{1,0:T(8,128)(2,1)}, u32[]{:S(2)}, u32[]{:S(2)}) collective-permute-start(bf16[1024,256]{1,0:T(8,128)(2,1)S(1)} %collective-permute-done.17), channel_id=1, source_target_pairs={{0,48},{16,0},{32,16},{48,32},{64,112},{80,64},{96,80},{112,96},{1... | collective-permute-start | bytes 1572872 | tf_op jit(solution)/shard_map/ppermute | solution.py:18
  65.2 11.3 %copy-start.10 = (bf16[1024,256]{1,0:T(8,128)(2,1)}, bf16[1024,256]{1,0:T(8,128)(2,1)S(1)}, u32[]{:S(2)}) copy-start(bf16[1024,256]{1,0:T(8,128)(2,1)S(1)} %collective-permute-done.15) | copy-start | bytes 1572868
  76.6 52.3 %copy-start.12 = (bf16[512,256]{1,0:T(8,128)(2,1)S(1)}, bf16[512,256]{1,0:T(8,128)(2,1)}, u32[]{:S(2)}) copy-start(bf16[512,256]{1,0:T(8,128)(2,1)} %refs_8_.1) | copy-start | bytes 786436
  76.6 52.3 %copy-start.14 = (s32[16]{0:T(128)S(1)}, s32[16]{0:T(128)}, u32[]{:S(2)}) copy-start(s32[16]{0:T(128)} %stack.67.block_ids) | copy-start | bytes 196
  128.8 1.0 copy-start.1
  129.9 1.0 copy-start.3
  130.9 1.0 copy-start.5
  132.0 1.0 copy-start.7
  133.0 1.0 copy-start.9
  134.0 1.0 copy-start.11
  136.8 10.5 %copy-start.13 = (f32[32,256]{1,0:T(8,128)}, f32[32,256]{1,0:T(8,128)S(1)}, u32[]{:S(2)}) copy-start(f32[32,256]{1,0:T(8,128)S(1)} %get-tuple-element.5.refs_1_) | copy-start | bytes 98308
Sparse Core Ops, SparseCore 0:
  9.8 60.1 all-gather.2

commit v3 on v2

v3 whole, which is shorter than its diff:
```python
import jax
import jax.numpy as jnp
from jax import lax
from jax.experimental import pallas as pl
from jax.experimental.pallas import tpu as pltpu
from jax.sharding import PartitionSpec as P

HEAD_DIM = 128
SIDE = 4
GROUP = 16
STEPS = (0, -1, 1, 2)
BF16 = jnp.bfloat16
F32 = jnp.float32


def pairs(move):
    out = []
    for agent in range(GROUP):
        for tensor in range(GROUP):
            y, x = move(agent // SIDE, agent % SIDE, tensor % 2)
            out.append((agent * GROUP + tensor, (y % SIDE * SIDE + x % SIDE) * GROUP + tensor))
    return out


def first(array, by):
    return lax.ppermute(array, ("agent", "tensor"), pairs(
        lambda y, x, core: (y, x + by) if core == 0 else (y + by, x)))


def second(array, by):
    return lax.ppermute(array, ("agent", "tensor"), pairs(
        lambda y, x, core: (y + by, x) if core == 0 else (y, x + by)))


def other_core(array):
    return lax.ppermute(array, "tensor", [(t, t ^ 1) for t in range(GROUP)])


def gather_weights(*weights):
    block = jnp.concatenate(weights, axis=0)
    half = block.shape[0] // 2
    low = first(block, 1)
    high = first(block, -1)
    far_top = first(block[:half], 2)
    far_bottom = first(block[half:], -2)
    near = jnp.concatenate([block, low], axis=0)
    rest = jnp.concatenate([high, far_top, far_bottom], axis=0)
    near, rest = lax.optimization_barrier((near, rest))
    near_low = second(near, 1)
    rest_high = second(rest, -1)
    rest_low = second(rest, 1)
    near_high = second(near, -1)
    near_far = second(near_low, 1)
    rest_far = second(rest_high, -1)
    parts = near, rest, near_low, rest_low, near_high, rest_high, near_far, rest_far
    return [part.reshape(2, len(weights), *weights[0].shape) for part in parts]


def block_table():
    agent, core = lax.axis_index("agent"), lax.axis_index("tensor") % 2
    y, x = agent // SIDE, agent % SIDE
    table = []
    for i in STEPS:
        for j in STEPS:
            dy, dx = jnp.where(core == 0, i, j), jnp.where(core == 0, j, i)
            table.append((y + dy + SIDE) % SIDE * SIDE + (x + dx + SIDE) % SIDE)
    return jnp.stack(table).astype(jnp.int32)


def attend_kernel(block_ids, feats, *refs):
    w_refs = refs[:8]
    valid, out, x_all, w_all, stat, x_sem, w_sem = refs[8:]
    rows = feats.shape[1] // 2
    depth = feats.shape[2]
    x_copies = [
        pltpu.make_async_copy(feats.at[block_ids[slot]], x_all.at[slot], x_sem.at[slot])
        for slot in range(GROUP)
    ]
    w_copies = [
        pltpu.make_async_copy(
            w_refs[n].at[:, pl.ds(0, 3)], w_all.at[pl.ds(2 * n, 2)], w_sem.at[n])
        for n in range(8)
    ]
    copies = [
        x_copies[part * SIDE:(part + 1) * SIDE] + w_copies[2 * part:2 * part + 2]
        for part in range(SIDE)
    ]
    for part in copies:
        for copy in part:
            copy.start()
    sums = [None] * 3
    for part in range(SIDE):
        for copy in copies[part]:
            copy.wait()
        for n, top in enumerate((rows, 0, 0)):
            left = jnp.concatenate(
                [x_all[part * SIDE + j, pl.ds(top, rows), :] for j in range(SIDE)], axis=1)
            right = w_all[pl.ds(part * SIDE, SIDE), n].reshape(SIDE * depth, -1)
            more = jnp.dot(left, right, preferred_element_type=F32)
            sums[n] = more if sums[n] is None else sums[n] + more
    query, keys, values = sums
    query = query.astype(BF16)
    keys = keys.astype(BF16)
    values = values.astype(BF16)
    scale = 1.0 / HEAD_DIM**0.5
    keep = valid[...] > 0
    lane = lax.broadcasted_iota(jnp.int32, (rows, HEAD_DIM), 1)
    tile = lax.broadcasted_iota(jnp.int32, (rows, HEAD_DIM), 0) // 8 % 4
    packed = jnp.zeros((rows, HEAD_DIM), F32)
    chunk = rows // GROUP
    for head in range(2):
        cols = slice(head * HEAD_DIM, (head + 1) * HEAD_DIM)
        scores = lax.dot_general(query[:, cols], keys[:, cols], (((1,), (1,)), ((), ())),
                                 preferred_element_type=F32) * scale
        scores = jnp.where(keep, scores, jnp.float32(-1000000000.0))
        top = jnp.max(scores, axis=1, keepdims=True)
        expo = jnp.exp(scores - top)
        total = jnp.sum(expo, axis=1, keepdims=True)
        coarse = expo.astype(BF16)
        fine = (expo - coarse.astype(F32)).astype(BF16)
        summed = jnp.dot(coarse, values[:, cols], preferred_element_type=F32)
        summed += jnp.dot(fine, values[:, cols], preferred_element_type=F32)
        out[:, pl.ds(head * chunk, chunk), :] = summed.reshape(GROUP, chunk, HEAD_DIM)
        packed = jnp.where(lane == 4 * tile + 2 * head, top, packed)
        packed = jnp.where(lane == 4 * tile + 2 * head + 1, total, packed)
    stat[...] = packed.reshape(GROUP, chunk // 8, 8, HEAD_DIM)
    out[:, pl.ds(2 * chunk, 8), :] = stat[:, 0] + stat[:, 1] + stat[:, 2] + stat[:, 3]


def combine_kernel(parts, out):
    chunk = out.shape[1]
    for tile in range(chunk // 8):
        for head in range(2):
            at = 4 * tile + 2 * head
            rows = pl.ds(2 * chunk, 8)
            tops = parts[:, rows, at:at + 1]
            totals = parts[:, rows, at + 1:at + 2]
            top = jnp.max(tops, axis=0, keepdims=True)
            factor = jnp.exp(tops - top)
            total = jnp.sum(totals * factor, axis=0)
            summed = jnp.sum(parts[:, pl.ds(head * chunk + 8 * tile, 8), :] * factor, axis=0)
            out_tile = (summed / total).astype(BF16)
            for t in range(out.shape[0]):
                out[t, pl.ds(8 * tile, 8), head * HEAD_DIM:(head + 1) * HEAD_DIM] = out_tile


def project_kernel(block_ids, me, mine, theirs, *refs):
    w_refs, (latents, upd, squares, w_all, w_sem) = refs[:8], refs[8:]
    copies = [
        pltpu.make_async_copy(w_refs[n].at[:, 3], w_all.at[pl.ds(2 * n, 2)], w_sem.at[n])
        for n in range(8)
    ]
    for copy in copies:
        copy.start()
    chunk = upd.shape[0]
    total = latents[pl.ds(pl.multiple_of(me[0] * chunk, chunk), chunk), :].astype(F32)
    for copy in copies:
        copy.wait()
    for slot in range(GROUP):
        block = block_ids[slot]
        left = jnp.where(block % 2 == me[1], mine[block // 2], theirs[block // 2])
        total += jnp.dot(left, w_all[slot], preferred_element_type=F32)
    upd[...] = total
    square = jnp.sum(total * total, axis=1, keepdims=True)
    lane = lax.broadcasted_iota(jnp.int32, (8, HEAD_DIM), 1)
    packed = jnp.zeros((8, HEAD_DIM), F32)
    for tile in range(chunk // 8):
        packed = jnp.where(lane == tile, square[8 * tile:8 * tile + 8], packed)
    for t in range(GROUP):
        squares[t] = packed


def finish_kernel(width, squares, upd, gain, out):
    total = jnp.sum(squares[...], axis=0)
    chunk = upd.shape[0]
    for tile in range(chunk // 8):
        rows = pl.ds(8 * tile, 8)
        mean_sq = total[:, tile:tile + 1] / width
        u = upd[rows, :]
        normed = gain[...] * u * lax.rsqrt(mean_sq + 1e-05)
        for a in range(GROUP):
            out[a, 0, rows, :] = u.astype(BF16)
            out[a, 1, rows, :] = normed.astype(BF16)


def whole(count):
    return [pl.BlockSpec(memory_space=pltpu.VMEM)] * count


def body(tokens, valid, latents, w_query, w_key, w_value, w_out, gain):
    me = lax.axis_index("agent")
    rows, depth = tokens.shape
    chunk = latents.shape[0] // GROUP
    width = depth * lax.axis_size("tensor")
    both = jnp.concatenate([tokens, latents], axis=0)
    feats = lax.all_gather(both, "tensor", axis=0, tiled=False)
    weights = gather_weights(w_query, w_key, w_value, w_out)
    block_ids = block_table()
    place = jnp.stack([me, lax.axis_index("tensor") % 2]).astype(jnp.int32)
    smem = pl.BlockSpec(memory_space=pltpu.SMEM)
    anywhere = pl.BlockSpec(memory_space=pl.ANY)
    partial = pl.pallas_call(
        attend_kernel,
        out_shape=jax.ShapeDtypeStruct((GROUP, 2 * chunk + 8, HEAD_DIM), F32),
        in_specs=[smem] + [anywhere] * 9 + whole(1),
        out_specs=whole(1)[0],
        scratch_shapes=[
            pltpu.VMEM((GROUP, 2 * rows, depth), BF16),
            pltpu.VMEM((GROUP, 3, depth, depth), BF16),
            pltpu.VMEM((GROUP, chunk // 8, 8, HEAD_DIM), F32),
            pltpu.SemaphoreType.DMA((GROUP,)),
            pltpu.SemaphoreType.DMA((8,)),
        ],
        compiler_params=pltpu.CompilerParams(vmem_limit_bytes=60 * 2**20),
        name="attend",
    )(block_ids, feats, *weights, valid.reshape(1, rows))
    partial = lax.all_to_all(partial, "agent", 0, 0)
    attended = pl.pallas_call(
        combine_kernel,
        out_shape=jax.ShapeDtypeStruct((GROUP // 2, chunk, depth), BF16),
        in_specs=whole(1),
        out_specs=whole(1)[0],
        name="combine",
    )(partial)
    same_core = [list(range(core, GROUP, 2)) for core in range(2)]
    attended = lax.all_to_all(attended, "tensor", 0, 0, axis_index_groups=same_core)
    theirs = other_core(attended)
    upd, squares = pl.pallas_call(
        project_kernel,
        out_shape=(jax.ShapeDtypeStruct((chunk, depth), F32),
                   jax.ShapeDtypeStruct((GROUP, 8, HEAD_DIM), F32)),
        in_specs=[smem, smem] + whole(2) + [anywhere] * 8 + whole(1),
        out_specs=tuple(whole(2)),
        scratch_shapes=[
            pltpu.VMEM((GROUP, depth, depth), BF16),
            pltpu.SemaphoreType.DMA((8,)),
        ],
        compiler_params=pltpu.CompilerParams(vmem_limit_bytes=60 * 2**20),
        name="project",
    )(block_ids, place, attended, theirs, *weights, latents)
    squares = lax.all_to_all(squares, "tensor", 0, 0)
    out = pl.pallas_call(
        lambda *refs: finish_kernel(width, *refs),
        out_shape=jax.ShapeDtypeStruct((GROUP, 2, chunk, depth), BF16),
        in_specs=whole(3),
        out_specs=whole(1)[0],
        name="finish",
    )(squares, upd, gain.reshape(1, depth))
    out = lax.all_to_all(out, "agent", 0, 0)
    return out[:, 0].reshape(-1, depth), out[:, 1].reshape(-1, depth)


def solution(mesh):
    return jax.shard_map(
        body,
        mesh=mesh,
        in_specs=(
            P("agent", "tensor"),
            P("agent"),
            P(None, "tensor"),
            P("agent", "tensor"),
            P("agent", "tensor"),
            P("agent", "tensor"),
            P("agent", "tensor"),
            P("tensor"),
        ),
        out_specs=(P(None, "tensor"), P(None, "tensor")),
        check_vma=False,
    )
```

time: 172 us -> 159 us (0.924)
  local copies, waits for them, and re-layouts: 11.7 us -> 4.12 us
  starting transfers between devices: 22.8 us -> 16.9 us
  blocking collectives: 62.9 us -> 57 us
  waiting for transfers between devices: 39.9 us -> 44.6 us
    all_to_all x1, blocking collectives: 23.8 us -> 11.9 us  [body(): lax.all_to_all(attended, 'tensor', 0, 0, axis_index_groups=same_core)]
    ppermute x20 -> x11, starting transfers between devices: 22.7 us -> 16.9 us  [the longest x6 6.89 us: second(): lax.ppermute(array, ('agent', 'tensor'), pairs(lambda y, x, core: (y + by...]
    unnamed x44 -> x21, local copies, waits for them, and re-layouts: 8.21 us -> 2.56 us
    all_to_all x1, blocking collectives: 14 us -> 18.2 us  [body(): partial = lax.all_to_all(partial, 'agent', 0, 0)]
    all_gather x1, waiting for transfers between devices: 0.01 us -> 3.64 us  [body(): feats = lax.all_gather(both, 'tensor', axis=0, tiled=False)]
    pallas_call x1, Pallas kernels: 1.75 us -> 3.84 us  [body(): pl.pallas_call(project_kernel, out_shape=(jax.ShapeDtypeStruct((chunk, de...]
    concatenate x6 -> x2, local copies, waits for them, and re-layouts: 1.91 us -> 0.05 us  [the longest x1 0.03 us: gather_weights(): near = jnp.concatenate([block, low], axis=0)]
    ppermute x20 -> x11, waiting for transfers between devices: 39.9 us -> 41 us  [the longest x6 30.2 us: second(): lax.ppermute(array, ('agent', 'tensor'), pairs(lambda y, x, core: (y + by...]
  transfers between devices with their start and end apart: 21 -> 12, of which waited for: 6 -> 9; matrix products, arithmetic and copies ran while one was open for 3% -> 2% of each run, Pallas kernels for 0% -> 0%
where the time goes in v3:
time: 159 us
  blocking collectives  57 us (36%)
  waiting for transfers between devices  44.6 us (28%)
  Pallas kernels  19.1 us (12%)
  starting transfers between devices  16.9 us (11%)
  between operations  14.2 us (9%)
  local copies, waits for them, and re-layouts  4.12 us (3%)
  other arithmetic  2.66 us (2%)
    ppermute x6, waiting for transfers between devices, second(): lax.ppermute(array, ('agent', 'tensor'), pairs(lambda y, x, core: (y + by...  30.2 us
    all_to_all x1, blocking collectives, body(): partial = lax.all_to_all(partial, 'agent', 0, 0)  18.2 us
    all_to_all x1, blocking collectives, body(): out = lax.all_to_all(out, 'agent', 0, 0)  14.8 us
    all_to_all x1, blocking collectives, body(): squares = lax.all_to_all(squares, 'tensor', 0, 0)  12.2 us
    all_to_all x1, blocking collectives, body(): lax.all_to_all(attended, 'tensor', 0, 0, axis_index_groups=same_core)  11.9 us
    pallas_call x1, Pallas kernels, body(): pl.pallas_call(attend_kernel, out_shape=jax.ShapeDtypeStruct((GROUP, 2 *...  11.1 us
    ppermute x4, waiting for transfers between devices, first(): lax.ppermute(array, ('agent', 'tensor'), pairs(lambda y, x, core: (y, x +...  10.3 us
    ppermute x6, starting transfers between devices, second(): lax.ppermute(array, ('agent', 'tensor'), pairs(lambda y, x, core: (y + by...  6.89 us
  transfers between devices with their start and end apart: 12, of which 9 were waited for; matrix products, arithmetic and copies ran while one was open for 2% of the time, Pallas kernels for 0%

profile of v3, /device:TPU:1, one launch (start us, length us, event | category | flops | bytes accessed | tf_op | source)
XLA Modules:
  0.0 158.6 jit_solution(17987374625845784258)
XLA Ops:
  7.2 0.0 copy-start.6
  7.2 0.0 copy-start.7
  7.2 0.0 copy-start.4
  7.2 0.0 copy-start.5
  7.2 0.0 all-gather.3.cloned.1.call-start
  7.3 2.0 %pad_maximum_fusion.1 = bf16[1024,256]{1,0:T(8,128)(2,1)} fusion(bf16[512,256]{1,0:T(8,128)(2,1)} %refs_8_.1, bf16[512,256]{1,0:T(8,128)(2,1)} %param.8), kind=kLoop, calls=%fused_computation.1 | loop fusion | flops 1048576 | bytes 1048576 | tf_op jit(solution)/shard_map/concatenate | solution.py:195
  9.2 0.0 all-gather.3.cloned.1.call-update
  9.3 0.9 constant_dynamic-update-slice_fusion.3
  10.2 0.9 constant_dynamic-update-slice_fusion.2
  11.1 0.0 copy-done.4
  11.2 0.0 copy-done.5
  11.2 2.2 %collective-permute-start = (bf16[1024,256]{1,0:T(8,128)(2,1)S(1)}, bf16[1024,256]{1,0:T(8,128)(2,1)S(1)}, u32[]{:S(2)}, u32[]{:S(2)}) collective-permute-start(bf16[1024,256]{1,0:T(8,128)(2,1)S(1)} %get-tuple-element.12), channel_id=1, source_target_pairs={{0,16},{1,65},{2,18},{3,67},{4,20},{5,69},{6,22},{7,71},{8,24},{9,... | collective-permute-start | bytes 1572872 | tf_op jit(solution)/shard_map/ppermute | solution.py:26
  13.4 1.5 collective-permute-start.1
  14.9 1.6 %collective-permute-start.3 = (bf16[512,256]{1,0:T(8,128)(2,1)S(1)}, bf16[512,256]{1,0:T(8,128)(2,1)S(1)}, u32[]{:S(2)}, u32[]{:S(2)}) collective-permute-start(bf16[512,256]{1,0:T(8,128)(2,1)S(1)} %pad_maximum_fusion.3), channel_id=1, source_target_pairs={{0,32},{1,129},{2,34},{3,131},{4,36},{5,133},{6,38},{7,135},{8,40}... | collective-permute-start | bytes 786440 | tf_op jit(solution)/shard_map/ppermute | solution.py:26
  16.6 0.0 copy-done.6
  16.6 0.0 copy-done.7
  16.6 1.5 collective-permute-start.2
  18.1 3.6 %collective-permute-done = bf16[1024,256]{1,0:T(8,128)(2,1)S(1)} collective-permute-done((bf16[1024,256]{1,0:T(8,128)(2,1)S(1)}, bf16[1024,256]{1,0:T(8,128)(2,1)S(1)}, u32[]{:S(2)}, u32[]{:S(2)}) %collective-permute-start) | collective-permute-done | bytes 524320 | tf_op jit(solution)/shard_map/ppermute | solution.py:26
  21.7 0.0 copy-start.1
  21.7 3.9 %collective-permute-done.3 = bf16[512,256]{1,0:T(8,128)(2,1)S(1)} collective-permute-done((bf16[512,256]{1,0:T(8,128)(2,1)S(1)}, bf16[512,256]{1,0:T(8,128)(2,1)S(1)}, u32[]{:S(2)}, u32[]{:S(2)}) %collective-permute-start.3) | collective-permute-done | bytes 262176 | tf_op jit(solution)/shard_map/ppermute | solution.py:26
  25.7 2.8 %collective-permute-done.2 = bf16[512,256]{1,0:T(8,128)(2,1)S(1)} collective-permute-done((bf16[512,256]{1,0:T(8,128)(2,1)S(1)}, bf16[512,256]{1,0:T(8,128)(2,1)S(1)}, u32[]{:S(2)}, u32[]{:S(2)}) %collective-permute-start.2) | collective-permute-done | bytes 262176 | tf_op jit(solution)/shard_map/ppermute | solution.py:26
  28.5 0.0 collective-permute-done.1
  28.5 0.1 pad_maximum_fusion
  28.6 0.0 copy-start
  28.6 1.0 collective-permute-start.4
  29.6 1.8 %collective-permute-start.7 = (bf16[2048,256]{1,0:T(8,128)(2,1)S(1)}, bf16[2048,256]{1,0:T(8,128)(2,1)}, u32[]{:S(2)}, u32[]{:S(2)}) collective-permute-start(bf16[2048,256]{1,0:T(8,128)(2,1)S(1)} %pad_maximum_fusion), channel_id=1, source_target_pairs={{0,192},{1,49},{2,194},{3,51},{4,196},{5,53},{6,198},{7,55},{8,200... | collective-permute-start | bytes 3145736 | tf_op jit(solution)/shard_map/ppermute | solution.py:31
  31.3 1.3 collective-permute-start.6
  32.6 0.2 collective-permute-start.5
  32.8 11.1 %collective-permute-done.4 = bf16[2048,256]{1,0:T(8,128)(2,1)S(1)} collective-permute-done((bf16[2048,256]{1,0:T(8,128)(2,1)S(1)}, bf16[2048,256]{1,0:T(8,128)(2,1)S(1)}, u32[]{:S(2)}, u32[]{:S(2)}) %collective-permute-start.4) | collective-permute-done | bytes 1048608 | tf_op jit(solution)/shard_map/ppermute | solution.py:31
  43.9 0.0 copy-start.2
  43.9 0.0 collective-permute-start.8
  43.9 0.0 collective-permute-done.7
  43.9 2.7 %collective-permute-start.9 = (bf16[2048,256]{1,0:T(8,128)(2,1)}, bf16[2048,256]{1,0:T(8,128)(2,1)}, u32[]{:S(2)}, u32[]{:S(2)}) collective-permute-start(bf16[2048,256]{1,0:T(8,128)(2,1)} %collective-permute-done.7), channel_id=1, source_target_pairs={{0,192},{1,49},{2,194},{3,51},{4,196},{5,53},{6,198},{7,55},{8,200... | collective-permute-start | bytes 3145736 | tf_op jit(solution)/shard_map/ppermute | solution.py:31
  46.6 0.7 stack.76.block_ids
  47.3 7.6 %collective-permute-done.6 = bf16[2048,256]{1,0:T(8,128)(2,1)} collective-permute-done((bf16[2048,256]{1,0:T(8,128)(2,1)S(1)}, bf16[2048,256]{1,0:T(8,128)(2,1)}, u32[]{:S(2)}, u32[]{:S(2)}) %collective-permute-start.6) | collective-permute-done | bytes 1048608 | tf_op jit(solution)/shard_map/ppermute | solution.py:31
  54.9 0.3 collective-permute-done.5
  55.2 11.2 %collective-permute-done.8 = bf16[2048,256]{1,0:T(8,128)(2,1)} collective-permute-done((bf16[2048,256]{1,0:T(8,128)(2,1)S(1)}, bf16[2048,256]{1,0:T(8,128)(2,1)}, u32[]{:S(2)}, u32[]{:S(2)}) %collective-permute-start.8) | collective-permute-done | bytes 1048608 | tf_op jit(solution)/shard_map/ppermute | solution.py:31
  66.4 0.0 collective-permute-done.9
  66.4 3.6 %all-gather.3.cloned.1.call-done = bf16[16384,256]{1,0:T(8,128)(2,1)} async-done(((bf16[1024,256]{1,0:T(8,128)(2,1)}), bf16[16384,256]{1,0:T(8,128)(2,1)}) %all-gather.3.cloned.1.call-update) | async-done | bytes 8388624 | tf_op jit(solution)/shard_map/all_gather | solution.py:196
  70.0 0.0 copy-done.1
  70.0 0.0 copy-done
  70.0 0.0 copy-done.2
  70.0 11.1 %attend.1 = f32[16,72,128]{2,1,0:T(8,128)} custom-call(s32[16]{0:T(128)} %stack.76.block_ids, bf16[16,1024,256]{2,1,0:T(8,128)(2,1)} %bitcast.33, bf16[2,4,256,256]{3,2,1,0:T(8,128)(2,1)} %bitcast.34, bf16[2,4,256,256]{3,2,1,0:T(8,128)(2,1)} %bitcast.31, bf16[2,4,256,256]{3,2,1,0:T(8,128)(2,1)} %bitcast.36, bf16[2,4,256,256]{3,2,1,0:T(8,128)(2,1)} %bitcast.22.refs_3_, ...), custom_call_target="tpu_custom_call" | custom-call | tf_op jit(solution)/shard_map/attend/pallas_call | solution.py:202
  81.1 18.2 %all_to_all.20.parts = f32[16,72,128]{2,1,0:T(8,128)} all-to-all(f32[16,72,128]{2,1,0:T(8,128)} %attend.1), channel_id=1, replica_groups=mesh['agent'=16,'tensor'=16] {'agent'}, dimensions={0} | all-to-all | bytes 1179648 | tf_op jit(solution)/shard_map/all_to_all | solution.py:217
  99.3 2.4 %combine.1 = bf16[8,32,256]{2,1,0:T(8,128)(2,1)} custom-call(f32[16,72,128]{2,1,0:T(8,128)} %all_to_all.20.parts), custom_call_target="tpu_custom_call" | custom-call | tf_op jit(solution)/shard_map/combine/pallas_call | solution.py:218
  101.6 11.9 %all_to_all.21.mine = bf16[8,32,256]{2,1,0:T(8,128)(2,1)S(1)} all-to-all(bf16[8,32,256]{2,1,0:T(8,128)(2,1)} %combine.1), channel_id=1, replica_groups={{0,2,4,6,8,10,12,14},{1,3,5,7,9,11,13,15},{16,18,20,22,24,26,28,30},{17..., dimensions={0} | all-to-all | bytes 262144 | tf_op jit(solution)/shard_map/all_to_all | solution.py:226
  113.6 0.0 copy-start.3
  113.6 3.1 %collective-permute-start.10 = (bf16[8,32,256]{2,1,0:T(8,128)(2,1)S(1)}, bf16[8,32,256]{2,1,0:T(8,128)(2,1)S(1)}, u32[]{:S(2)}, u32[]{:S(2)}) collective-permute-start(bf16[8,32,256]{2,1,0:T(8,128)(2,1)S(1)} %all_to_all.21.mine), channel_id=1, source_target_pairs={{0,1},{1,0},{2,3},{3,2},{4,5},{5,4},{6,7},{7,6},{8,9},{9,8},{10,11... | collective-permute-start | bytes 393224 | tf_op jit(solution)/shard_map/ppermute | solution.py:36
  116.7 0.6 pad_add_fusion.me
  117.2 0.4 collective-permute-done.10.theirs
  117.7 0.0 copy-done.3
  117.7 0.0 copy-start.8
  117.7 0.7 copy-done.8
  118.3 3.8 %project.1 = (f32[32,256]{1,0:T(8,128)}, f32[16,8,128]{2,1,0:T(8,128)}) custom-call(s32[16]{0:T(128)} %stack.76.block_ids, s32[2]{0:T(128)} %pad_add_fusion.me, bf16[8,32,256]{2,1,0:T(8,128)(2,1)} %copy-done.3, bf16[8,32,256]{2,1,0:T(8,128)(2,1)} %copy-done.8, bf16[2,4,256,256]{3,2,1,0:T(8,128)(2,1)} %bitcast.35, bf16[2,4,256,256]{3,2,1,0:T(8,128)(2,1)} %bitcast.32, ...), custom_call_target="tpu_custom_call" | custom-call | tf_op jit(solution)/shard_map/project/pallas_call | solution.py:228
  122.2 12.2 %all_to_all.22.refs_0_ = f32[16,8,128]{2,1,0:T(8,128)} all-to-all(f32[16,8,128]{2,1,0:T(8,128)} %get-tuple-element.8), channel_id=1, replica_groups=mesh['agent'=16,'tensor'=16] {'tensor'}, dimensions={0} | all-to-all | bytes 131072 | tf_op jit(solution)/shard_map/all_to_all | solution.py:241
  134.3 1.8 %finish.1 = bf16[16,2,32,256]{3,2,1,0:T(8,128)(2,1)} custom-call(f32[16,8,128]{2,1,0:T(8,128)} %all_to_all.22.refs_0_, f32[32,256]{1,0:T(8,128)} %get-tuple-element.9.refs_1_, f32[1,256]{1,0:T(1,128)} %bitcast.41), custom_call_target="tpu_custom_call" | custom-call | tf_op jit(solution)/shard_map/finish/pallas_call | solution.py:242
  136.1 14.8 %all_to_all.23 = bf16[16,2,32,256]{3,2,1,0:T(8,128)(2,1)S(1)} all-to-all(bf16[16,2,32,256]{3,2,1,0:T(8,128)(2,1)} %finish.1), channel_id=1, replica_groups=mesh['agent'=16,'tensor'=16] {'agent'}, dimensions={0} | all-to-all | bytes 1048576 | tf_op jit(solution)/shard_map/all_to_all | solution.py:249
  150.9 0.8 fusion
  (5 shorter events, 0.1 us)
Async XLA Ops:
  7.2 9.4 %copy-start.6 = (bf16[256,256]{1,0:T(8,128)(2,1)S(1)}, bf16[256,256]{1,0:T(8,128)(2,1)}, u32[]{:S(2)}) copy-start(bf16[256,256]{1,0:T(8,128)(2,1)} %param.11) | copy-start | bytes 393220
  7.2 9.4 %copy-start.7 = (bf16[256,256]{1,0:T(8,128)(2,1)S(1)}, bf16[256,256]{1,0:T(8,128)(2,1)}, u32[]{:S(2)}) copy-start(bf16[256,256]{1,0:T(8,128)(2,1)} %param.12) | copy-start | bytes 393220
  7.2 3.9 %copy-start.4 = (bf16[256,256]{1,0:T(8,128)(2,1)S(1)}, bf16[256,256]{1,0:T(8,128)(2,1)}, u32[]{:S(2)}) copy-start(bf16[256,256]{1,0:T(8,128)(2,1)} %param.13) | copy-start | bytes 393220
  7.2 4.0 %copy-start.5 = (bf16[256,256]{1,0:T(8,128)(2,1)S(1)}, bf16[256,256]{1,0:T(8,128)(2,1)}, u32[]{:S(2)}) copy-start(bf16[256,256]{1,0:T(8,128)(2,1)} %param.14) | copy-start | bytes 393220
  7.2 62.8 %all-gather.3.cloned.1.call-start = ((), (), s32[]{:S(2)}) async-start(), calls=%async_computation.4 | async-start | bytes 8912896 | tf_op jit(solution)/shard_map/all_gather | solution.py:196
  11.2 10.5 %collective-permute-start = (bf16[1024,256]{1,0:T(8,128)(2,1)S(1)}, bf16[1024,256]{1,0:T(8,128)(2,1)S(1)}, u32[]{:S(2)}, u32[]{:S(2)}) collective-permute-start(bf16[1024,256]{1,0:T(8,128)(2,1)S(1)} %get-tuple-element.12), channel_id=1, source_target_pairs={{0,16},{1,65},{2,18},{3,67},{4,20},{5,69},{6,22},{7,71},{8,24},{9,... | collective-permute-start | bytes 1572872 | tf_op jit(solution)/shard_map/ppermute | solution.py:26
  13.4 15.1 %collective-permute-start.1 = (bf16[1024,256]{1,0:T(8,128)(2,1)S(1)}, bf16[1024,256]{1,0:T(8,128)(2,1)S(1)}, u32[]{:S(2)}, u32[]{:S(2)}) collective-permute-start(bf16[1024,256]{1,0:T(8,128)(2,1)S(1)} %get-tuple-element.12), channel_id=1, source_target_pairs={{0,48},{1,193},{2,50},{3,195},{4,52},{5,197},{6,54},{7,199},{8,56}... | collective-permute-start | bytes 1572872 | tf_op jit(solution)/shard_map/ppermute | solution.py:26
  14.9 10.7 %collective-permute-start.3 = (bf16[512,256]{1,0:T(8,128)(2,1)S(1)}, bf16[512,256]{1,0:T(8,128)(2,1)S(1)}, u32[]{:S(2)}, u32[]{:S(2)}) collective-permute-start(bf16[512,256]{1,0:T(8,128)(2,1)S(1)} %pad_maximum_fusion.3), channel_id=1, source_target_pairs={{0,32},{1,129},{2,34},{3,131},{4,36},{5,133},{6,38},{7,135},{8,40}... | collective-permute-start | bytes 786440 | tf_op jit(solution)/shard_map/ppermute | solution.py:26
  16.6 11.9 %collective-permute-start.2 = (bf16[512,256]{1,0:T(8,128)(2,1)S(1)}, bf16[512,256]{1,0:T(8,128)(2,1)S(1)}, u32[]{:S(2)}, u32[]{:S(2)}) collective-permute-start(bf16[512,256]{1,0:T(8,128)(2,1)S(1)} %pad_maximum_fusion.2), channel_id=1, source_target_pairs={{0,32},{1,129},{2,34},{3,131},{4,36},{5,133},{6,38},{7,135},{8,40}... | collective-permute-start | bytes 786440 | tf_op jit(solution)/shard_map/ppermute | solution.py:26
  21.7 48.3 %copy-start.1 = (bf16[2048,256]{1,0:T(8,128)(2,1)}, bf16[2048,256]{1,0:T(8,128)(2,1)S(1)}, u32[]{:S(2)}) copy-start(bf16[2048,256]{1,0:T(8,128)(2,1)S(1)} %constant_dynamic-update-slice_fusion.4) | copy-start | bytes 3145732
  28.6 41.5 %copy-start = (bf16[2048,256]{1,0:T(8,128)(2,1)}, bf16[2048,256]{1,0:T(8,128)(2,1)S(1)}, u32[]{:S(2)}) copy-start(bf16[2048,256]{1,0:T(8,128)(2,1)S(1)} %pad_maximum_fusion) | copy-start | bytes 3145732
  28.6 15.3 %collective-permute-start.4 = (bf16[2048,256]{1,0:T(8,128)(2,1)S(1)}, bf16[2048,256]{1,0:T(8,128)(2,1)S(1)}, u32[]{:S(2)}, u32[]{:S(2)}) collective-permute-start(bf16[2048,256]{1,0:T(8,128)(2,1)S(1)} %constant_dynamic-update-slice_fusion.4), channel_id=1, source_target_pairs={{0,64},{1,17},{2,66},{3,19},{4,68},{5,21},{6,70},{7,23},{8,72},{9,... | collective-permute-start | bytes 3145736 | tf_op jit(solution)/shard_map/ppermute | solution.py:31
  29.6 14.4 %collective-permute-start.7 = (bf16[2048,256]{1,0:T(8,128)(2,1)S(1)}, bf16[2048,256]{1,0:T(8,128)(2,1)}, u32[]{:S(2)}, u32[]{:S(2)}) collective-permute-start(bf16[2048,256]{1,0:T(8,128)(2,1)S(1)} %pad_maximum_fusion), channel_id=1, source_target_pairs={{0,192},{1,49},{2,194},{3,51},{4,196},{5,53},{6,198},{7,55},{8,200... | collective-permute-start | bytes 3145736 | tf_op jit(solution)/shard_map/ppermute | solution.py:31
  31.3 23.5 %collective-permute-start.6 = (bf16[2048,256]{1,0:T(8,128)(2,1)S(1)}, bf16[2048,256]{1,0:T(8,128)(2,1)}, u32[]{:S(2)}, u32[]{:S(2)}) collective-permute-start(bf16[2048,256]{1,0:T(8,128)(2,1)S(1)} %constant_dynamic-update-slice_fusion.4), channel_id=1, source_target_pairs={{0,192},{1,49},{2,194},{3,51},{4,196},{5,53},{6,198},{7,55},{8,200... | collective-permute-start | bytes 3145736 | tf_op jit(solution)/shard_map/ppermute | solution.py:31
  32.6 22.5 %collective-permute-start.5 = (bf16[2048,256]{1,0:T(8,128)(2,1)S(1)}, bf16[2048,256]{1,0:T(8,128)(2,1)}, u32[]{:S(2)}, u32[]{:S(2)}) collective-permute-start(bf16[2048,256]{1,0:T(8,128)(2,1)S(1)} %pad_maximum_fusion), channel_id=1, source_target_pairs={{0,64},{1,17},{2,66},{3,19},{4,68},{5,21},{6,70},{7,23},{8,72},{9,... | collective-permute-start | bytes 3145736 | tf_op jit(solution)/shard_map/ppermute | solution.py:31
  43.9 26.1 %copy-start.2 = (bf16[2048,256]{1,0:T(8,128)(2,1)}, bf16[2048,256]{1,0:T(8,128)(2,1)S(1)}, u32[]{:S(2)}) copy-start(bf16[2048,256]{1,0:T(8,128)(2,1)S(1)} %collective-permute-done.4) | copy-start | bytes 3145732
  43.9 22.5 %collective-permute-start.8 = (bf16[2048,256]{1,0:T(8,128)(2,1)S(1)}, bf16[2048,256]{1,0:T(8,128)(2,1)}, u32[]{:S(2)}, u32[]{:S(2)}) collective-permute-start(bf16[2048,256]{1,0:T(8,128)(2,1)S(1)} %collective-permute-done.4), channel_id=1, source_target_pairs={{0,64},{1,17},{2,66},{3,19},{4,68},{5,21},{6,70},{7,23},{8,72},{9,... | collective-permute-start | bytes 3145736 | tf_op jit(solution)/shard_map/ppermute | solution.py:31
  43.9 22.5 %collective-permute-start.9 = (bf16[2048,256]{1,0:T(8,128)(2,1)}, bf16[2048,256]{1,0:T(8,128)(2,1)}, u32[]{:S(2)}, u32[]{:S(2)}) collective-permute-start(bf16[2048,256]{1,0:T(8,128)(2,1)} %collective-permute-done.7), channel_id=1, source_target_pairs={{0,192},{1,49},{2,194},{3,51},{4,196},{5,53},{6,198},{7,55},{8,200... | collective-permute-start | bytes 3145736 | tf_op jit(solution)/shard_map/ppermute | solution.py:31
  113.6 4.1 %copy-start.3 = (bf16[8,32,256]{2,1,0:T(8,128)(2,1)}, bf16[8,32,256]{2,1,0:T(8,128)(2,1)S(1)}, u32[]{:S(2)}) copy-start(bf16[8,32,256]{2,1,0:T(8,128)(2,1)S(1)} %all_to_all.21.mine) | copy-start | bytes 393220
  113.6 4.1 %collective-permute-start.10 = (bf16[8,32,256]{2,1,0:T(8,128)(2,1)S(1)}, bf16[8,32,256]{2,1,0:T(8,128)(2,1)S(1)}, u32[]{:S(2)}, u32[]{:S(2)}) collective-permute-start(bf16[8,32,256]{2,1,0:T(8,128)(2,1)S(1)} %all_to_all.21.mine), channel_id=1, source_target_pairs={{0,1},{1,0},{2,3},{3,2},{4,5},{5,4},{6,7},{7,6},{8,9},{9,8},{10,11... | collective-permute-start | bytes 393224 | tf_op jit(solution)/shard_map/ppermute | solution.py:36
  117.7 0.7 copy-start.8
Sparse Core Ops, SparseCore 0:
  9.9 60.1 all-gather.2

commit v4 on v3

--- a/solution.py
+++ b/solution.py
@@ -32,70 +32,85 @@
         lambda y, x, core: (y + by, x) if core == 0 else (y, x + by)))
 
 
+def along_z(array):
+    return lax.ppermute(array, "tensor", [(t, (t + 2 - 4 * (t % 2)) % GROUP) for t in range(GROUP)])
+
+
 def other_core(array):
     return lax.ppermute(array, "tensor", [(t, t ^ 1) for t in range(GROUP)])
 
 
-def gather_weights(*weights):
-    block = jnp.concatenate(weights, axis=0)
+def gather(own, block):
     half = block.shape[0] // 2
     low = first(block, 1)
     high = first(block, -1)
     far_top = first(block[:half], 2)
     far_bottom = first(block[half:], -2)
+    a0, b0 = own, other_core(own)
+    a1 = along_z(a0)
+    low, high, far_top, far_bottom, a0, b0, a1 = lax.optimization_barrier(
+        (low, high, far_top, far_bottom, a0, b0, a1))
     near = jnp.concatenate([block, low], axis=0)
     rest = jnp.concatenate([high, far_top, far_bottom], axis=0)
-    near, rest = lax.optimization_barrier((near, rest))
     near_low = second(near, 1)
     rest_high = second(rest, -1)
     rest_low = second(rest, 1)
     near_high = second(near, -1)
+    a2, b1 = along_z(a1), along_z(b0)
+    a1s = other_core(a1)
+    near_low, rest_high, a1, a1s, a2, b1 = lax.optimization_barrier(
+        (near_low, rest_high, a1, a1s, a2, b1))
     near_far = second(near_low, 1)
     rest_far = second(rest_high, -1)
-    parts = near, rest, near_low, rest_low, near_high, rest_high, near_far, rest_far
-    return [part.reshape(2, len(weights), *weights[0].shape) for part in parts]
-
-
-def block_table():
-    agent, core = lax.axis_index("agent"), lax.axis_index("tensor") % 2
-    y, x = agent // SIDE, agent % SIDE
+    a3, b2 = along_z(a2), along_z(b1)
+    a2s, b1s = other_core(a2), other_core(b1)
+    rest_low, near_high, a3, b2, a2s, b1s = lax.optimization_barrier(
+        (rest_low, near_high, a3, b2, a2s, b1s))
+    a4, b3 = along_z(a3), along_z(b2)
+    a3s, b2s = other_core(a3), other_core(b2)
+    a4s, b3s = other_core(a4), other_core(b3)
+    pieces = [a0, b0, a1, b1, a1s, b1s, a2, b2, a2s, b2s, a3, b3, a3s, b3s, a4, a4s]
+    return pieces, [near, rest, near_low, rest_low, near_high, rest_high, near_far, rest_far]
+
+
+def tables():
+    agent, tensor = lax.axis_index("agent"), lax.axis_index("tensor")
+    y, x, z, core = agent // SIDE, agent % SIDE, tensor // 2, tensor % 2
     table = []
     for i in STEPS:
         for j in STEPS:
             dy, dx = jnp.where(core == 0, i, j), jnp.where(core == 0, j, i)
             table.append((y + dy + SIDE) % SIDE * SIDE + (x + dx + SIDE) % SIDE)
-    return jnp.stack(table).astype(jnp.int32)
-
-
-def attend_kernel(block_ids, feats, *refs):
-    w_refs = refs[:8]
-    valid, out, x_all, w_all, stat, x_sem, w_sem = refs[8:]
-    rows = feats.shape[1] // 2
-    depth = feats.shape[2]
-    x_copies = [
-        pltpu.make_async_copy(feats.at[block_ids[slot]], x_all.at[slot], x_sem.at[slot])
-        for slot in range(GROUP)
+    chips = GROUP // 2
+    back = 2 * core - 1
+    for k in range(chips // 2 + 1):
+        for way in (1, -1) if 0 < k < chips // 2 else (1,):
+            chip = (z + way * back * k + chips) % chips
+            turn = core if way == 1 else 1 - core
+            table += [2 * chip + turn, 2 * chip + 1 - turn]
+    return jnp.stack(table + [agent, core]).astype(jnp.int32)
+
+
+def attend_kernel(table, *refs):
+    x_refs, w_refs = refs[:GROUP], refs[GROUP:GROUP + 8]
+    valid, out, x_all, stat, x_sem = refs[GROUP + 8:]
+    rows = x_all.shape[1] // 2
+    depth = x_all.shape[2]
+    copies = [
+        pltpu.make_async_copy(x_refs[n], x_all.at[table[GROUP + n]], x_sem.at[n])
+        for n in range(GROUP)
     ]
-    w_copies = [
-        pltpu.make_async_copy(
-            w_refs[n].at[:, pl.ds(0, 3)], w_all.at[pl.ds(2 * n, 2)], w_sem.at[n])
-        for n in range(8)
-    ]
-    copies = [
-        x_copies[part * SIDE:(part + 1) * SIDE] + w_copies[2 * part:2 * part + 2]
-        for part in range(SIDE)
-    ]
-    for part in copies:
-        for copy in part:
-            copy.start()
+    for copy in copies:
+        copy.start()
+    for copy in copies:
+        copy.wait()
     sums = [None] * 3
     for part in range(SIDE):
-        for copy in copies[part]:
-            copy.wait()
+        lefts = [x_all.at[table[part * SIDE + j]] for j in range(SIDE)]
         for n, top in enumerate((rows, 0, 0)):
-            left = jnp.concatenate(
-                [x_all[part * SIDE + j, pl.ds(top, rows), :] for j in range(SIDE)], axis=1)
-            right = w_all[pl.ds(part * SIDE, SIDE), n].reshape(SIDE * depth, -1)
+            left = jnp.concatenate([ref[pl.ds(top, rows), :] for ref in lefts], axis=1)
+            right = jnp.concatenate(
+                [w_refs[2 * part + m][:, n].reshape(2 * depth, -1) for m in range(2)], axis=0)
             more = jnp.dot(left, right, preferred_element_type=F32)
             sums[n] = more if sums[n] is None else sums[n] + more
     query, keys, values = sums
@@ -144,22 +159,23 @@
                 out[t, pl.ds(8 * tile, 8), head * HEAD_DIM:(head + 1) * HEAD_DIM] = out_tile
 
 
-def project_kernel(block_ids, me, mine, theirs, *refs):
-    w_refs, (latents, upd, squares, w_all, w_sem) = refs[:8], refs[8:]
-    copies = [
-        pltpu.make_async_copy(w_refs[n].at[:, 3], w_all.at[pl.ds(2 * n, 2)], w_sem.at[n])
-        for n in range(8)
-    ]
-    for copy in copies:
-        copy.start()
-    chunk = upd.shape[0]
-    total = latents[pl.ds(pl.multiple_of(me[0] * chunk, chunk), chunk), :].astype(F32)
-    for copy in copies:
-        copy.wait()
-    for slot in range(GROUP):
-        block = block_ids[slot]
-        left = jnp.where(block % 2 == me[1], mine[block // 2], theirs[block // 2])
-        total += jnp.dot(left, w_all[slot], preferred_element_type=F32)
+def project_kernel(table, mine, theirs, *refs):
+    w_refs, (latents, upd, squares, rows, sem) = refs[:8], refs[8:]
+    chunk, depth = upd.shape
+    agent, core = table[2 * GROUP], table[2 * GROUP + 1]
+    copy = pltpu.make_async_copy(
+        latents.at[pl.ds(pl.multiple_of(agent * chunk, chunk), chunk)], rows, sem)
+    copy.start()
+    total = jnp.zeros((chunk, depth), F32)
+    for n in range(8):
+        lefts = []
+        for m in range(2):
+            block = table[2 * n + m]
+            lefts.append(jnp.where(block % 2 == core, mine[block // 2], theirs[block // 2]))
+        total += jnp.dot(jnp.concatenate(lefts, axis=1), w_refs[n][:, 3].reshape(2 * depth, depth),
+                         preferred_element_type=F32)
+    copy.wait()
+    total += rows[...].astype(F32)
     upd[...] = total
     square = jnp.sum(total * total, axis=1, keepdims=True)
     lane = lax.broadcasted_iota(jnp.int32, (8, HEAD_DIM), 1)
@@ -188,32 +204,29 @@
 
 
 def body(tokens, valid, latents, w_query, w_key, w_value, w_out, gain):
-    me = lax.axis_index("agent")
     rows, depth = tokens.shape
     chunk = latents.shape[0] // GROUP
     width = depth * lax.axis_size("tensor")
-    both = jnp.concatenate([tokens, latents], axis=0)
-    feats = lax.all_gather(both, "tensor", axis=0, tiled=False)
-    weights = gather_weights(w_query, w_key, w_value, w_out)
-    block_ids = block_table()
-    place = jnp.stack([me, lax.axis_index("tensor") % 2]).astype(jnp.int32)
+    pieces, weights = gather(
+        jnp.concatenate([tokens, latents], axis=0),
+        jnp.concatenate([w_query, w_key, w_value, w_out], axis=0))
+    weights = [part.reshape(2, 4, depth, depth) for part in weights]
+    table = tables()
     smem = pl.BlockSpec(memory_space=pltpu.SMEM)
     anywhere = pl.BlockSpec(memory_space=pl.ANY)
     partial = pl.pallas_call(
         attend_kernel,
         out_shape=jax.ShapeDtypeStruct((GROUP, 2 * chunk + 8, HEAD_DIM), F32),
-        in_specs=[smem] + [anywhere] * 9 + whole(1),
+        in_specs=[smem] + [anywhere] * GROUP + whole(9),
         out_specs=whole(1)[0],
         scratch_shapes=[
             pltpu.VMEM((GROUP, 2 * rows, depth), BF16),
-            pltpu.VMEM((GROUP, 3, depth, depth), BF16),
             pltpu.VMEM((GROUP, chunk // 8, 8, HEAD_DIM), F32),
             pltpu.SemaphoreType.DMA((GROUP,)),
-            pltpu.SemaphoreType.DMA((8,)),
         ],
-        compiler_params=pltpu.CompilerParams(vmem_limit_bytes=60 * 2**20),
+        compiler_params=pltpu.CompilerParams(vmem_limit_bytes=24 * 2**20),
         name="attend",
-    )(block_ids, feats, *weights, valid.reshape(1, rows))
+    )(table, *pieces, *weights, valid.reshape(1, rows))
     partial = lax.all_to_all(partial, "agent", 0, 0)
     attended = pl.pallas_call(
         combine_kernel,
@@ -229,15 +242,15 @@
         project_kernel,
         out_shape=(jax.ShapeDtypeStruct((chunk, depth), F32),
                    jax.ShapeDtypeStruct((GROUP, 8, HEAD_DIM), F32)),
-        in_specs=[smem, smem] + whole(2) + [anywhere] * 8 + whole(1),
+        in_specs=[smem] + whole(10) + [anywhere],
         out_specs=tuple(whole(2)),
         scratch_shapes=[
-            pltpu.VMEM((GROUP, depth, depth), BF16),
-            pltpu.SemaphoreType.DMA((8,)),
+            pltpu.VMEM((chunk, depth), BF16),
+            pltpu.SemaphoreType.DMA,
         ],
-        compiler_params=pltpu.CompilerParams(vmem_limit_bytes=60 * 2**20),
+        compiler_params=pltpu.CompilerParams(vmem_limit_bytes=16 * 2**20),
         name="project",
-    )(block_ids, place, attended, theirs, *weights, latents)
+    )(table, attended, theirs, *weights, latents)
     squares = lax.all_to_all(squares, "tensor", 0, 0)
     out = pl.pallas_call(
         lambda *refs: finish_kernel(width, *refs),

time: 159 us -> 179 us (1.13)
  starting transfers between devices: 16.9 us -> 53.2 us
  local copies, waits for them, and re-layouts: 4.12 us -> 25.8 us
  waiting for transfers between devices: 44.6 us -> 27.3 us
  between operations: 14.2 us -> 0.93 us
  blocking collectives: 57 us -> 53.8 us
  other arithmetic: 2.66 us -> 0.04 us
  Pallas kernels: 19.1 us -> 16.7 us
    ppermute x6, waiting for transfers between devices: 30.2 us -> 6.67 us  [second(): lax.ppermute(array, ('agent', 'tensor'), pairs(lambda y, x, core: (y + by...]
    unnamed x21 -> x73, local copies, waits for them, and re-layouts: 2.56 us -> 24.8 us
    ppermute x1 -> x9, starting transfers between devices: 3.11 us -> 23 us  [other_core(): return lax.ppermute(array, 'tensor', [(t, t ^ 1) for t in range(GROUP)])]
    ppermute x0 -> x7, starting transfers between devices: none -> 17.4 us  [along_z(): lax.ppermute(array, 'tensor', [(t, (t + 2 - 4 * (t % 2)) % GROUP) for t i...]
    ppermute x0 -> x7, waiting for transfers between devices: none -> 9.25 us  [along_z(): lax.ppermute(array, 'tensor', [(t, (t + 2 - 4 * (t % 2)) % GROUP) for t i...]
    all_gather x1 -> x0, waiting for transfers between devices: 3.64 us -> none  [body(): feats = lax.all_gather(both, 'tensor', axis=0, tiled=False)]
    all_to_all x1, blocking collectives: 18.2 us -> 15 us  [body(): partial = lax.all_to_all(partial, 'agent', 0, 0)]
    ppermute x1 -> x9, waiting for transfers between devices: 0.41 us -> 2.73 us  [other_core(): return lax.ppermute(array, 'tensor', [(t, t ^ 1) for t in range(GROUP)])]
  transfers between devices with their start and end apart: 12 -> 26, of which waited for: 9 -> 11; matrix products, arithmetic and copies ran while one was open for 2% -> 0% of each run, Pallas kernels for 0% -> 0%
where the time goes in v4:
time: 179 us; the launch traced here: 178 us
  blocking collectives  53.8 us (30%)
  starting transfers between devices  53.2 us (30%)
  waiting for transfers between devices  27.3 us (15%)
  local copies, waits for them, and re-layouts  25.8 us (14%)
  Pallas kernels  16.7 us (9%)
    unnamed x73, local copies, waits for them, and re-layouts  24.8 us
    ppermute x9, starting transfers between devices, other_core(): return lax.ppermute(array, 'tensor', [(t, t ^ 1) for t in range(GROUP)])  23 us
    ppermute x7, starting transfers between devices, along_z(): lax.ppermute(array, 'tensor', [(t, (t + 2 - 4 * (t % 2)) % GROUP) for t i...  17.4 us
    all_to_all x1, blocking collectives, body(): partial = lax.all_to_all(partial, 'agent', 0, 0)  15 us
    all_to_all x1, blocking collectives, body(): out = lax.all_to_all(out, 'agent', 0, 0)  14.8 us
    all_to_all x1, blocking collectives, body(): lax.all_to_all(attended, 'tensor', 0, 0, axis_index_groups=same_core)  12.8 us
    all_to_all x1, blocking collectives, body(): squares = lax.all_to_all(squares, 'tensor', 0, 0)  11.3 us
    pallas_call x1, Pallas kernels, body(): pl.pallas_call(attend_kernel, out_shape=jax.ShapeDtypeStruct((GROUP, 2 *...  10.1 us
  transfers between devices with their start and end apart: 26, of which 11 were waited for; matrix products, arithmetic and copies ran while one was open for 0% of the time, Pallas kernels for 0%

profile of v4, /device:TPU:1, one launch (start us, length us, event | category | flops | bytes accessed | tf_op | source)
XLA Modules:
  0.0 177.7 jit_solution(61584721579956099)
XLA Ops:
  0.6 1.0 constant_dynamic-update-slice_fusion.5
  1.7 6.5 %collective-permute-start.5 = (bf16[1024,256]{1,0:T(8,128)(2,1)S(1)}, bf16[1024,256]{1,0:T(8,128)(2,1)S(1)}, u32[]{:S(2)}, u32[]{:S(2)}) collective-permute-start(bf16[1024,256]{1,0:T(8,128)(2,1)S(1)} %constant_dynamic-update-slice_fusion.4.refs_0_), channel_id=1, source_target_pairs={{0,2},{1,15},{2,4},{3,1},{4,6},{5,3},{6,8},{7,5},{8,10},{9,7},{10,... | collective-permute-start | bytes 1572872 | tf_op jit(solution)/shard_map/ppermute | solution.py:36
  8.3 3.0 %collective-permute-start.3 = (bf16[512,256]{1,0:T(8,128)(2,1)S(1)}, bf16[512,256]{1,0:T(8,128)(2,1)S(1)}, u32[]{:S(2)}, u32[]{:S(2)}) collective-permute-start(bf16[512,256]{1,0:T(8,128)(2,1)S(1)} %pad_maximum_fusion.1), channel_id=1, source_target_pairs={{0,32},{1,129},{2,34},{3,131},{4,36},{5,133},{6,38},{7,135},{8,40}... | collective-permute-start | bytes 786440 | tf_op jit(solution)/shard_map/ppermute | solution.py:26
  11.4 0.9 collective-permute-start.1
  12.3 0.7 collective-permute-start
  13.0 2.4 %collective-permute-done.3 = bf16[512,256]{1,0:T(8,128)(2,1)S(1)} collective-permute-done((bf16[512,256]{1,0:T(8,128)(2,1)S(1)}, bf16[512,256]{1,0:T(8,128)(2,1)S(1)}, u32[]{:S(2)}, u32[]{:S(2)}) %collective-permute-start.3) | collective-permute-done | bytes 262176 | tf_op jit(solution)/shard_map/ppermute | solution.py:26
  15.4 3.0 %collective-permute-start.2 = (bf16[512,256]{1,0:T(8,128)(2,1)S(1)}, bf16[512,256]{1,0:T(8,128)(2,1)S(1)}, u32[]{:S(2)}, u32[]{:S(2)}) collective-permute-start(bf16[512,256]{1,0:T(8,128)(2,1)S(1)} %pad_maximum_fusion), channel_id=1, source_target_pairs={{0,32},{1,129},{2,34},{3,131},{4,36},{5,133},{6,38},{7,135},{8,40}... | collective-permute-start | bytes 786440 | tf_op jit(solution)/shard_map/ppermute | solution.py:26
  18.3 5.5 %collective-permute-done.2 = bf16[512,256]{1,0:T(8,128)(2,1)S(1)} collective-permute-done((bf16[512,256]{1,0:T(8,128)(2,1)S(1)}, bf16[512,256]{1,0:T(8,128)(2,1)S(1)}, u32[]{:S(2)}, u32[]{:S(2)}) %collective-permute-start.2) | collective-permute-done | bytes 262176 | tf_op jit(solution)/shard_map/ppermute | solution.py:26
  23.9 0.7 collective-permute-done
  24.6 0.9 collective-permute-start.10
  25.6 2.6 %collective-permute-start.7 = (bf16[2048,256]{1,0:T(8,128)(2,1)S(1)}, bf16[2048,256]{1,0:T(8,128)(2,1)S(1)}, u32[]{:S(2)}, u32[]{:S(2)}) collective-permute-start(bf16[2048,256]{1,0:T(8,128)(2,1)S(1)} %constant_dynamic-update-slice_fusion.11), channel_id=1, source_target_pairs={{0,192},{1,49},{2,194},{3,51},{4,196},{5,53},{6,198},{7,55},{8,200... | collective-permute-start | bytes 3145736 | tf_op jit(solution)/shard_map/ppermute | solution.py:31
  28.3 1.2 collective-permute-start.9
  29.7 3.2 %collective-permute-done.10.refs_3_ = bf16[1024,256]{1,0:T(8,128)(2,1)S(1)} collective-permute-done((bf16[1024,256]{1,0:T(8,128)(2,1)S(1)}, bf16[1024,256]{1,0:T(8,128)(2,1)S(1)}, u32[]{:S(2)}, u32[]{:S(2)}) %collective-permute-start.10) | collective-permute-done | bytes 524320 | tf_op jit(solution)/shard_map/ppermute | solution.py:36
  32.9 3.9 %collective-permute-start.8 = (bf16[1024,256]{1,0:T(8,128)(2,1)S(1)}, bf16[1024,256]{1,0:T(8,128)(2,1)S(1)}, u32[]{:S(2)}, u32[]{:S(2)}) collective-permute-start(bf16[1024,256]{1,0:T(8,128)(2,1)S(1)} %collective-permute-done.5.refs_2_), channel_id=1, source_target_pairs={{0,1},{1,0},{2,3},{3,2},{4,5},{5,4},{6,7},{7,6},{8,9},{9,8},{10,11... | collective-permute-start | bytes 1572872 | tf_op jit(solution)/shard_map/ppermute | solution.py:40
  36.8 1.8 %collective-permute-done.9.refs_6_ = bf16[1024,256]{1,0:T(8,128)(2,1)S(1)} collective-permute-done((bf16[1024,256]{1,0:T(8,128)(2,1)S(1)}, bf16[1024,256]{1,0:T(8,128)(2,1)S(1)}, u32[]{:S(2)}, u32[]{:S(2)}) %collective-permute-start.9) | collective-permute-done | bytes 524320 | tf_op jit(solution)/shard_map/ppermute | solution.py:36
  38.6 2.5 %collective-permute-start.12 = (bf16[2048,256]{1,0:T(8,128)(2,1)S(1)}, bf16[2048,256]{1,0:T(8,128)(2,1)S(1)}, u32[]{:S(2)}, u32[]{:S(2)}) collective-permute-start(bf16[2048,256]{1,0:T(8,128)(2,1)S(1)} %constant_dynamic-update-slice_fusion.6), channel_id=1, source_target_pairs={{0,192},{1,49},{2,194},{3,51},{4,196},{5,53},{6,198},{7,55},{8,200... | collective-permute-start | bytes 3145736 | tf_op jit(solution)/shard_map/ppermute | solution.py:31
  41.1 0.8 copy-done.17
  42.0 1.6 collective-permute-done.6
  43.6 2.7 %collective-permute-start.16 = (bf16[1024,256]{1,0:T(8,128)(2,1)S(1)}, bf16[1024,256]{1,0:T(8,128)(2,1)S(1)}, u32[]{:S(2)}, u32[]{:S(2)}) collective-permute-start(bf16[1024,256]{1,0:T(8,128)(2,1)S(1)} %collective-permute-done.10.refs_3_), channel_id=1, source_target_pairs={{0,1},{1,0},{2,3},{3,2},{4,5},{5,4},{6,7},{7,6},{8,9},{9,8},{10,11... | collective-permute-start | bytes 1572872 | tf_op jit(solution)/shard_map/ppermute | solution.py:40
  46.3 2.5 %collective-permute-start.14 = (bf16[1024,256]{1,0:T(8,128)(2,1)S(1)}, bf16[1024,256]{1,0:T(8,128)(2,1)S(1)}, u32[]{:S(2)}, u32[]{:S(2)}) collective-permute-start(bf16[1024,256]{1,0:T(8,128)(2,1)S(1)} %collective-permute-done.10.refs_3_), channel_id=1, source_target_pairs={{0,2},{1,15},{2,4},{3,1},{4,6},{5,3},{6,8},{7,5},{8,10},{9,7},{10,... | collective-permute-start | bytes 1572872 | tf_op jit(solution)/shard_map/ppermute | solution.py:36
  48.8 0.9 copy-done.13
  49.7 5.0 %collective-permute-done.11 = bf16[2048,256]{1,0:T(8,128)(2,1)S(1)} collective-permute-done((bf16[2048,256]{1,0:T(8,128)(2,1)S(1)}, bf16[2048,256]{1,0:T(8,128)(2,1)S(1)}, u32[]{:S(2)}, u32[]{:S(2)}) %collective-permute-start.11) | collective-permute-done | bytes 1048608 | tf_op jit(solution)/shard_map/ppermute | solution.py:31
  54.7 1.0 copy-done
  55.7 1.2 collective-permute-start.13
  56.9 0.8 copy-done.15
  57.7 1.0 copy-done.3
  58.6 0.8 copy-done.19
  59.5 0.8 copy-done.23
  60.3 3.8 %collective-permute-done.13.refs_10_ = bf16[1024,256]{1,0:T(8,128)(2,1)} collective-permute-done((bf16[1024,256]{1,0:T(8,128)(2,1)S(1)}, bf16[1024,256]{1,0:T(8,128)(2,1)}, u32[]{:S(2)}, u32[]{:S(2)}) %collective-permute-start.13) | collective-permute-done | bytes 524320 | tf_op jit(solution)/shard_map/ppermute | solution.py:36
  64.1 2.1 %collective-permute-start.18 = (bf16[1024,256]{1,0:T(8,128)(2,1)S(1)}, bf16[1024,256]{1,0:T(8,128)(2,1)}, u32[]{:S(2)}, u32[]{:S(2)}) collective-permute-start(bf16[1024,256]{1,0:T(8,128)(2,1)S(1)} %collective-permute-done.14.refs_7_), channel_id=1, source_target_pairs={{0,2},{1,15},{2,4},{3,1},{4,6},{5,3},{6,8},{7,5},{8,10},{9,7},{10,... | collective-permute-start | bytes 1572872 | tf_op jit(solution)/shard_map/ppermute | solution.py:36
  66.2 2.3 %collective-permute-start.17 = (bf16[1024,256]{1,0:T(8,128)(2,1)S(1)}, bf16[1024,256]{1,0:T(8,128)(2,1)S(1)}, u32[]{:S(2)}, u32[]{:S(2)}) collective-permute-start(bf16[1024,256]{1,0:T(8,128)(2,1)S(1)} %collective-permute-done.14.refs_7_), channel_id=1, source_target_pairs={{0,1},{1,0},{2,3},{3,2},{4,5},{5,4},{6,7},{7,6},{8,9},{9,8},{10,11... | collective-permute-start | bytes 1572872 | tf_op jit(solution)/shard_map/ppermute | solution.py:40
  68.5 0.8 copy-done.21
  69.3 3.0 %collective-permute-start.21 = (bf16[1024,256]{1,0:T(8,128)(2,1)}, bf16[1024,256]{1,0:T(8,128)(2,1)}, u32[]{:S(2)}, u32[]{:S(2)}) collective-permute-start(bf16[1024,256]{1,0:T(8,128)(2,1)} %collective-permute-done.13.refs_10_), channel_id=1, source_target_pairs={{0,2},{1,15},{2,4},{3,1},{4,6},{5,3},{6,8},{7,5},{8,10},{9,7},{10,... | collective-permute-start | bytes 1572872 | tf_op jit(solution)/shard_map/ppermute | solution.py:36
  72.2 0.3 collective-permute-done.18.refs_11_
  72.6 6.4 %collective-permute-start.19 = (bf16[1024,256]{1,0:T(8,128)(2,1)}, bf16[1024,256]{1,0:T(8,128)(2,1)}, u32[]{:S(2)}, u32[]{:S(2)}) collective-permute-start(bf16[1024,256]{1,0:T(8,128)(2,1)} %collective-permute-done.13.refs_10_), channel_id=1, source_target_pairs={{0,1},{1,0},{2,3},{3,2},{4,5},{5,4},{6,7},{7,6},{8,9},{9,8},{10,11... | collective-permute-start | bytes 1572872 | tf_op jit(solution)/shard_map/ppermute | solution.py:40
  79.0 0.8 copy-done.25
  79.8 4.8 %collective-permute-start.22 = (bf16[1024,256]{1,0:T(8,128)(2,1)}, bf16[1024,256]{1,0:T(8,128)(2,1)}, u32[]{:S(2)}, u32[]{:S(2)}) collective-permute-start(bf16[1024,256]{1,0:T(8,128)(2,1)} %collective-permute-done.21.refs_14_), channel_id=1, source_target_pairs={{0,1},{1,0},{2,3},{3,2},{4,5},{5,4},{6,7},{7,6},{8,9},{9,8},{10,11... | collective-permute-start | bytes 1572872 | tf_op jit(solution)/shard_map/ppermute | solution.py:40
  84.8 1.7 collective-permute-done.22.refs_15_
  86.5 0.7 copy-done.28
  87.2 1.2 copy-done.1
  88.4 1.2 copy-done.4
  89.6 1.0 copy-done.7
  90.7 1.0 copy-done.10
  91.7 1.0 copy-done.12
  92.7 1.0 copy-done.14
  93.8 1.0 copy-done.16
  94.8 1.0 copy-done.18
  95.9 1.0 copy-done.20
  96.9 1.0 copy-done.22
  97.9 1.0 copy-done.24
  99.0 1.0 copy-done.26
  100.0 10.1 %attend.1 = f32[16,72,128]{2,1,0:T(8,128)S(1)} custom-call(s32[34]{0:T(128)S(1)} %stack.139.table, bf16[1024,256]{1,0:T(8,128)(2,1)S(1)} %copy-done.7, bf16[1024,256]{1,0:T(8,128)(2,1)S(1)} %copy-done.12, bf16[1024,256]{1,0:T(8,128)(2,1)S(1)} %copy-done.10, bf16[1024,256]{1,0:T(8,128)(2,1)S(1)} %copy-done.14, bf16[1024,256]{1,0:T(8,128)(2,1)S(1)} %copy-done.18, ...), custom_call_target="tpu_custom_call" | custom-call | tf_op jit(solution)/shard_map/attend/pallas_call | solution.py:217
  110.1 15.0 %all_to_all.20.parts = f32[16,72,128]{2,1,0:T(8,128)} all-to-all(f32[16,72,128]{2,1,0:T(8,128)S(1)} %attend.1), channel_id=1, replica_groups=mesh['agent'=16,'tensor'=16] {'agent'}, dimensions={0} | all-to-all | bytes 1179648 | tf_op jit(solution)/shard_map/all_to_all | solution.py:230
  125.1 2.4 %combine.1 = bf16[8,32,256]{2,1,0:T(8,128)(2,1)} custom-call(f32[16,72,128]{2,1,0:T(8,128)} %all_to_all.20.parts), custom_call_target="tpu_custom_call" | custom-call | tf_op jit(solution)/shard_map/combine/pallas_call | solution.py:231
  127.4 12.8 %all_to_all.21.mine = bf16[8,32,256]{2,1,0:T(8,128)(2,1)S(1)} all-to-all(bf16[8,32,256]{2,1,0:T(8,128)(2,1)} %combine.1), channel_id=1, replica_groups={{0,2,4,6,8,10,12,14},{1,3,5,7,9,11,13,15},{16,18,20,22,24,26,28,30},{17..., dimensions={0} | all-to-all | bytes 262144 | tf_op jit(solution)/shard_map/all_to_all | solution.py:239
  140.2 2.9 %collective-permute-start.25 = (bf16[8,32,256]{2,1,0:T(8,128)(2,1)S(1)}, bf16[8,32,256]{2,1,0:T(8,128)(2,1)S(1)}, u32[]{:S(2)}, u32[]{:S(2)}) collective-permute-start(bf16[8,32,256]{2,1,0:T(8,128)(2,1)S(1)} %all_to_all.21.mine), channel_id=1, source_target_pairs={{0,1},{1,0},{2,3},{3,2},{4,5},{5,4},{6,7},{7,6},{8,9},{9,8},{10,11... | collective-permute-start | bytes 393224 | tf_op jit(solution)/shard_map/ppermute | solution.py:40
  143.1 1.0 collective-permute-done.25.theirs
  144.1 1.2 copy-done.2
  145.3 1.2 copy-done.5
  146.5 2.5 %project.1 = (f32[32,256]{1,0:T(8,128)S(1)}, f32[16,8,128]{2,1,0:T(8,128)S(1)}) custom-call(s32[34]{0:T(128)S(1)} %stack.139.table, bf16[8,32,256]{2,1,0:T(8,128)(2,1)S(1)} %all_to_all.21.mine, bf16[8,32,256]{2,1,0:T(8,128)(2,1)S(1)} %collective-permute-done.25.theirs, bf16[2,4,256,256]{3,2,1,0:T(8,128)(2,1)S(1)} %bitcast.49, ...), custom_call_target="tpu_custom_call" | custom-call | tf_op jit(solution)/shard_map/project/pallas_call | solution.py:241
  149.0 11.3 %all_to_all.22.refs_0_ = f32[16,8,128]{2,1,0:T(8,128)} all-to-all(f32[16,8,128]{2,1,0:T(8,128)S(1)} %get-tuple-element.42), channel_id=1, replica_groups=mesh['agent'=16,'tensor'=16] {'tensor'}, dimensions={0} | all-to-all | bytes 131072 | tf_op jit(solution)/shard_map/all_to_all | solution.py:254
  160.3 1.8 %finish.1 = bf16[16,2,32,256]{3,2,1,0:T(8,128)(2,1)} custom-call(f32[16,8,128]{2,1,0:T(8,128)} %all_to_all.22.refs_0_, f32[32,256]{1,0:T(8,128)} %copy-done.27, f32[1,256]{1,0:T(1,128)} %bitcast.59), custom_call_target="tpu_custom_call" | custom-call | tf_op jit(solution)/shard_map/finish/pallas_call | solution.py:255
  162.1 14.8 %all_to_all.23 = bf16[16,2,32,256]{3,2,1,0:T(8,128)(2,1)S(1)} all-to-all(bf16[16,2,32,256]{3,2,1,0:T(8,128)(2,1)} %finish.1), channel_id=1, replica_groups=mesh['agent'=16,'tensor'=16] {'agent'}, dimensions={0} | all-to-all | bytes 1048576 | tf_op jit(solution)/shard_map/all_to_all | solution.py:262
  176.9 0.8 fusion
  (76 shorter events, 0.7 us)
Async XLA Ops:
  0.6 1.0 copy-start.8
  1.7 6.6 %copy-start.29 = (bf16[256,256]{1,0:T(8,128)(2,1)S(1)}, bf16[256,256]{1,0:T(8,128)(2,1)}, u32[]{:S(2)}) copy-start(bf16[256,256]{1,0:T(8,128)(2,1)} %param.13) | copy-start | bytes 393220
  1.7 6.6 %copy-start.30 = (bf16[256,256]{1,0:T(8,128)(2,1)S(1)}, bf16[256,256]{1,0:T(8,128)(2,1)}, u32[]{:S(2)}) copy-start(bf16[256,256]{1,0:T(8,128)(2,1)} %param.14) | copy-start | bytes 393220
  1.7 9.6 %copy-start.6 = (bf16[1024,256]{1,0:T(8,128)(2,1)}, bf16[1024,256]{1,0:T(8,128)(2,1)S(1)}, u32[]{:S(2)}) copy-start(bf16[1024,256]{1,0:T(8,128)(2,1)S(1)} %constant_dynamic-update-slice_fusion.4.refs_0_) | copy-start | bytes 1572868
  1.7 9.5 %copy-start.31 = (bf16[256,256]{1,0:T(8,128)(2,1)S(1)}, bf16[256,256]{1,0:T(8,128)(2,1)}, u32[]{:S(2)}) copy-start(bf16[256,256]{1,0:T(8,128)(2,1)} %param.11) | copy-start | bytes 393220
  1.7 22.1 %collective-permute-start.5 = (bf16[1024,256]{1,0:T(8,128)(2,1)S(1)}, bf16[1024,256]{1,0:T(8,128)(2,1)S(1)}, u32[]{:S(2)}, u32[]{:S(2)}) collective-permute-start(bf16[1024,256]{1,0:T(8,128)(2,1)S(1)} %constant_dynamic-update-slice_fusion.4.refs_0_), channel_id=1, source_target_pairs={{0,2},{1,15},{2,4},{3,1},{4,6},{5,3},{6,8},{7,5},{8,10},{9,7},{10,... | collective-permute-start | bytes 1572872 | tf_op jit(solution)/shard_map/ppermute | solution.py:36
  8.2 15.6 %collective-permute-start.4 = (bf16[1024,256]{1,0:T(8,128)(2,1)S(1)}, bf16[1024,256]{1,0:T(8,128)(2,1)S(1)}, u32[]{:S(2)}, u32[]{:S(2)}) collective-permute-start(bf16[1024,256]{1,0:T(8,128)(2,1)S(1)} %constant_dynamic-update-slice_fusion.4.refs_0_), channel_id=1, source_target_pairs={{0,1},{1,0},{2,3},{3,2},{4,5},{5,4},{6,7},{7,6},{8,9},{9,8},{10,11... | collective-permute-start | bytes 1572872 | tf_op jit(solution)/shard_map/ppermute | solution.py:40
  8.3 3.0 %copy-start.32 = (bf16[256,256]{1,0:T(8,128)(2,1)S(1)}, bf16[256,256]{1,0:T(8,128)(2,1)}, u32[]{:S(2)}) copy-start(bf16[256,256]{1,0:T(8,128)(2,1)} %param.12) | copy-start | bytes 393220
  8.3 7.1 %collective-permute-start.3 = (bf16[512,256]{1,0:T(8,128)(2,1)S(1)}, bf16[512,256]{1,0:T(8,128)(2,1)S(1)}, u32[]{:S(2)}, u32[]{:S(2)}) collective-permute-start(bf16[512,256]{1,0:T(8,128)(2,1)S(1)} %pad_maximum_fusion.1), channel_id=1, source_target_pairs={{0,32},{1,129},{2,34},{3,131},{4,36},{5,133},{6,38},{7,135},{8,40}... | collective-permute-start | bytes 786440 | tf_op jit(solution)/shard_map/ppermute | solution.py:26
  11.4 12.5 %collective-permute-start.1 = (bf16[1024,256]{1,0:T(8,128)(2,1)S(1)}, bf16[1024,256]{1,0:T(8,128)(2,1)S(1)}, u32[]{:S(2)}, u32[]{:S(2)}) collective-permute-start(bf16[1024,256]{1,0:T(8,128)(2,1)S(1)} %get-tuple-element.47), channel_id=1, source_target_pairs={{0,48},{1,193},{2,50},{3,195},{4,52},{5,197},{6,54},{7,199},{8,56}... | collective-permute-start | bytes 1572872 | tf_op jit(solution)/shard_map/ppermute | solution.py:26
  12.3 12.3 %collective-permute-start = (bf16[1024,256]{1,0:T(8,128)(2,1)S(1)}, bf16[1024,256]{1,0:T(8,128)(2,1)S(1)}, u32[]{:S(2)}, u32[]{:S(2)}) collective-permute-start(bf16[1024,256]{1,0:T(8,128)(2,1)S(1)} %get-tuple-element.47), channel_id=1, source_target_pairs={{0,16},{1,65},{2,18},{3,67},{4,20},{5,69},{6,22},{7,71},{8,24},{9,... | collective-permute-start | bytes 1572872 | tf_op jit(solution)/shard_map/ppermute | solution.py:26
  15.4 8.5 %collective-permute-start.2 = (bf16[512,256]{1,0:T(8,128)(2,1)S(1)}, bf16[512,256]{1,0:T(8,128)(2,1)S(1)}, u32[]{:S(2)}, u32[]{:S(2)}) collective-permute-start(bf16[512,256]{1,0:T(8,128)(2,1)S(1)} %pad_maximum_fusion), channel_id=1, source_target_pairs={{0,32},{1,129},{2,34},{3,131},{4,36},{5,133},{6,38},{7,135},{8,40}... | collective-permute-start | bytes 786440 | tf_op jit(solution)/shard_map/ppermute | solution.py:26
  23.9 9.1 %copy-start.9 = (bf16[1024,256]{1,0:T(8,128)(2,1)}, bf16[1024,256]{1,0:T(8,128)(2,1)S(1)}, u32[]{:S(2)}) copy-start(bf16[1024,256]{1,0:T(8,128)(2,1)S(1)} %collective-permute-done.5.refs_2_) | copy-start | bytes 1572868
  23.9 1.7 copy-start.11
  24.6 8.3 %collective-permute-start.10 = (bf16[1024,256]{1,0:T(8,128)(2,1)S(1)}, bf16[1024,256]{1,0:T(8,128)(2,1)S(1)}, u32[]{:S(2)}, u32[]{:S(2)}) collective-permute-start(bf16[1024,256]{1,0:T(8,128)(2,1)S(1)} %collective-permute-done.4.refs_1_), channel_id=1, source_target_pairs={{0,2},{1,15},{2,4},{3,1},{4,6},{5,3},{6,8},{7,5},{8,10},{9,7},{10,... | collective-permute-start | bytes 1572872 | tf_op jit(solution)/shard_map/ppermute | solution.py:36
  25.6 16.3 %collective-permute-start.7 = (bf16[2048,256]{1,0:T(8,128)(2,1)S(1)}, bf16[2048,256]{1,0:T(8,128)(2,1)S(1)}, u32[]{:S(2)}, u32[]{:S(2)}) collective-permute-start(bf16[2048,256]{1,0:T(8,128)(2,1)S(1)} %constant_dynamic-update-slice_fusion.11), channel_id=1, source_target_pairs={{0,192},{1,49},{2,194},{3,51},{4,196},{5,53},{6,198},{7,55},{8,200... | collective-permute-start | bytes 3145736 | tf_op jit(solution)/shard_map/ppermute | solution.py:31
  28.2 15.3 %collective-permute-start.6 = (bf16[2048,256]{1,0:T(8,128)(2,1)S(1)}, bf16[2048,256]{1,0:T(8,128)(2,1)}, u32[]{:S(2)}, u32[]{:S(2)}) collective-permute-start(bf16[2048,256]{1,0:T(8,128)(2,1)S(1)} %constant_dynamic-update-slice_fusion.6), channel_id=1, source_target_pairs={{0,64},{1,17},{2,66},{3,19},{4,68},{5,21},{6,70},{7,23},{8,72},{9,... | collective-permute-start | bytes 3145736 | tf_op jit(solution)/shard_map/ppermute | solution.py:31
  28.3 10.3 %collective-permute-start.9 = (bf16[1024,256]{1,0:T(8,128)(2,1)S(1)}, bf16[1024,256]{1,0:T(8,128)(2,1)S(1)}, u32[]{:S(2)}, u32[]{:S(2)}) collective-permute-start(bf16[1024,256]{1,0:T(8,128)(2,1)S(1)} %collective-permute-done.5.refs_2_), channel_id=1, source_target_pairs={{0,2},{1,15},{2,4},{3,1},{4,6},{5,3},{6,8},{7,5},{8,10},{9,7},{10,... | collective-permute-start | bytes 1572872 | tf_op jit(solution)/shard_map/ppermute | solution.py:36
  29.6 25.1 %collective-permute-start.11 = (bf16[2048,256]{1,0:T(8,128)(2,1)S(1)}, bf16[2048,256]{1,0:T(8,128)(2,1)S(1)}, u32[]{:S(2)}, u32[]{:S(2)}) collective-permute-start(bf16[2048,256]{1,0:T(8,128)(2,1)S(1)} %constant_dynamic-update-slice_fusion.11), channel_id=1, source_target_pairs={{0,64},{1,17},{2,66},{3,19},{4,68},{5,21},{6,70},{7,23},{8,72},{9,... | collective-permute-start | bytes 3145736 | tf_op jit(solution)/shard_map/ppermute | solution.py:31
  32.9 8.2 %collective-permute-start.8 = (bf16[1024,256]{1,0:T(8,128)(2,1)S(1)}, bf16[1024,256]{1,0:T(8,128)(2,1)S(1)}, u32[]{:S(2)}, u32[]{:S(2)}) collective-permute-start(bf16[1024,256]{1,0:T(8,128)(2,1)S(1)} %collective-permute-done.5.refs_2_), channel_id=1, source_target_pairs={{0,1},{1,0},{2,3},{3,2},{4,5},{5,4},{6,7},{7,6},{8,9},{9,8},{10,11... | collective-permute-start | bytes 1572872 | tf_op jit(solution)/shard_map/ppermute | solution.py:40
  38.6 19.0 %collective-permute-start.12 = (bf16[2048,256]{1,0:T(8,128)(2,1)S(1)}, bf16[2048,256]{1,0:T(8,128)(2,1)S(1)}, u32[]{:S(2)}, u32[]{:S(2)}) collective-permute-start(bf16[2048,256]{1,0:T(8,128)(2,1)S(1)} %constant_dynamic-update-slice_fusion.6), channel_id=1, source_target_pairs={{0,192},{1,49},{2,194},{3,51},{4,196},{5,53},{6,198},{7,55},{8,200... | collective-permute-start | bytes 3145736 | tf_op jit(solution)/shard_map/ppermute | solution.py:31
  41.1 0.8 copy-start.17
  43.6 15.1 %collective-permute-start.16 = (bf16[1024,256]{1,0:T(8,128)(2,1)S(1)}, bf16[1024,256]{1,0:T(8,128)(2,1)S(1)}, u32[]{:S(2)}, u32[]{:S(2)}) collective-permute-start(bf16[1024,256]{1,0:T(8,128)(2,1)S(1)} %collective-permute-done.10.refs_3_), channel_id=1, source_target_pairs={{0,1},{1,0},{2,3},{3,2},{4,5},{5,4},{6,7},{7,6},{8,9},{9,8},{10,11... | collective-permute-start | bytes 1572872 | tf_op jit(solution)/shard_map/ppermute | solution.py:40
  46.3 13.2 %collective-permute-start.14 = (bf16[1024,256]{1,0:T(8,128)(2,1)S(1)}, bf16[1024,256]{1,0:T(8,128)(2,1)S(1)}, u32[]{:S(2)}, u32[]{:S(2)}) collective-permute-start(bf16[1024,256]{1,0:T(8,128)(2,1)S(1)} %collective-permute-done.10.refs_3_), channel_id=1, source_target_pairs={{0,2},{1,15},{2,4},{3,1},{4,6},{5,3},{6,8},{7,5},{8,10},{9,7},{10,... | collective-permute-start | bytes 1572872 | tf_op jit(solution)/shard_map/ppermute | solution.py:36
  48.8 0.9 copy-start.13
  49.7 9.8 %collective-permute-start.15 = (bf16[1024,256]{1,0:T(8,128)(2,1)S(1)}, bf16[1024,256]{1,0:T(8,128)(2,1)S(1)}, u32[]{:S(2)}, u32[]{:S(2)}) collective-permute-start(bf16[1024,256]{1,0:T(8,128)(2,1)S(1)} %collective-permute-done.9.refs_6_), channel_id=1, source_target_pairs={{0,1},{1,0},{2,3},{3,2},{4,5},{5,4},{6,7},{7,6},{8,9},{9,8},{10,11... | collective-permute-start | bytes 1572872 | tf_op jit(solution)/shard_map/ppermute | solution.py:40
  54.7 1.0 copy-start
  55.7 8.4 %collective-permute-start.13 = (bf16[1024,256]{1,0:T(8,128)(2,1)S(1)}, bf16[1024,256]{1,0:T(8,128)(2,1)}, u32[]{:S(2)}, u32[]{:S(2)}) collective-permute-start(bf16[1024,256]{1,0:T(8,128)(2,1)S(1)} %collective-permute-done.9.refs_6_), channel_id=1, source_target_pairs={{0,2},{1,15},{2,4},{3,1},{4,6},{5,3},{6,8},{7,5},{8,10},{9,7},{10,... | collective-permute-start | bytes 1572872 | tf_op jit(solution)/shard_map/ppermute | solution.py:36
  56.9 0.8 copy-start.15
  57.7 1.0 copy-start.3
  58.6 26.1 %collective-permute-start.23 = (bf16[2048,256]{1,0:T(8,128)(2,1)}, bf16[2048,256]{1,0:T(8,128)(2,1)}, u32[]{:S(2)}, u32[]{:S(2)}) collective-permute-start(bf16[2048,256]{1,0:T(8,128)(2,1)} %collective-permute-done.6), channel_id=1, source_target_pairs={{0,64},{1,17},{2,66},{3,19},{4,68},{5,21},{6,70},{7,23},{8,72},{9,... | collective-permute-start | bytes 3145736 | tf_op jit(solution)/shard_map/ppermute | solution.py:31
  58.6 0.8 copy-start.19
  59.5 0.8 copy-start.23
  64.1 8.4 %collective-permute-start.18 = (bf16[1024,256]{1,0:T(8,128)(2,1)S(1)}, bf16[1024,256]{1,0:T(8,128)(2,1)}, u32[]{:S(2)}, u32[]{:S(2)}) collective-permute-start(bf16[1024,256]{1,0:T(8,128)(2,1)S(1)} %collective-permute-done.14.refs_7_), channel_id=1, source_target_pairs={{0,2},{1,15},{2,4},{3,1},{4,6},{5,3},{6,8},{7,5},{8,10},{9,7},{10,... | collective-permute-start | bytes 1572872 | tf_op jit(solution)/shard_map/ppermute | solution.py:36
  66.2 18.5 %collective-permute-start.24 = (bf16[2048,256]{1,0:T(8,128)(2,1)S(1)}, bf16[2048,256]{1,0:T(8,128)(2,1)}, u32[]{:S(2)}, u32[]{:S(2)}) collective-permute-start(bf16[2048,256]{1,0:T(8,128)(2,1)S(1)} %collective-permute-done.7), channel_id=1, source_target_pairs={{0,192},{1,49},{2,194},{3,51},{4,196},{5,53},{6,198},{7,55},{8,200... | collective-permute-start | bytes 3145736 | tf_op jit(solution)/shard_map/ppermute | solution.py:31
  66.2 12.8 %collective-permute-start.17 = (bf16[1024,256]{1,0:T(8,128)(2,1)S(1)}, bf16[1024,256]{1,0:T(8,128)(2,1)S(1)}, u32[]{:S(2)}, u32[]{:S(2)}) collective-permute-start(bf16[1024,256]{1,0:T(8,128)(2,1)S(1)} %collective-permute-done.14.refs_7_), channel_id=1, source_target_pairs={{0,1},{1,0},{2,3},{3,2},{4,5},{5,4},{6,7},{7,6},{8,9},{9,8},{10,11... | collective-permute-start | bytes 1572872 | tf_op jit(solution)/shard_map/ppermute | solution.py:40
  68.5 0.8 copy-start.21
  69.3 10.5 %collective-permute-start.21 = (bf16[1024,256]{1,0:T(8,128)(2,1)}, bf16[1024,256]{1,0:T(8,128)(2,1)}, u32[]{:S(2)}, u32[]{:S(2)}) collective-permute-start(bf16[1024,256]{1,0:T(8,128)(2,1)} %collective-permute-done.13.refs_10_), channel_id=1, source_target_pairs={{0,2},{1,15},{2,4},{3,1},{4,6},{5,3},{6,8},{7,5},{8,10},{9,7},{10,... | collective-permute-start | bytes 1572872 | tf_op jit(solution)/shard_map/ppermute | solution.py:36
  72.6 12.1 %collective-permute-start.19 = (bf16[1024,256]{1,0:T(8,128)(2,1)}, bf16[1024,256]{1,0:T(8,128)(2,1)}, u32[]{:S(2)}, u32[]{:S(2)}) collective-permute-start(bf16[1024,256]{1,0:T(8,128)(2,1)} %collective-permute-done.13.refs_10_), channel_id=1, source_target_pairs={{0,1},{1,0},{2,3},{3,2},{4,5},{5,4},{6,7},{7,6},{8,9},{9,8},{10,11... | collective-permute-start | bytes 1572872 | tf_op jit(solution)/shard_map/ppermute | solution.py:40
  79.0 0.8 copy-start.25
  79.8 5.0 %collective-permute-start.20 = (bf16[1024,256]{1,0:T(8,128)(2,1)}, bf16[1024,256]{1,0:T(8,128)(2,1)}, u32[]{:S(2)}, u32[]{:S(2)}) collective-permute-start(bf16[1024,256]{1,0:T(8,128)(2,1)} %collective-permute-done.18.refs_11_), channel_id=1, source_target_pairs={{0,1},{1,0},{2,3},{3,2},{4,5},{5,4},{6,7},{7,6},{8,9},{9,8},{10,11... | collective-permute-start | bytes 1572872 | tf_op jit(solution)/shard_map/ppermute | solution.py:40
  79.8 6.7 %collective-permute-start.22 = (bf16[1024,256]{1,0:T(8,128)(2,1)}, bf16[1024,256]{1,0:T(8,128)(2,1)}, u32[]{:S(2)}, u32[]{:S(2)}) collective-permute-start(bf16[1024,256]{1,0:T(8,128)(2,1)} %collective-permute-done.21.refs_14_), channel_id=1, source_target_pairs={{0,1},{1,0},{2,3},{3,2},{4,5},{5,4},{6,7},{7,6},{8,9},{9,8},{10,11... | collective-permute-start | bytes 1572872 | tf_op jit(solution)/shard_map/ppermute | solution.py:40
  86.5 0.7 copy-start.28
  87.2 1.2 copy-start.1
  88.4 1.2 copy-start.4
  89.6 1.0 copy-start.7
  90.7 1.0 copy-start.10
  91.7 1.0 copy-start.12
  92.7 1.0 copy-start.14
  93.8 1.0 copy-start.16
  94.8 1.0 copy-start.18
  95.9 1.0 copy-start.20
  96.9 1.0 copy-start.22
  97.9 1.0 copy-start.24
  99.0 1.0 copy-start.26
  140.2 3.9 %collective-permute-start.25 = (bf16[8,32,256]{2,1,0:T(8,128)(2,1)S(1)}, bf16[8,32,256]{2,1,0:T(8,128)(2,1)S(1)}, u32[]{:S(2)}, u32[]{:S(2)}) collective-permute-start(bf16[8,32,256]{2,1,0:T(8,128)(2,1)S(1)} %all_to_all.21.mine), channel_id=1, source_target_pairs={{0,1},{1,0},{2,3},{3,2},{4,5},{5,4},{6,7},{7,6},{8,9},{9,8},{10,11... | collective-permute-start | bytes 393224 | tf_op jit(solution)/shard_map/ppermute | solution.py:40
  144.1 1.2 copy-start.2
  145.3 1.2 copy-start.5
  149.0 11.3 %copy-start.27 = (f32[32,256]{1,0:T(8,128)}, f32[32,256]{1,0:T(8,128)S(1)}, u32[]{:S(2)}) copy-start(f32[32,256]{1,0:T(8,128)S(1)} %get-tuple-element.43.refs_1_) | copy-start | bytes 98308

commit v5 on v3

--- a/solution.py
+++ b/solution.py
@@ -56,7 +56,7 @@
     return [part.reshape(2, len(weights), *weights[0].shape) for part in parts]
 
 
-def block_table():
+def index_table():
     agent, core = lax.axis_index("agent"), lax.axis_index("tensor") % 2
     y, x = agent // SIDE, agent % SIDE
     table = []
@@ -64,40 +64,44 @@
         for j in STEPS:
             dy, dx = jnp.where(core == 0, i, j), jnp.where(core == 0, j, i)
             table.append((y + dy + SIDE) % SIDE * SIDE + (x + dx + SIDE) % SIDE)
-    return jnp.stack(table).astype(jnp.int32)
-
-
-def attend_kernel(block_ids, feats, *refs):
+    return jnp.stack(table + [agent, core]).astype(jnp.int32)
+
+
+def attend_kernel(table, feats, *refs):
     w_refs = refs[:8]
-    valid, out, x_all, w_all, stat, x_sem, w_sem = refs[8:]
+    valid, out, x_all, w_all, acc, stat, x_sem, w_sem = refs[8:]
     rows = feats.shape[1] // 2
     depth = feats.shape[2]
-    x_copies = [
-        pltpu.make_async_copy(feats.at[block_ids[slot]], x_all.at[slot], x_sem.at[slot])
-        for slot in range(GROUP)
-    ]
-    w_copies = [
-        pltpu.make_async_copy(
-            w_refs[n].at[:, pl.ds(0, 3)], w_all.at[pl.ds(2 * n, 2)], w_sem.at[n])
-        for n in range(8)
-    ]
-    copies = [
-        x_copies[part * SIDE:(part + 1) * SIDE] + w_copies[2 * part:2 * part + 2]
-        for part in range(SIDE)
-    ]
+    parts = 8
+    step = GROUP // parts
+    copies = [[] for _ in range(parts)]
+    for slot in range(GROUP):
+        copies[slot // step].append(pltpu.make_async_copy(
+            feats.at[table[slot]], x_all.at[:, pl.ds(slot * depth, depth)], x_sem.at[slot]))
+    for part in range(2, parts):
+        for n in range(3):
+            copies[part].append(pltpu.make_async_copy(
+                w_refs[part].at[:, n], w_all.at[n, pl.ds(part * step, step)], w_sem.at[n, part]))
     for part in copies:
         for copy in part:
             copy.start()
     sums = [None] * 3
-    for part in range(SIDE):
+    for part in range(parts):
         for copy in copies[part]:
             copy.wait()
         for n, top in enumerate((rows, 0, 0)):
-            left = jnp.concatenate(
-                [x_all[part * SIDE + j, pl.ds(top, rows), :] for j in range(SIDE)], axis=1)
-            right = w_all[pl.ds(part * SIDE, SIDE), n].reshape(SIDE * depth, -1)
-            more = jnp.dot(left, right, preferred_element_type=F32)
-            sums[n] = more if sums[n] is None else sums[n] + more
+            left = x_all[pl.ds(top, rows), pl.ds(part * step * depth, step * depth)]
+            if part < 2:
+                right = w_refs[part][:, n]
+            else:
+                right = w_all[n, pl.ds(part * step, step)]
+            more = jnp.dot(left, right.reshape(step * depth, depth), preferred_element_type=F32)
+            if part == 0:
+                acc[n] = more
+            elif part < parts - 1:
+                acc[n] += more
+            else:
+                sums[n] = acc[n] + more
     query, keys, values = sums
     query = query.astype(BF16)
     keys = keys.astype(BF16)
@@ -129,37 +133,48 @@
 
 def combine_kernel(parts, out):
     chunk = out.shape[1]
-    for tile in range(chunk // 8):
-        for head in range(2):
+    stat = parts[:, pl.ds(2 * chunk, 8), :]
+    factor = jnp.exp(stat - jnp.max(stat, axis=0, keepdims=True))
+    lane = lax.broadcasted_iota(jnp.int32, (1, 8, HEAD_DIM), 2)
+    factor = jnp.where(lane % 2 == 0, factor, 0.0)
+    total = jnp.sum(pltpu.roll(factor, 1, 2) * stat, axis=0, keepdims=True)
+    factor = factor / jnp.where(lane % 2 == 0, pltpu.roll(total, HEAD_DIM - 1, 2), 1.0)
+    heads = []
+    for head in range(2):
+        tiles = []
+        for tile in range(chunk // 8):
             at = 4 * tile + 2 * head
-            rows = pl.ds(2 * chunk, 8)
-            tops = parts[:, rows, at:at + 1]
-            totals = parts[:, rows, at + 1:at + 2]
-            top = jnp.max(tops, axis=0, keepdims=True)
-            factor = jnp.exp(tops - top)
-            total = jnp.sum(totals * factor, axis=0)
-            summed = jnp.sum(parts[:, pl.ds(head * chunk + 8 * tile, 8), :] * factor, axis=0)
-            out_tile = (summed / total).astype(BF16)
-            for t in range(out.shape[0]):
-                out[t, pl.ds(8 * tile, 8), head * HEAD_DIM:(head + 1) * HEAD_DIM] = out_tile
-
-
-def project_kernel(block_ids, me, mine, theirs, *refs):
-    w_refs, (latents, upd, squares, w_all, w_sem) = refs[:8], refs[8:]
+            rows = pl.ds(head * chunk + 8 * tile, 8)
+            tiles.append(jnp.sum(parts[:, rows, :] * factor[:, :, at:at + 1], axis=0))
+        heads.append(jnp.concatenate(tiles, axis=0))
+    attended = jnp.concatenate(heads, axis=1).astype(BF16)
+    for t in range(out.shape[0]):
+        out[t] = attended
+
+
+def project_kernel(table, mine, theirs, *refs):
+    w_refs, (latents, upd, squares, w_all, rows, w_sem, sem) = refs[:8], refs[8:]
+    chunk, depth = upd.shape
+    agent, core = table[GROUP], table[GROUP + 1]
     copies = [
         pltpu.make_async_copy(w_refs[n].at[:, 3], w_all.at[pl.ds(2 * n, 2)], w_sem.at[n])
         for n in range(8)
     ]
     for copy in copies:
         copy.start()
-    chunk = upd.shape[0]
-    total = latents[pl.ds(pl.multiple_of(me[0] * chunk, chunk), chunk), :].astype(F32)
-    for copy in copies:
-        copy.wait()
+    copy = pltpu.make_async_copy(
+        latents.at[pl.ds(pl.multiple_of(agent * chunk, chunk), chunk)], rows, sem)
+    copy.start()
+    lefts = []
     for slot in range(GROUP):
-        block = block_ids[slot]
-        left = jnp.where(block % 2 == me[1], mine[block // 2], theirs[block // 2])
-        total += jnp.dot(left, w_all[slot], preferred_element_type=F32)
+        block = table[slot]
+        lefts.append(jnp.where(block % 2 == core, mine[block // 2], theirs[block // 2]))
+    for each in copies:
+        each.wait()
+    total = jnp.dot(jnp.concatenate(lefts, axis=1), w_all[...].reshape(GROUP * depth, depth),
+                    preferred_element_type=F32)
+    copy.wait()
+    total += rows[...].astype(F32)
     upd[...] = total
     square = jnp.sum(total * total, axis=1, keepdims=True)
     lane = lax.broadcasted_iota(jnp.int32, (8, HEAD_DIM), 1)
@@ -173,14 +188,13 @@
 def finish_kernel(width, squares, upd, gain, out):
     total = jnp.sum(squares[...], axis=0)
     chunk = upd.shape[0]
-    for tile in range(chunk // 8):
-        rows = pl.ds(8 * tile, 8)
-        mean_sq = total[:, tile:tile + 1] / width
-        u = upd[rows, :]
-        normed = gain[...] * u * lax.rsqrt(mean_sq + 1e-05)
-        for a in range(GROUP):
-            out[a, 0, rows, :] = u.astype(BF16)
-            out[a, 1, rows, :] = normed.astype(BF16)
+    mean_sq = jnp.concatenate([total[:, n:n + 1] for n in range(chunk // 8)], axis=0) / width
+    u = upd[...]
+    normed = (gain[...] * u * lax.rsqrt(mean_sq + 1e-05)).astype(BF16)
+    u = u.astype(BF16)
+    for a in range(GROUP):
+        out[a, 0] = u
+        out[a, 1] = normed
 
 
 def whole(count):
@@ -188,32 +202,31 @@
 
 
 def body(tokens, valid, latents, w_query, w_key, w_value, w_out, gain):
-    me = lax.axis_index("agent")
     rows, depth = tokens.shape
     chunk = latents.shape[0] // GROUP
     width = depth * lax.axis_size("tensor")
     both = jnp.concatenate([tokens, latents], axis=0)
     feats = lax.all_gather(both, "tensor", axis=0, tiled=False)
     weights = gather_weights(w_query, w_key, w_value, w_out)
-    block_ids = block_table()
-    place = jnp.stack([me, lax.axis_index("tensor") % 2]).astype(jnp.int32)
+    table = index_table()
     smem = pl.BlockSpec(memory_space=pltpu.SMEM)
     anywhere = pl.BlockSpec(memory_space=pl.ANY)
     partial = pl.pallas_call(
         attend_kernel,
         out_shape=jax.ShapeDtypeStruct((GROUP, 2 * chunk + 8, HEAD_DIM), F32),
-        in_specs=[smem] + [anywhere] * 9 + whole(1),
+        in_specs=[smem, anywhere] + whole(2) + [anywhere] * 6 + whole(1),
         out_specs=whole(1)[0],
         scratch_shapes=[
-            pltpu.VMEM((GROUP, 2 * rows, depth), BF16),
-            pltpu.VMEM((GROUP, 3, depth, depth), BF16),
+            pltpu.VMEM((2 * rows, GROUP * depth), BF16),
+            pltpu.VMEM((3, GROUP, depth, depth), BF16),
+            pltpu.VMEM((3, rows, depth), F32),
             pltpu.VMEM((GROUP, chunk // 8, 8, HEAD_DIM), F32),
             pltpu.SemaphoreType.DMA((GROUP,)),
-            pltpu.SemaphoreType.DMA((8,)),
+            pltpu.SemaphoreType.DMA((3, 8)),
         ],
-        compiler_params=pltpu.CompilerParams(vmem_limit_bytes=60 * 2**20),
+        compiler_params=pltpu.CompilerParams(vmem_limit_bytes=40 * 2**20),
         name="attend",
-    )(block_ids, feats, *weights, valid.reshape(1, rows))
+    )(table, feats, *weights, valid.reshape(1, rows))
     partial = lax.all_to_all(partial, "agent", 0, 0)
     attended = pl.pallas_call(
         combine_kernel,
@@ -229,15 +242,17 @@
         project_kernel,
         out_shape=(jax.ShapeDtypeStruct((chunk, depth), F32),
                    jax.ShapeDtypeStruct((GROUP, 8, HEAD_DIM), F32)),
-        in_specs=[smem, smem] + whole(2) + [anywhere] * 8 + whole(1),
+        in_specs=[smem] + whole(2) + [anywhere] * 9,
         out_specs=tuple(whole(2)),
         scratch_shapes=[
             pltpu.VMEM((GROUP, depth, depth), BF16),
+            pltpu.VMEM((chunk, depth), BF16),
             pltpu.SemaphoreType.DMA((8,)),
+            pltpu.SemaphoreType.DMA,
         ],
         compiler_params=pltpu.CompilerParams(vmem_limit_bytes=60 * 2**20),
         name="project",
-    )(block_ids, place, attended, theirs, *weights, latents)
+    )(table, attended, theirs, *weights, latents)
     squares = lax.all_to_all(squares, "tensor", 0, 0)
     out = pl.pallas_call(
         lambda *refs: finish_kernel(width, *refs),

time: 159 us -> 156 us (0.981)
  Pallas kernels: 19.1 us -> 16.5 us
    pallas_call x1, Pallas kernels: 11.1 us -> 8.6 us  [body(): pl.pallas_call(attend_kernel, out_shape=jax.ShapeDtypeStruct((GROUP, 2 *...]
  transfers between devices with their start and end apart: 12 -> 12, of which waited for: 9 -> 9; matrix products, arithmetic and copies ran while one was open for 2% -> 1% of each run, Pallas kernels for 0% -> 0%
where the time goes in v5:
time: 156 us
  blocking collectives  56.8 us (36%)
  waiting for transfers between devices  45.7 us (29%)
  starting transfers between devices  16.9 us (11%)
  Pallas kernels  16.5 us (11%)
  between operations  14.2 us (9%)
  local copies, waits for them, and re-layouts  3.54 us (2%)
  other arithmetic  2.11 us (1%)
    ppermute x6, waiting for transfers between devices, second(): lax.ppermute(array, ('agent', 'tensor'), pairs(lambda y, x, core: (y + by...  30.8 us
    all_to_all x1, blocking collectives, body(): partial = lax.all_to_all(partial, 'agent', 0, 0)  18 us
    all_to_all x1, blocking collectives, body(): out = lax.all_to_all(out, 'agent', 0, 0)  14.8 us
    all_to_all x1, blocking collectives, body(): squares = lax.all_to_all(squares, 'tensor', 0, 0)  12.2 us
    all_to_all x1, blocking collectives, body(): lax.all_to_all(attended, 'tensor', 0, 0, axis_index_groups=same_core)  11.9 us
    ppermute x4, waiting for transfers between devices, first(): lax.ppermute(array, ('agent', 'tensor'), pairs(lambda y, x, core: (y, x +...  10.3 us
    pallas_call x1, Pallas kernels, body(): pl.pallas_call(attend_kernel, out_shape=jax.ShapeDtypeStruct((GROUP, 2 *...  8.6 us
    ppermute x6, starting transfers between devices, second(): lax.ppermute(array, ('agent', 'tensor'), pairs(lambda y, x, core: (y + by...  6.89 us
  transfers between devices with their start and end apart: 12, of which 9 were waited for; matrix products, arithmetic and copies ran while one was open for 1% of the time, Pallas kernels for 0%

profile of v5, /device:TPU:1, one launch (start us, length us, event | category | flops | bytes accessed | tf_op | source)
XLA Modules:
  0.0 155.8 jit_solution(8098851492472161847)
XLA Ops:
  7.2 0.0 copy-start.8
  7.2 0.0 copy-start.9
  7.2 0.0 copy-start.6
  7.2 0.0 copy-start.7
  7.2 0.0 all-gather.3.cloned.1.call-start
  7.3 2.0 %pad_maximum_fusion.1 = bf16[1024,256]{1,0:T(8,128)(2,1)} fusion(bf16[512,256]{1,0:T(8,128)(2,1)} %refs_8_.1, bf16[512,256]{1,0:T(8,128)(2,1)} %param.8), kind=kLoop, calls=%fused_computation.1 | loop fusion | flops 1048576 | bytes 1048576 | tf_op jit(solution)/shard_map/concatenate | solution.py:208
  9.3 0.0 all-gather.3.cloned.1.call-update
  9.3 0.9 constant_dynamic-update-slice_fusion.3
  10.2 0.9 constant_dynamic-update-slice_fusion.2
  11.1 0.0 copy-done.6
  11.2 0.0 copy-done.7
  11.2 2.2 %collective-permute-start = (bf16[1024,256]{1,0:T(8,128)(2,1)S(1)}, bf16[1024,256]{1,0:T(8,128)(2,1)S(1)}, u32[]{:S(2)}, u32[]{:S(2)}) collective-permute-start(bf16[1024,256]{1,0:T(8,128)(2,1)S(1)} %get-tuple-element.12), channel_id=1, source_target_pairs={{0,16},{1,65},{2,18},{3,67},{4,20},{5,69},{6,22},{7,71},{8,24},{9,... | collective-permute-start | bytes 1572872 | tf_op jit(solution)/shard_map/ppermute | solution.py:26
  13.4 1.5 collective-permute-start.1
  15.0 1.6 %collective-permute-start.3 = (bf16[512,256]{1,0:T(8,128)(2,1)S(1)}, bf16[512,256]{1,0:T(8,128)(2,1)S(1)}, u32[]{:S(2)}, u32[]{:S(2)}) collective-permute-start(bf16[512,256]{1,0:T(8,128)(2,1)S(1)} %pad_maximum_fusion.3), channel_id=1, source_target_pairs={{0,32},{1,129},{2,34},{3,131},{4,36},{5,133},{6,38},{7,135},{8,40}... | collective-permute-start | bytes 786440 | tf_op jit(solution)/shard_map/ppermute | solution.py:26
  16.6 0.0 copy-done.8
  16.6 0.0 copy-done.9
  16.6 0.0 copy-start.4
  16.7 1.5 collective-permute-start.2
  18.2 3.6 %collective-permute-done = bf16[1024,256]{1,0:T(8,128)(2,1)S(1)} collective-permute-done((bf16[1024,256]{1,0:T(8,128)(2,1)S(1)}, bf16[1024,256]{1,0:T(8,128)(2,1)S(1)}, u32[]{:S(2)}, u32[]{:S(2)}) %collective-permute-start) | collective-permute-done | bytes 524320 | tf_op jit(solution)/shard_map/ppermute | solution.py:26
  21.8 0.0 copy-start.1
  21.8 3.9 %collective-permute-done.3 = bf16[512,256]{1,0:T(8,128)(2,1)S(1)} collective-permute-done((bf16[512,256]{1,0:T(8,128)(2,1)S(1)}, bf16[512,256]{1,0:T(8,128)(2,1)S(1)}, u32[]{:S(2)}, u32[]{:S(2)}) %collective-permute-start.3) | collective-permute-done | bytes 262176 | tf_op jit(solution)/shard_map/ppermute | solution.py:26
  25.7 2.8 %collective-permute-done.2 = bf16[512,256]{1,0:T(8,128)(2,1)S(1)} collective-permute-done((bf16[512,256]{1,0:T(8,128)(2,1)S(1)}, bf16[512,256]{1,0:T(8,128)(2,1)S(1)}, u32[]{:S(2)}, u32[]{:S(2)}) %collective-permute-start.2) | collective-permute-done | bytes 262176 | tf_op jit(solution)/shard_map/ppermute | solution.py:26
  28.5 0.0 collective-permute-done.1
  28.5 0.1 pad_maximum_fusion
  28.6 0.0 copy-start
  28.6 1.0 collective-permute-start.4
  29.6 1.8 %collective-permute-start.7 = (bf16[2048,256]{1,0:T(8,128)(2,1)S(1)}, bf16[2048,256]{1,0:T(8,128)(2,1)}, u32[]{:S(2)}, u32[]{:S(2)}) collective-permute-start(bf16[2048,256]{1,0:T(8,128)(2,1)S(1)} %pad_maximum_fusion), channel_id=1, source_target_pairs={{0,192},{1,49},{2,194},{3,51},{4,196},{5,53},{6,198},{7,55},{8,200... | collective-permute-start | bytes 3145736 | tf_op jit(solution)/shard_map/ppermute | solution.py:31
  31.4 1.3 collective-permute-start.6
  32.6 0.2 collective-permute-start.5
  32.8 11.1 %collective-permute-done.4 = bf16[2048,256]{1,0:T(8,128)(2,1)S(1)} collective-permute-done((bf16[2048,256]{1,0:T(8,128)(2,1)S(1)}, bf16[2048,256]{1,0:T(8,128)(2,1)S(1)}, u32[]{:S(2)}, u32[]{:S(2)}) %collective-permute-start.4) | collective-permute-done | bytes 1048608 | tf_op jit(solution)/shard_map/ppermute | solution.py:31
  43.9 0.0 copy-start.2
  43.9 0.0 collective-permute-start.8
  43.9 0.0 collective-permute-done.7
  44.0 2.7 %collective-permute-start.9 = (bf16[2048,256]{1,0:T(8,128)(2,1)}, bf16[2048,256]{1,0:T(8,128)(2,1)}, u32[]{:S(2)}, u32[]{:S(2)}) collective-permute-start(bf16[2048,256]{1,0:T(8,128)(2,1)} %collective-permute-done.7), channel_id=1, source_target_pairs={{0,192},{1,49},{2,194},{3,51},{4,196},{5,53},{6,198},{7,55},{8,200... | collective-permute-start | bytes 3145736 | tf_op jit(solution)/shard_map/ppermute | solution.py:31
  46.6 0.1 stack.75.table
  46.7 0.0 copy-start.3
  46.7 8.2 %collective-permute-done.6 = bf16[2048,256]{1,0:T(8,128)(2,1)} collective-permute-done((bf16[2048,256]{1,0:T(8,128)(2,1)S(1)}, bf16[2048,256]{1,0:T(8,128)(2,1)}, u32[]{:S(2)}, u32[]{:S(2)}) %collective-permute-start.6) | collective-permute-done | bytes 1048608 | tf_op jit(solution)/shard_map/ppermute | solution.py:31
  54.9 0.3 collective-permute-done.5
  55.2 11.2 %collective-permute-done.8 = bf16[2048,256]{1,0:T(8,128)(2,1)} collective-permute-done((bf16[2048,256]{1,0:T(8,128)(2,1)S(1)}, bf16[2048,256]{1,0:T(8,128)(2,1)}, u32[]{:S(2)}, u32[]{:S(2)}) %collective-permute-start.8) | collective-permute-done | bytes 1048608 | tf_op jit(solution)/shard_map/ppermute | solution.py:31
  66.4 0.0 collective-permute-done.9
  66.4 3.6 %all-gather.3.cloned.1.call-done = bf16[16384,256]{1,0:T(8,128)(2,1)} async-done(((bf16[1024,256]{1,0:T(8,128)(2,1)}), bf16[16384,256]{1,0:T(8,128)(2,1)}) %all-gather.3.cloned.1.call-update) | async-done | bytes 8388624 | tf_op jit(solution)/shard_map/all_gather | solution.py:209
  70.0 0.0 copy-done.4
  70.0 8.6 %attend.1 = f32[16,72,128]{2,1,0:T(8,128)S(1)} custom-call(s32[18]{0:T(128)S(1)} %stack.75.table, bf16[16,1024,256]{2,1,0:T(8,128)(2,1)} %bitcast.38, bf16[2,4,256,256]{3,2,1,0:T(8,128)(2,1)S(1)} %bitcast.33, bf16[2,4,256,256]{3,2,1,0:T(8,128)(2,1)S(1)} %bitcast.31, bf16[2,4,256,256]{3,2,1,0:T(8,128)(2,1)S(1)} %bitcast.35, ...), custom_call_target="tpu_custom_call" | custom-call | tf_op jit(solution)/shard_map/attend/pallas_call | solution.py:214
  78.6 0.0 copy-done.1
  78.7 0.0 copy-done
  78.7 0.0 copy-done.2
  78.7 0.0 copy-done.3
  78.7 18.0 %all_to_all.20.parts = f32[16,72,128]{2,1,0:T(8,128)} all-to-all(f32[16,72,128]{2,1,0:T(8,128)S(1)} %attend.1), channel_id=1, replica_groups=mesh['agent'=16,'tensor'=16] {'agent'}, dimensions={0} | all-to-all | bytes 1179648 | tf_op jit(solution)/shard_map/all_to_all | solution.py:230
  96.7 2.1 %combine.1 = bf16[8,32,256]{2,1,0:T(8,128)(2,1)} custom-call(f32[16,72,128]{2,1,0:T(8,128)} %all_to_all.20.parts), custom_call_target="tpu_custom_call" | custom-call | tf_op jit(solution)/shard_map/combine/pallas_call | solution.py:231
  98.8 11.9 %all_to_all.21.mine = bf16[8,32,256]{2,1,0:T(8,128)(2,1)S(1)} all-to-all(bf16[8,32,256]{2,1,0:T(8,128)(2,1)} %combine.1), channel_id=1, replica_groups={{0,2,4,6,8,10,12,14},{1,3,5,7,9,11,13,15},{16,18,20,22,24,26,28,30},{17..., dimensions={0} | all-to-all | bytes 262144 | tf_op jit(solution)/shard_map/all_to_all | solution.py:239
  110.7 0.0 copy-start.5
  110.7 3.1 %collective-permute-start.10 = (bf16[8,32,256]{2,1,0:T(8,128)(2,1)S(1)}, bf16[8,32,256]{2,1,0:T(8,128)(2,1)S(1)}, u32[]{:S(2)}, u32[]{:S(2)}) collective-permute-start(bf16[8,32,256]{2,1,0:T(8,128)(2,1)S(1)} %all_to_all.21.mine), channel_id=1, source_target_pairs={{0,1},{1,0},{2,3},{3,2},{4,5},{5,4},{6,7},{7,6},{8,9},{9,8},{10,11... | collective-permute-start | bytes 393224 | tf_op jit(solution)/shard_map/ppermute | solution.py:36
  113.8 1.0 collective-permute-done.10.theirs
  114.8 0.0 copy-done.5
  114.8 0.0 copy-start.10
  114.8 0.7 copy-done.10
  115.4 3.9 %project.1 = (f32[32,256]{1,0:T(8,128)}, f32[16,8,128]{2,1,0:T(8,128)}) custom-call(s32[18]{0:T(128)} %copy-done.3, bf16[8,32,256]{2,1,0:T(8,128)(2,1)} %copy-done.5, bf16[8,32,256]{2,1,0:T(8,128)(2,1)} %copy-done.10, bf16[2,4,256,256]{3,2,1,0:T(8,128)(2,1)} %bitcast.34, bf16[2,4,256,256]{3,2,1,0:T(8,128)(2,1)} %bitcast.32, ...), custom_call_target="tpu_custom_call" | custom-call | tf_op jit(solution)/shard_map/project/pallas_call | solution.py:241
  119.3 12.2 %all_to_all.22.refs_0_ = f32[16,8,128]{2,1,0:T(8,128)} all-to-all(f32[16,8,128]{2,1,0:T(8,128)} %get-tuple-element.8), channel_id=1, replica_groups=mesh['agent'=16,'tensor'=16] {'tensor'}, dimensions={0} | all-to-all | bytes 131072 | tf_op jit(solution)/shard_map/all_to_all | solution.py:256
  131.5 1.9 %finish.1 = bf16[16,2,32,256]{3,2,1,0:T(8,128)(2,1)} custom-call(f32[16,8,128]{2,1,0:T(8,128)} %all_to_all.22.refs_0_, f32[32,256]{1,0:T(8,128)} %get-tuple-element.9.refs_1_, f32[1,256]{1,0:T(1,128)} %bitcast.41), custom_call_target="tpu_custom_call" | custom-call | tf_op jit(solution)/shard_map/finish/pallas_call | solution.py:257
  133.4 14.8 %all_to_all.23 = bf16[16,2,32,256]{3,2,1,0:T(8,128)(2,1)S(1)} all-to-all(bf16[16,2,32,256]{3,2,1,0:T(8,128)(2,1)} %finish.1), channel_id=1, replica_groups=mesh['agent'=16,'tensor'=16] {'agent'}, dimensions={0} | all-to-all | bytes 1048576 | tf_op jit(solution)/shard_map/all_to_all | solution.py:264
  148.1 0.8 fusion
  (5 shorter events, 0.1 us)
Async XLA Ops:
  7.2 9.4 %copy-start.8 = (bf16[256,256]{1,0:T(8,128)(2,1)S(1)}, bf16[256,256]{1,0:T(8,128)(2,1)}, u32[]{:S(2)}) copy-start(bf16[256,256]{1,0:T(8,128)(2,1)} %param.11) | copy-start | bytes 393220
  7.2 9.4 %copy-start.9 = (bf16[256,256]{1,0:T(8,128)(2,1)S(1)}, bf16[256,256]{1,0:T(8,128)(2,1)}, u32[]{:S(2)}) copy-start(bf16[256,256]{1,0:T(8,128)(2,1)} %param.12) | copy-start | bytes 393220
  7.2 4.0 %copy-start.6 = (bf16[256,256]{1,0:T(8,128)(2,1)S(1)}, bf16[256,256]{1,0:T(8,128)(2,1)}, u32[]{:S(2)}) copy-start(bf16[256,256]{1,0:T(8,128)(2,1)} %param.13) | copy-start | bytes 393220
  7.2 4.0 %copy-start.7 = (bf16[256,256]{1,0:T(8,128)(2,1)S(1)}, bf16[256,256]{1,0:T(8,128)(2,1)}, u32[]{:S(2)}) copy-start(bf16[256,256]{1,0:T(8,128)(2,1)} %param.14) | copy-start | bytes 393220
  7.2 62.8 %all-gather.3.cloned.1.call-start = ((), (), s32[]{:S(2)}) async-start(), calls=%async_computation.4 | async-start | bytes 8912896 | tf_op jit(solution)/shard_map/all_gather | solution.py:209
  11.2 10.5 %collective-permute-start = (bf16[1024,256]{1,0:T(8,128)(2,1)S(1)}, bf16[1024,256]{1,0:T(8,128)(2,1)S(1)}, u32[]{:S(2)}, u32[]{:S(2)}) collective-permute-start(bf16[1024,256]{1,0:T(8,128)(2,1)S(1)} %get-tuple-element.12), channel_id=1, source_target_pairs={{0,16},{1,65},{2,18},{3,67},{4,20},{5,69},{6,22},{7,71},{8,24},{9,... | collective-permute-start | bytes 1572872 | tf_op jit(solution)/shard_map/ppermute | solution.py:26
  13.4 15.1 %collective-permute-start.1 = (bf16[1024,256]{1,0:T(8,128)(2,1)S(1)}, bf16[1024,256]{1,0:T(8,128)(2,1)S(1)}, u32[]{:S(2)}, u32[]{:S(2)}) collective-permute-start(bf16[1024,256]{1,0:T(8,128)(2,1)S(1)} %get-tuple-element.12), channel_id=1, source_target_pairs={{0,48},{1,193},{2,50},{3,195},{4,52},{5,197},{6,54},{7,199},{8,56}... | collective-permute-start | bytes 1572872 | tf_op jit(solution)/shard_map/ppermute | solution.py:26
  15.0 10.7 %collective-permute-start.3 = (bf16[512,256]{1,0:T(8,128)(2,1)S(1)}, bf16[512,256]{1,0:T(8,128)(2,1)S(1)}, u32[]{:S(2)}, u32[]{:S(2)}) collective-permute-start(bf16[512,256]{1,0:T(8,128)(2,1)S(1)} %pad_maximum_fusion.3), channel_id=1, source_target_pairs={{0,32},{1,129},{2,34},{3,131},{4,36},{5,133},{6,38},{7,135},{8,40}... | collective-permute-start | bytes 786440 | tf_op jit(solution)/shard_map/ppermute | solution.py:26
  16.6 53.4 %copy-start.4 = (s32[512]{0:T(512)S(1)}, s32[512]{0:T(512)}, u32[]{:S(2)}) copy-start(s32[512]{0:T(512)} %param.9) | copy-start | bytes 6148
  16.7 11.9 %collective-permute-start.2 = (bf16[512,256]{1,0:T(8,128)(2,1)S(1)}, bf16[512,256]{1,0:T(8,128)(2,1)S(1)}, u32[]{:S(2)}, u32[]{:S(2)}) collective-permute-start(bf16[512,256]{1,0:T(8,128)(2,1)S(1)} %pad_maximum_fusion.2), channel_id=1, source_target_pairs={{0,32},{1,129},{2,34},{3,131},{4,36},{5,133},{6,38},{7,135},{8,40}... | collective-permute-start | bytes 786440 | tf_op jit(solution)/shard_map/ppermute | solution.py:26
  21.8 56.9 %copy-start.1 = (bf16[2048,256]{1,0:T(8,128)(2,1)}, bf16[2048,256]{1,0:T(8,128)(2,1)S(1)}, u32[]{:S(2)}) copy-start(bf16[2048,256]{1,0:T(8,128)(2,1)S(1)} %constant_dynamic-update-slice_fusion.4) | copy-start | bytes 3145732
  28.6 50.1 %copy-start = (bf16[2048,256]{1,0:T(8,128)(2,1)}, bf16[2048,256]{1,0:T(8,128)(2,1)S(1)}, u32[]{:S(2)}) copy-start(bf16[2048,256]{1,0:T(8,128)(2,1)S(1)} %pad_maximum_fusion) | copy-start | bytes 3145732
  28.6 15.3 %collective-permute-start.4 = (bf16[2048,256]{1,0:T(8,128)(2,1)S(1)}, bf16[2048,256]{1,0:T(8,128)(2,1)S(1)}, u32[]{:S(2)}, u32[]{:S(2)}) collective-permute-start(bf16[2048,256]{1,0:T(8,128)(2,1)S(1)} %constant_dynamic-update-slice_fusion.4), channel_id=1, source_target_pairs={{0,64},{1,17},{2,66},{3,19},{4,68},{5,21},{6,70},{7,23},{8,72},{9,... | collective-permute-start | bytes 3145736 | tf_op jit(solution)/shard_map/ppermute | solution.py:31
  29.6 14.4 %collective-permute-start.7 = (bf16[2048,256]{1,0:T(8,128)(2,1)S(1)}, bf16[2048,256]{1,0:T(8,128)(2,1)}, u32[]{:S(2)}, u32[]{:S(2)}) collective-permute-start(bf16[2048,256]{1,0:T(8,128)(2,1)S(1)} %pad_maximum_fusion), channel_id=1, source_target_pairs={{0,192},{1,49},{2,194},{3,51},{4,196},{5,53},{6,198},{7,55},{8,200... | collective-permute-start | bytes 3145736 | tf_op jit(solution)/shard_map/ppermute | solution.py:31
  31.4 23.5 %collective-permute-start.6 = (bf16[2048,256]{1,0:T(8,128)(2,1)S(1)}, bf16[2048,256]{1,0:T(8,128)(2,1)}, u32[]{:S(2)}, u32[]{:S(2)}) collective-permute-start(bf16[2048,256]{1,0:T(8,128)(2,1)S(1)} %constant_dynamic-update-slice_fusion.4), channel_id=1, source_target_pairs={{0,192},{1,49},{2,194},{3,51},{4,196},{5,53},{6,198},{7,55},{8,200... | collective-permute-start | bytes 3145736 | tf_op jit(solution)/shard_map/ppermute | solution.py:31
  32.6 22.5 %collective-permute-start.5 = (bf16[2048,256]{1,0:T(8,128)(2,1)S(1)}, bf16[2048,256]{1,0:T(8,128)(2,1)}, u32[]{:S(2)}, u32[]{:S(2)}) collective-permute-start(bf16[2048,256]{1,0:T(8,128)(2,1)S(1)} %pad_maximum_fusion), channel_id=1, source_target_pairs={{0,64},{1,17},{2,66},{3,19},{4,68},{5,21},{6,70},{7,23},{8,72},{9,... | collective-permute-start | bytes 3145736 | tf_op jit(solution)/shard_map/ppermute | solution.py:31
  43.9 34.7 %copy-start.2 = (bf16[2048,256]{1,0:T(8,128)(2,1)}, bf16[2048,256]{1,0:T(8,128)(2,1)S(1)}, u32[]{:S(2)}) copy-start(bf16[2048,256]{1,0:T(8,128)(2,1)S(1)} %collective-permute-done.4) | copy-start | bytes 3145732
  43.9 22.5 %collective-permute-start.8 = (bf16[2048,256]{1,0:T(8,128)(2,1)S(1)}, bf16[2048,256]{1,0:T(8,128)(2,1)}, u32[]{:S(2)}, u32[]{:S(2)}) collective-permute-start(bf16[2048,256]{1,0:T(8,128)(2,1)S(1)} %collective-permute-done.4), channel_id=1, source_target_pairs={{0,64},{1,17},{2,66},{3,19},{4,68},{5,21},{6,70},{7,23},{8,72},{9,... | collective-permute-start | bytes 3145736 | tf_op jit(solution)/shard_map/ppermute | solution.py:31
  44.0 22.5 %collective-permute-start.9 = (bf16[2048,256]{1,0:T(8,128)(2,1)}, bf16[2048,256]{1,0:T(8,128)(2,1)}, u32[]{:S(2)}, u32[]{:S(2)}) collective-permute-start(bf16[2048,256]{1,0:T(8,128)(2,1)} %collective-permute-done.7), channel_id=1, source_target_pairs={{0,192},{1,49},{2,194},{3,51},{4,196},{5,53},{6,198},{7,55},{8,200... | collective-permute-start | bytes 3145736 | tf_op jit(solution)/shard_map/ppermute | solution.py:31
  46.7 32.0 %copy-start.3 = (s32[18]{0:T(128)}, s32[18]{0:T(128)S(1)}, u32[]{:S(2)}) copy-start(s32[18]{0:T(128)S(1)} %stack.75.table) | copy-start | bytes 220
  110.7 4.1 %copy-start.5 = (bf16[8,32,256]{2,1,0:T(8,128)(2,1)}, bf16[8,32,256]{2,1,0:T(8,128)(2,1)S(1)}, u32[]{:S(2)}) copy-start(bf16[8,32,256]{2,1,0:T(8,128)(2,1)S(1)} %all_to_all.21.mine) | copy-start | bytes 393220
  110.7 4.1 %collective-permute-start.10 = (bf16[8,32,256]{2,1,0:T(8,128)(2,1)S(1)}, bf16[8,32,256]{2,1,0:T(8,128)(2,1)S(1)}, u32[]{:S(2)}, u32[]{:S(2)}) collective-permute-start(bf16[8,32,256]{2,1,0:T(8,128)(2,1)S(1)} %all_to_all.21.mine), channel_id=1, source_target_pairs={{0,1},{1,0},{2,3},{3,2},{4,5},{5,4},{6,7},{7,6},{8,9},{9,8},{10,11... | collective-permute-start | bytes 393224 | tf_op jit(solution)/shard_map/ppermute | solution.py:36
  114.8 0.7 copy-start.10
Sparse Core Ops, SparseCore 0:
  9.9 60.1 all-gather.2

commit v6 on v5

--- a/solution.py
+++ b/solution.py
@@ -210,11 +210,11 @@
     weights = gather_weights(w_query, w_key, w_value, w_out)
     table = index_table()
     smem = pl.BlockSpec(memory_space=pltpu.SMEM)
-    anywhere = pl.BlockSpec(memory_space=pl.ANY)
+    hbm = pl.BlockSpec(memory_space=pltpu.HBM)
     partial = pl.pallas_call(
         attend_kernel,
         out_shape=jax.ShapeDtypeStruct((GROUP, 2 * chunk + 8, HEAD_DIM), F32),
-        in_specs=[smem, anywhere] + whole(2) + [anywhere] * 6 + whole(1),
+        in_specs=[smem, hbm] + whole(2) + [hbm] * 6 + whole(1),
         out_specs=whole(1)[0],
         scratch_shapes=[
             pltpu.VMEM((2 * rows, GROUP * depth), BF16),
@@ -233,6 +233,7 @@
         out_shape=jax.ShapeDtypeStruct((GROUP // 2, chunk, depth), BF16),
         in_specs=whole(1),
         out_specs=whole(1)[0],
+        compiler_params=pltpu.CompilerParams(vmem_limit_bytes=4 * 2**20),
         name="combine",
     )(partial)
     same_core = [list(range(core, GROUP, 2)) for core in range(2)]
@@ -242,7 +243,7 @@
         project_kernel,
         out_shape=(jax.ShapeDtypeStruct((chunk, depth), F32),
                    jax.ShapeDtypeStruct((GROUP, 8, HEAD_DIM), F32)),
-        in_specs=[smem] + whole(2) + [anywhere] * 9,
+        in_specs=[smem] + whole(2) + [hbm] * 9,
         out_specs=tuple(whole(2)),
         scratch_shapes=[
             pltpu.VMEM((GROUP, depth, depth), BF16),
@@ -250,7 +251,7 @@
             pltpu.SemaphoreType.DMA((8,)),
             pltpu.SemaphoreType.DMA,
         ],
-        compiler_params=pltpu.CompilerParams(vmem_limit_bytes=60 * 2**20),
+        compiler_params=pltpu.CompilerParams(vmem_limit_bytes=8 * 2**20),
         name="project",
     )(table, attended, theirs, *weights, latents)
     squares = lax.all_to_all(squares, "tensor", 0, 0)
@@ -259,6 +260,7 @@
         out_shape=jax.ShapeDtypeStruct((GROUP, 2, chunk, depth), BF16),
         in_specs=whole(3),
         out_specs=whole(1)[0],
+        compiler_params=pltpu.CompilerParams(vmem_limit_bytes=4 * 2**20),
         name="finish",
     )(squares, upd, gain.reshape(1, depth))
     out = lax.all_to_all(out, "agent", 0, 0)

time: 156 us -> 148 us (0.949)
  Pallas kernels: 16.5 us -> 11.8 us
  blocking collectives: 56.8 us -> 54.1 us
    pallas_call x1, Pallas kernels: 2.11 us -> 0.39 us  [body(): pl.pallas_call(combine_kernel, out_shape=jax.ShapeDtypeStruct((GROUP // 2...]
    pallas_call x1, Pallas kernels: 1.87 us -> 0.18 us  [body(): pl.pallas_call(lambda *refs: finish_kernel(width, *refs), out_shape=jax.S...]
    all_to_all x1, blocking collectives: 12.2 us -> 10.6 us  [body(): squares = lax.all_to_all(squares, 'tensor', 0, 0)]
where the time goes in v6:
time: 148 us
  blocking collectives  54.1 us (37%)
  waiting for transfers between devices  45.8 us (31%)
  starting transfers between devices  16.9 us (11%)
  between operations  14.2 us (10%)
  Pallas kernels  11.8 us (8%)
  local copies, waits for them, and re-layouts  2.88 us (2%)
  other arithmetic  2.08 us (1%)
    ppermute x6, waiting for transfers between devices, second(): lax.ppermute(array, ('agent', 'tensor'), pairs(lambda y, x, core: (y + by...  30.8 us
    all_to_all x1, blocking collectives, body(): partial = lax.all_to_all(partial, 'agent', 0, 0)  18 us
    all_to_all x1, blocking collectives, body(): out = lax.all_to_all(out, 'agent', 0, 0)  13.8 us
    all_to_all x1, blocking collectives, body(): lax.all_to_all(attended, 'tensor', 0, 0, axis_index_groups=same_core)  11.7 us
    all_to_all x1, blocking collectives, body(): squares = lax.all_to_all(squares, 'tensor', 0, 0)  10.6 us
    ppermute x4, waiting for transfers between devices, first(): lax.ppermute(array, ('agent', 'tensor'), pairs(lambda y, x, core: (y, x +...  10.3 us
    pallas_call x1, Pallas kernels, body(): pl.pallas_call(attend_kernel, out_shape=jax.ShapeDtypeStruct((GROUP, 2 *...  8.6 us
    ppermute x6, starting transfers between devices, second(): lax.ppermute(array, ('agent', 'tensor'), pairs(lambda y, x, core: (y + by...  6.9 us
  transfers between devices with their start and end apart: 12, of which 9 were waited for; matrix products, arithmetic and copies ran while one was open for 1% of the time, Pallas kernels for 0%

profile of v6, /device:TPU:1, one launch (start us, length us, event | category | flops | bytes accessed | tf_op | source)
XLA Modules:
  0.0 147.7 jit_solution(3186004511396555278)
XLA Ops:
  7.2 0.0 copy-start.5
  7.2 0.0 copy-start.6
  7.2 0.0 copy-start.3
  7.2 0.0 copy-start.4
  7.2 0.0 all-gather.3.cloned.1.call-start
  7.3 2.0 %pad_maximum_fusion.1 = bf16[1024,256]{1,0:T(8,128)(2,1)} fusion(bf16[512,256]{1,0:T(8,128)(2,1)} %refs_8_.1, bf16[512,256]{1,0:T(8,128)(2,1)} %param.8), kind=kLoop, calls=%fused_computation.1 | loop fusion | flops 1048576 | bytes 1048576 | tf_op jit(solution)/shard_map/concatenate | solution.py:208
  9.2 0.0 all-gather.3.cloned.1.call-update
  9.3 0.9 constant_dynamic-update-slice_fusion.3
  10.2 0.9 constant_dynamic-update-slice_fusion.2
  11.1 0.0 copy-done.3
  11.1 0.0 copy-done.4
  11.2 2.2 %collective-permute-start = (bf16[1024,256]{1,0:T(8,128)(2,1)S(1)}, bf16[1024,256]{1,0:T(8,128)(2,1)S(1)}, u32[]{:S(2)}, u32[]{:S(2)}) collective-permute-start(bf16[1024,256]{1,0:T(8,128)(2,1)S(1)} %get-tuple-element.12), channel_id=1, source_target_pairs={{0,16},{1,65},{2,18},{3,67},{4,20},{5,69},{6,22},{7,71},{8,24},{9,... | collective-permute-start | bytes 1572872 | tf_op jit(solution)/shard_map/ppermute | solution.py:26
  13.4 1.5 %collective-permute-start.1 = (bf16[1024,256]{1,0:T(8,128)(2,1)S(1)}, bf16[1024,256]{1,0:T(8,128)(2,1)S(1)}, u32[]{:S(2)}, u32[]{:S(2)}) collective-permute-start(bf16[1024,256]{1,0:T(8,128)(2,1)S(1)} %get-tuple-element.12), channel_id=1, source_target_pairs={{0,48},{1,193},{2,50},{3,195},{4,52},{5,197},{6,54},{7,199},{8,56}... | collective-permute-start | bytes 1572872 | tf_op jit(solution)/shard_map/ppermute | solution.py:26
  14.9 1.6 %collective-permute-start.3 = (bf16[512,256]{1,0:T(8,128)(2,1)S(1)}, bf16[512,256]{1,0:T(8,128)(2,1)S(1)}, u32[]{:S(2)}, u32[]{:S(2)}) collective-permute-start(bf16[512,256]{1,0:T(8,128)(2,1)S(1)} %pad_maximum_fusion.3), channel_id=1, source_target_pairs={{0,32},{1,129},{2,34},{3,131},{4,36},{5,133},{6,38},{7,135},{8,40}... | collective-permute-start | bytes 786440 | tf_op jit(solution)/shard_map/ppermute | solution.py:26
  16.6 0.0 copy-done.5
  16.6 0.0 copy-done.6
  16.6 0.0 copy-start.1
  16.6 1.5 %collective-permute-start.2 = (bf16[512,256]{1,0:T(8,128)(2,1)S(1)}, bf16[512,256]{1,0:T(8,128)(2,1)S(1)}, u32[]{:S(2)}, u32[]{:S(2)}) collective-permute-start(bf16[512,256]{1,0:T(8,128)(2,1)S(1)} %pad_maximum_fusion.2), channel_id=1, source_target_pairs={{0,32},{1,129},{2,34},{3,131},{4,36},{5,133},{6,38},{7,135},{8,40}... | collective-permute-start | bytes 786440 | tf_op jit(solution)/shard_map/ppermute | solution.py:26
  18.1 3.6 %collective-permute-done = bf16[1024,256]{1,0:T(8,128)(2,1)S(1)} collective-permute-done((bf16[1024,256]{1,0:T(8,128)(2,1)S(1)}, bf16[1024,256]{1,0:T(8,128)(2,1)S(1)}, u32[]{:S(2)}, u32[]{:S(2)}) %collective-permute-start) | collective-permute-done | bytes 524320 | tf_op jit(solution)/shard_map/ppermute | solution.py:26
  21.7 3.9 %collective-permute-done.3 = bf16[512,256]{1,0:T(8,128)(2,1)S(1)} collective-permute-done((bf16[512,256]{1,0:T(8,128)(2,1)S(1)}, bf16[512,256]{1,0:T(8,128)(2,1)S(1)}, u32[]{:S(2)}, u32[]{:S(2)}) %collective-permute-start.3) | collective-permute-done | bytes 262176 | tf_op jit(solution)/shard_map/ppermute | solution.py:26
  25.7 2.8 %collective-permute-done.2 = bf16[512,256]{1,0:T(8,128)(2,1)S(1)} collective-permute-done((bf16[512,256]{1,0:T(8,128)(2,1)S(1)}, bf16[512,256]{1,0:T(8,128)(2,1)S(1)}, u32[]{:S(2)}, u32[]{:S(2)}) %collective-permute-start.2) | collective-permute-done | bytes 262176 | tf_op jit(solution)/shard_map/ppermute | solution.py:26
  28.5 0.0 collective-permute-done.1
  28.5 0.1 pad_maximum_fusion
  28.6 1.0 collective-permute-start.4
  29.6 1.8 %collective-permute-start.7 = (bf16[2048,256]{1,0:T(8,128)(2,1)S(1)}, bf16[2048,256]{1,0:T(8,128)(2,1)}, u32[]{:S(2)}, u32[]{:S(2)}) collective-permute-start(bf16[2048,256]{1,0:T(8,128)(2,1)S(1)} %pad_maximum_fusion), channel_id=1, source_target_pairs={{0,192},{1,49},{2,194},{3,51},{4,196},{5,53},{6,198},{7,55},{8,200... | collective-permute-start | bytes 3145736 | tf_op jit(solution)/shard_map/ppermute | solution.py:31
  31.3 1.3 collective-permute-start.6
  32.6 0.2 collective-permute-start.5
  32.8 11.1 %collective-permute-done.4 = bf16[2048,256]{1,0:T(8,128)(2,1)S(1)} collective-permute-done((bf16[2048,256]{1,0:T(8,128)(2,1)S(1)}, bf16[2048,256]{1,0:T(8,128)(2,1)S(1)}, u32[]{:S(2)}, u32[]{:S(2)}) %collective-permute-start.4) | collective-permute-done | bytes 1048608 | tf_op jit(solution)/shard_map/ppermute | solution.py:31
  43.9 0.0 collective-permute-start.8
  43.9 0.0 collective-permute-done.7
  43.9 2.7 %collective-permute-start.9 = (bf16[2048,256]{1,0:T(8,128)(2,1)}, bf16[2048,256]{1,0:T(8,128)(2,1)}, u32[]{:S(2)}, u32[]{:S(2)}) collective-permute-start(bf16[2048,256]{1,0:T(8,128)(2,1)} %collective-permute-done.7), channel_id=1, source_target_pairs={{0,192},{1,49},{2,194},{3,51},{4,196},{5,53},{6,198},{7,55},{8,200... | collective-permute-start | bytes 3145736 | tf_op jit(solution)/shard_map/ppermute | solution.py:31
  46.6 0.1 stack.75.table
  46.7 8.2 %collective-permute-done.6 = bf16[2048,256]{1,0:T(8,128)(2,1)} collective-permute-done((bf16[2048,256]{1,0:T(8,128)(2,1)S(1)}, bf16[2048,256]{1,0:T(8,128)(2,1)}, u32[]{:S(2)}, u32[]{:S(2)}) %collective-permute-start.6) | collective-permute-done | bytes 1048608 | tf_op jit(solution)/shard_map/ppermute | solution.py:31
  54.8 0.3 collective-permute-done.5
  55.1 11.2 %collective-permute-done.8 = bf16[2048,256]{1,0:T(8,128)(2,1)} collective-permute-done((bf16[2048,256]{1,0:T(8,128)(2,1)S(1)}, bf16[2048,256]{1,0:T(8,128)(2,1)}, u32[]{:S(2)}, u32[]{:S(2)}) %collective-permute-start.8) | collective-permute-done | bytes 1048608 | tf_op jit(solution)/shard_map/ppermute | solution.py:31
  66.4 0.0 collective-permute-done.9
  66.4 3.7 %all-gather.3.cloned.1.call-done = bf16[16384,256]{1,0:T(8,128)(2,1)} async-done(((bf16[1024,256]{1,0:T(8,128)(2,1)}), bf16[16384,256]{1,0:T(8,128)(2,1)}) %all-gather.3.cloned.1.call-update) | async-done | bytes 8388624 | tf_op jit(solution)/shard_map/all_gather | solution.py:209
  70.0 0.0 copy-done.1
  70.0 8.6 %attend.1 = f32[16,72,128]{2,1,0:T(8,128)S(1)} custom-call(s32[18]{0:T(128)S(1)} %stack.75.table, bf16[16,1024,256]{2,1,0:T(8,128)(2,1)} %bitcast.39, bf16[2,4,256,256]{3,2,1,0:T(8,128)(2,1)S(1)} %bitcast.33, bf16[2,4,256,256]{3,2,1,0:T(8,128)(2,1)S(1)} %bitcast.31, bf16[2,4,256,256]{3,2,1,0:T(8,128)(2,1)S(1)} %bitcast.35, ...), custom_call_target="tpu_custom_call" | custom-call | tf_op jit(solution)/shard_map/attend/pallas_call | solution.py:214
  78.6 0.0 copy-start
  78.7 18.0 %all_to_all.20.parts = f32[16,72,128]{2,1,0:T(8,128)S(1)} all-to-all(f32[16,72,128]{2,1,0:T(8,128)S(1)} %attend.1), channel_id=1, replica_groups=mesh['agent'=16,'tensor'=16] {'agent'}, dimensions={0} | all-to-all | bytes 1179648 | tf_op jit(solution)/shard_map/all_to_all | solution.py:230
  96.7 0.4 combine.1
  97.1 11.7 %all_to_all.21.mine = bf16[8,32,256]{2,1,0:T(8,128)(2,1)S(1)} all-to-all(bf16[8,32,256]{2,1,0:T(8,128)(2,1)S(1)} %combine.1), channel_id=1, replica_groups={{0,2,4,6,8,10,12,14},{1,3,5,7,9,11,13,15},{16,18,20,22,24,26,28,30},{17..., dimensions={0} | all-to-all | bytes 262144 | tf_op jit(solution)/shard_map/all_to_all | solution.py:240
  108.8 0.0 copy-start.2
  108.8 3.1 %collective-permute-start.10 = (bf16[8,32,256]{2,1,0:T(8,128)(2,1)S(1)}, bf16[8,32,256]{2,1,0:T(8,128)(2,1)S(1)}, u32[]{:S(2)}, u32[]{:S(2)}) collective-permute-start(bf16[8,32,256]{2,1,0:T(8,128)(2,1)S(1)} %all_to_all.21.mine), channel_id=1, source_target_pairs={{0,1},{1,0},{2,3},{3,2},{4,5},{5,4},{6,7},{7,6},{8,9},{9,8},{10,11... | collective-permute-start | bytes 393224 | tf_op jit(solution)/shard_map/ppermute | solution.py:36
  111.9 1.0 collective-permute-done.10.theirs
  112.9 0.0 copy-done
  112.9 2.6 %project.1 = (f32[32,256]{1,0:T(8,128)S(1)}, f32[16,8,128]{2,1,0:T(8,128)S(1)}) custom-call(s32[18]{0:T(128)S(1)} %stack.75.table, bf16[8,32,256]{2,1,0:T(8,128)(2,1)S(1)} %all_to_all.21.mine, bf16[8,32,256]{2,1,0:T(8,128)(2,1)S(1)} %collective-permute-done.10.theirs, bf16[2,4,256,256]{3,2,1,0:T(8,128)(2,1)S(1)} %bitcast.34, ...), custom_call_target="tpu_custom_call" | custom-call | tf_op jit(solution)/shard_map/project/pallas_call | solution.py:242
  115.5 10.6 %all_to_all.22.refs_0_ = f32[16,8,128]{2,1,0:T(8,128)S(1)} all-to-all(f32[16,8,128]{2,1,0:T(8,128)S(1)} %get-tuple-element.8), channel_id=1, replica_groups=mesh['agent'=16,'tensor'=16] {'tensor'}, dimensions={0} | all-to-all | bytes 131072 | tf_op jit(solution)/shard_map/all_to_all | solution.py:257
  126.1 0.0 copy-done.2
  126.1 0.2 finish.1
  126.3 13.8 %all_to_all.23 = bf16[16,2,32,256]{3,2,1,0:T(8,128)(2,1)S(1)} all-to-all(bf16[16,2,32,256]{3,2,1,0:T(8,128)(2,1)S(1)} %finish.1), channel_id=1, replica_groups=mesh['agent'=16,'tensor'=16] {'agent'}, dimensions={0} | all-to-all | bytes 1048576 | tf_op jit(solution)/shard_map/all_to_all | solution.py:266
  140.1 0.8 fusion
  (5 shorter events, 0.1 us)
Async XLA Ops:
  7.2 9.4 %copy-start.5 = (bf16[256,256]{1,0:T(8,128)(2,1)S(1)}, bf16[256,256]{1,0:T(8,128)(2,1)}, u32[]{:S(2)}) copy-start(bf16[256,256]{1,0:T(8,128)(2,1)} %param.11) | copy-start | bytes 393220
  7.2 9.4 %copy-start.6 = (bf16[256,256]{1,0:T(8,128)(2,1)S(1)}, bf16[256,256]{1,0:T(8,128)(2,1)}, u32[]{:S(2)}) copy-start(bf16[256,256]{1,0:T(8,128)(2,1)} %param.12) | copy-start | bytes 393220
  7.2 3.9 %copy-start.3 = (bf16[256,256]{1,0:T(8,128)(2,1)S(1)}, bf16[256,256]{1,0:T(8,128)(2,1)}, u32[]{:S(2)}) copy-start(bf16[256,256]{1,0:T(8,128)(2,1)} %param.13) | copy-start | bytes 393220
  7.2 4.0 %copy-start.4 = (bf16[256,256]{1,0:T(8,128)(2,1)S(1)}, bf16[256,256]{1,0:T(8,128)(2,1)}, u32[]{:S(2)}) copy-start(bf16[256,256]{1,0:T(8,128)(2,1)} %param.14) | copy-start | bytes 393220
  7.2 62.8 %all-gather.3.cloned.1.call-start = ((), (), s32[]{:S(2)}) async-start(), calls=%async_computation.4 | async-start | bytes 8912896 | tf_op jit(solution)/shard_map/all_gather | solution.py:209
  11.2 10.5 %collective-permute-start = (bf16[1024,256]{1,0:T(8,128)(2,1)S(1)}, bf16[1024,256]{1,0:T(8,128)(2,1)S(1)}, u32[]{:S(2)}, u32[]{:S(2)}) collective-permute-start(bf16[1024,256]{1,0:T(8,128)(2,1)S(1)} %get-tuple-element.12), channel_id=1, source_target_pairs={{0,16},{1,65},{2,18},{3,67},{4,20},{5,69},{6,22},{7,71},{8,24},{9,... | collective-permute-start | bytes 1572872 | tf_op jit(solution)/shard_map/ppermute | solution.py:26
  13.4 15.1 %collective-permute-start.1 = (bf16[1024,256]{1,0:T(8,128)(2,1)S(1)}, bf16[1024,256]{1,0:T(8,128)(2,1)S(1)}, u32[]{:S(2)}, u32[]{:S(2)}) collective-permute-start(bf16[1024,256]{1,0:T(8,128)(2,1)S(1)} %get-tuple-element.12), channel_id=1, source_target_pairs={{0,48},{1,193},{2,50},{3,195},{4,52},{5,197},{6,54},{7,199},{8,56}... | collective-permute-start | bytes 1572872 | tf_op jit(solution)/shard_map/ppermute | solution.py:26
  14.9 10.7 %collective-permute-start.3 = (bf16[512,256]{1,0:T(8,128)(2,1)S(1)}, bf16[512,256]{1,0:T(8,128)(2,1)S(1)}, u32[]{:S(2)}, u32[]{:S(2)}) collective-permute-start(bf16[512,256]{1,0:T(8,128)(2,1)S(1)} %pad_maximum_fusion.3), channel_id=1, source_target_pairs={{0,32},{1,129},{2,34},{3,131},{4,36},{5,133},{6,38},{7,135},{8,40}... | collective-permute-start | bytes 786440 | tf_op jit(solution)/shard_map/ppermute | solution.py:26
  16.6 53.4 %copy-start.1 = (s32[512]{0:T(512)S(1)}, s32[512]{0:T(512)}, u32[]{:S(2)}) copy-start(s32[512]{0:T(512)} %param.9) | copy-start | bytes 6148
  16.6 11.9 %collective-permute-start.2 = (bf16[512,256]{1,0:T(8,128)(2,1)S(1)}, bf16[512,256]{1,0:T(8,128)(2,1)S(1)}, u32[]{:S(2)}, u32[]{:S(2)}) collective-permute-start(bf16[512,256]{1,0:T(8,128)(2,1)S(1)} %pad_maximum_fusion.2), channel_id=1, source_target_pairs={{0,32},{1,129},{2,34},{3,131},{4,36},{5,133},{6,38},{7,135},{8,40}... | collective-permute-start | bytes 786440 | tf_op jit(solution)/shard_map/ppermute | solution.py:26
  28.6 15.3 %collective-permute-start.4 = (bf16[2048,256]{1,0:T(8,128)(2,1)S(1)}, bf16[2048,256]{1,0:T(8,128)(2,1)S(1)}, u32[]{:S(2)}, u32[]{:S(2)}) collective-permute-start(bf16[2048,256]{1,0:T(8,128)(2,1)S(1)} %constant_dynamic-update-slice_fusion.4), channel_id=1, source_target_pairs={{0,64},{1,17},{2,66},{3,19},{4,68},{5,21},{6,70},{7,23},{8,72},{9,... | collective-permute-start | bytes 3145736 | tf_op jit(solution)/shard_map/ppermute | solution.py:31
  29.6 14.3 %collective-permute-start.7 = (bf16[2048,256]{1,0:T(8,128)(2,1)S(1)}, bf16[2048,256]{1,0:T(8,128)(2,1)}, u32[]{:S(2)}, u32[]{:S(2)}) collective-permute-start(bf16[2048,256]{1,0:T(8,128)(2,1)S(1)} %pad_maximum_fusion), channel_id=1, source_target_pairs={{0,192},{1,49},{2,194},{3,51},{4,196},{5,53},{6,198},{7,55},{8,200... | collective-permute-start | bytes 3145736 | tf_op jit(solution)/shard_map/ppermute | solution.py:31
  31.3 23.5 %collective-permute-start.6 = (bf16[2048,256]{1,0:T(8,128)(2,1)S(1)}, bf16[2048,256]{1,0:T(8,128)(2,1)}, u32[]{:S(2)}, u32[]{:S(2)}) collective-permute-start(bf16[2048,256]{1,0:T(8,128)(2,1)S(1)} %constant_dynamic-update-slice_fusion.4), channel_id=1, source_target_pairs={{0,192},{1,49},{2,194},{3,51},{4,196},{5,53},{6,198},{7,55},{8,200... | collective-permute-start | bytes 3145736 | tf_op jit(solution)/shard_map/ppermute | solution.py:31
  32.6 22.5 %collective-permute-start.5 = (bf16[2048,256]{1,0:T(8,128)(2,1)S(1)}, bf16[2048,256]{1,0:T(8,128)(2,1)}, u32[]{:S(2)}, u32[]{:S(2)}) collective-permute-start(bf16[2048,256]{1,0:T(8,128)(2,1)S(1)} %pad_maximum_fusion), channel_id=1, source_target_pairs={{0,64},{1,17},{2,66},{3,19},{4,68},{5,21},{6,70},{7,23},{8,72},{9,... | collective-permute-start | bytes 3145736 | tf_op jit(solution)/shard_map/ppermute | solution.py:31
  43.9 22.5 %collective-permute-start.8 = (bf16[2048,256]{1,0:T(8,128)(2,1)S(1)}, bf16[2048,256]{1,0:T(8,128)(2,1)}, u32[]{:S(2)}, u32[]{:S(2)}) collective-permute-start(bf16[2048,256]{1,0:T(8,128)(2,1)S(1)} %collective-permute-done.4), channel_id=1, source_target_pairs={{0,64},{1,17},{2,66},{3,19},{4,68},{5,21},{6,70},{7,23},{8,72},{9,... | collective-permute-start | bytes 3145736 | tf_op jit(solution)/shard_map/ppermute | solution.py:31
  43.9 22.5 %collective-permute-start.9 = (bf16[2048,256]{1,0:T(8,128)(2,1)}, bf16[2048,256]{1,0:T(8,128)(2,1)}, u32[]{:S(2)}, u32[]{:S(2)}) collective-permute-start(bf16[2048,256]{1,0:T(8,128)(2,1)} %collective-permute-done.7), channel_id=1, source_target_pairs={{0,192},{1,49},{2,194},{3,51},{4,196},{5,53},{6,198},{7,55},{8,200... | collective-permute-start | bytes 3145736 | tf_op jit(solution)/shard_map/ppermute | solution.py:31
  78.6 34.2 %copy-start = (bf16[512,256]{1,0:T(8,128)(2,1)S(1)}, bf16[512,256]{1,0:T(8,128)(2,1)}, u32[]{:S(2)}) copy-start(bf16[512,256]{1,0:T(8,128)(2,1)} %refs_8_.1) | copy-start | bytes 786436
  108.8 17.3 %copy-start.2 = (f32[256]{0:T(256)S(1)}, f32[256]{0:T(256)}, u32[]{:S(2)}) copy-start(f32[256]{0:T(256)} %param.15) | copy-start | bytes 3076
  108.8 4.1 %collective-permute-start.10 = (bf16[8,32,256]{2,1,0:T(8,128)(2,1)S(1)}, bf16[8,32,256]{2,1,0:T(8,128)(2,1)S(1)}, u32[]{:S(2)}, u32[]{:S(2)}) collective-permute-start(bf16[8,32,256]{2,1,0:T(8,128)(2,1)S(1)} %all_to_all.21.mine), channel_id=1, source_target_pairs={{0,1},{1,0},{2,3},{3,2},{4,5},{5,4},{6,7},{7,6},{8,9},{9,8},{10,11... | collective-permute-start | bytes 393224 | tf_op jit(solution)/shard_map/ppermute | solution.py:36
Sparse Core Ops, SparseCore 0:
  9.9 60.1 all-gather.2

commit v7 on v6

--- a/solution.py
+++ b/solution.py
@@ -69,7 +69,7 @@
 
 def attend_kernel(table, feats, *refs):
     w_refs = refs[:8]
-    valid, out, x_all, w_all, acc, stat, x_sem, w_sem = refs[8:]
+    valid, out, w_out, x_all, w_all, acc, stat, x_sem, w_sem, out_sem = refs[8:]
     rows = feats.shape[1] // 2
     depth = feats.shape[2]
     parts = 8
@@ -85,6 +85,15 @@
     for part in copies:
         for copy in part:
             copy.start()
+    out_copies = [
+        pltpu.make_async_copy(
+            w_refs[n].at[:, 3], w_out.at[pl.ds(n * step, step)], out_sem.at[n])
+        for n in range(2, parts)
+    ]
+    for copy in out_copies:
+        copy.start()
+    for n in range(2):
+        w_out[pl.ds(n * step, step)] = w_refs[n][:, 3]
     sums = [None] * 3
     for part in range(parts):
         for copy in copies[part]:
@@ -129,6 +138,8 @@
         packed = jnp.where(lane == 4 * tile + 2 * head + 1, total, packed)
     stat[...] = packed.reshape(GROUP, chunk // 8, 8, HEAD_DIM)
     out[:, pl.ds(2 * chunk, 8), :] = stat[:, 0] + stat[:, 1] + stat[:, 2] + stat[:, 3]
+    for copy in out_copies:
+        copy.wait()
 
 
 def combine_kernel(parts, out):
@@ -152,16 +163,9 @@
         out[t] = attended
 
 
-def project_kernel(table, mine, theirs, *refs):
-    w_refs, (latents, upd, squares, w_all, rows, w_sem, sem) = refs[:8], refs[8:]
+def project_kernel(table, mine, theirs, w_out, latents, upd, squares, rows, sem):
     chunk, depth = upd.shape
     agent, core = table[GROUP], table[GROUP + 1]
-    copies = [
-        pltpu.make_async_copy(w_refs[n].at[:, 3], w_all.at[pl.ds(2 * n, 2)], w_sem.at[n])
-        for n in range(8)
-    ]
-    for copy in copies:
-        copy.start()
     copy = pltpu.make_async_copy(
         latents.at[pl.ds(pl.multiple_of(agent * chunk, chunk), chunk)], rows, sem)
     copy.start()
@@ -169,9 +173,7 @@
     for slot in range(GROUP):
         block = table[slot]
         lefts.append(jnp.where(block % 2 == core, mine[block // 2], theirs[block // 2]))
-    for each in copies:
-        each.wait()
-    total = jnp.dot(jnp.concatenate(lefts, axis=1), w_all[...].reshape(GROUP * depth, depth),
+    total = jnp.dot(jnp.concatenate(lefts, axis=1), w_out[...].reshape(GROUP * depth, depth),
                     preferred_element_type=F32)
     copy.wait()
     total += rows[...].astype(F32)
@@ -211,11 +213,12 @@
     table = index_table()
     smem = pl.BlockSpec(memory_space=pltpu.SMEM)
     hbm = pl.BlockSpec(memory_space=pltpu.HBM)
-    partial = pl.pallas_call(
+    partial, out_weight = pl.pallas_call(
         attend_kernel,
-        out_shape=jax.ShapeDtypeStruct((GROUP, 2 * chunk + 8, HEAD_DIM), F32),
+        out_shape=(jax.ShapeDtypeStruct((GROUP, 2 * chunk + 8, HEAD_DIM), F32),
+                   jax.ShapeDtypeStruct((GROUP, depth, depth), BF16)),
         in_specs=[smem, hbm] + whole(2) + [hbm] * 6 + whole(1),
-        out_specs=whole(1)[0],
+        out_specs=tuple(whole(2)),
         scratch_shapes=[
             pltpu.VMEM((2 * rows, GROUP * depth), BF16),
             pltpu.VMEM((3, GROUP, depth, depth), BF16),
@@ -223,6 +226,7 @@
             pltpu.VMEM((GROUP, chunk // 8, 8, HEAD_DIM), F32),
             pltpu.SemaphoreType.DMA((GROUP,)),
             pltpu.SemaphoreType.DMA((3, 8)),
+            pltpu.SemaphoreType.DMA((8,)),
         ],
         compiler_params=pltpu.CompilerParams(vmem_limit_bytes=40 * 2**20),
         name="attend",
@@ -243,17 +247,15 @@
         project_kernel,
         out_shape=(jax.ShapeDtypeStruct((chunk, depth), F32),
                    jax.ShapeDtypeStruct((GROUP, 8, HEAD_DIM), F32)),
-        in_specs=[smem] + whole(2) + [hbm] * 9,
+        in_specs=[smem] + whole(3) + [hbm],
         out_specs=tuple(whole(2)),
         scratch_shapes=[
-            pltpu.VMEM((GROUP, depth, depth), BF16),
             pltpu.VMEM((chunk, depth), BF16),
-            pltpu.SemaphoreType.DMA((8,)),
             pltpu.SemaphoreType.DMA,
         ],
         compiler_params=pltpu.CompilerParams(vmem_limit_bytes=8 * 2**20),
         name="project",
-    )(table, attended, theirs, *weights, latents)
+    )(table, attended, theirs, out_weight, latents)
     squares = lax.all_to_all(squares, "tensor", 0, 0)
     out = pl.pallas_call(
         lambda *refs: finish_kernel(width, *refs),

time: 148 us -> 147 us (level)
  no operation moved by 1% of the time
where the time goes in v7:
time: 147 us
  blocking collectives  54.1 us (37%)
  waiting for transfers between devices  45.8 us (31%)
  starting transfers between devices  16.9 us (11%)
  between operations  14.2 us (10%)
  Pallas kernels  10.6 us (7%)
  local copies, waits for them, and re-layouts  2.88 us (2%)
  other arithmetic  2.08 us (1%)
    ppermute x6, waiting for transfers between devices, second(): lax.ppermute(array, ('agent', 'tensor'), pairs(lambda y, x, core: (y + by...  30.8 us
    all_to_all x1, blocking collectives, body(): partial = lax.all_to_all(partial, 'agent', 0, 0)  18 us
    all_to_all x1, blocking collectives, body(): out = lax.all_to_all(out, 'agent', 0, 0)  13.8 us
    all_to_all x1, blocking collectives, body(): lax.all_to_all(attended, 'tensor', 0, 0, axis_index_groups=same_core)  11.7 us
    all_to_all x1, blocking collectives, body(): squares = lax.all_to_all(squares, 'tensor', 0, 0)  10.6 us
    ppermute x4, waiting for transfers between devices, first(): lax.ppermute(array, ('agent', 'tensor'), pairs(lambda y, x, core: (y, x +...  10.3 us
    pallas_call x1, Pallas kernels, body(): pl.pallas_call(attend_kernel, out_shape=(jax.ShapeDtypeStruct((GROUP, 2 *...  8.68 us
    ppermute x6, starting transfers between devices, second(): lax.ppermute(array, ('agent', 'tensor'), pairs(lambda y, x, core: (y + by...  6.9 us
  transfers between devices with their start and end apart: 12, of which 9 were waited for; matrix products, arithmetic and copies ran while one was open for 1% of the time, Pallas kernels for 0%

profile of v7, /device:TPU:1, one launch (start us, length us, event | category | flops | bytes accessed | tf_op | source)
XLA Modules:
  0.0 146.5 jit_solution(15249209538129277054)
XLA Ops:
  7.2 0.0 copy-start.5
  7.2 0.0 copy-start.6
  7.2 0.0 copy-start.3
  7.2 0.0 copy-start.4
  7.2 0.0 all-gather.3.cloned.1.call-start
  7.3 2.0 %pad_maximum_fusion.1 = bf16[1024,256]{1,0:T(8,128)(2,1)} fusion(bf16[512,256]{1,0:T(8,128)(2,1)} %latents.1, bf16[512,256]{1,0:T(8,128)(2,1)} %param.8), kind=kLoop, calls=%fused_computation.1 | loop fusion | flops 1048576 | bytes 1048576 | tf_op jit(solution)/shard_map/concatenate | solution.py:210
  9.2 0.0 all-gather.3.cloned.1.call-update
  9.3 0.9 constant_dynamic-update-slice_fusion.3
  10.2 0.9 constant_dynamic-update-slice_fusion.2
  11.1 0.0 copy-done.3
  11.2 0.0 copy-done.4
  11.2 2.2 %collective-permute-start = (bf16[1024,256]{1,0:T(8,128)(2,1)S(1)}, bf16[1024,256]{1,0:T(8,128)(2,1)S(1)}, u32[]{:S(2)}, u32[]{:S(2)}) collective-permute-start(bf16[1024,256]{1,0:T(8,128)(2,1)S(1)} %get-tuple-element.16), channel_id=1, source_target_pairs={{0,16},{1,65},{2,18},{3,67},{4,20},{5,69},{6,22},{7,71},{8,24},{9,... | collective-permute-start | bytes 1572872 | tf_op jit(solution)/shard_map/ppermute | solution.py:26
  13.4 1.5 %collective-permute-start.1 = (bf16[1024,256]{1,0:T(8,128)(2,1)S(1)}, bf16[1024,256]{1,0:T(8,128)(2,1)S(1)}, u32[]{:S(2)}, u32[]{:S(2)}) collective-permute-start(bf16[1024,256]{1,0:T(8,128)(2,1)S(1)} %get-tuple-element.16), channel_id=1, source_target_pairs={{0,48},{1,193},{2,50},{3,195},{4,52},{5,197},{6,54},{7,199},{8,56}... | collective-permute-start | bytes 1572872 | tf_op jit(solution)/shard_map/ppermute | solution.py:26
  14.9 1.6 %collective-permute-start.3 = (bf16[512,256]{1,0:T(8,128)(2,1)S(1)}, bf16[512,256]{1,0:T(8,128)(2,1)S(1)}, u32[]{:S(2)}, u32[]{:S(2)}) collective-permute-start(bf16[512,256]{1,0:T(8,128)(2,1)S(1)} %pad_maximum_fusion.3), channel_id=1, source_target_pairs={{0,32},{1,129},{2,34},{3,131},{4,36},{5,133},{6,38},{7,135},{8,40}... | collective-permute-start | bytes 786440 | tf_op jit(solution)/shard_map/ppermute | solution.py:26
  16.6 0.0 copy-done.5
  16.6 0.0 copy-done.6
  16.6 0.0 copy-start.1
  16.6 1.5 %collective-permute-start.2 = (bf16[512,256]{1,0:T(8,128)(2,1)S(1)}, bf16[512,256]{1,0:T(8,128)(2,1)S(1)}, u32[]{:S(2)}, u32[]{:S(2)}) collective-permute-start(bf16[512,256]{1,0:T(8,128)(2,1)S(1)} %pad_maximum_fusion.2), channel_id=1, source_target_pairs={{0,32},{1,129},{2,34},{3,131},{4,36},{5,133},{6,38},{7,135},{8,40}... | collective-permute-start | bytes 786440 | tf_op jit(solution)/shard_map/ppermute | solution.py:26
  18.1 3.6 %collective-permute-done = bf16[1024,256]{1,0:T(8,128)(2,1)S(1)} collective-permute-done((bf16[1024,256]{1,0:T(8,128)(2,1)S(1)}, bf16[1024,256]{1,0:T(8,128)(2,1)S(1)}, u32[]{:S(2)}, u32[]{:S(2)}) %collective-permute-start) | collective-permute-done | bytes 524320 | tf_op jit(solution)/shard_map/ppermute | solution.py:26
  21.7 3.9 %collective-permute-done.3 = bf16[512,256]{1,0:T(8,128)(2,1)S(1)} collective-permute-done((bf16[512,256]{1,0:T(8,128)(2,1)S(1)}, bf16[512,256]{1,0:T(8,128)(2,1)S(1)}, u32[]{:S(2)}, u32[]{:S(2)}) %collective-permute-start.3) | collective-permute-done | bytes 262176 | tf_op jit(solution)/shard_map/ppermute | solution.py:26
  25.7 2.8 %collective-permute-done.2 = bf16[512,256]{1,0:T(8,128)(2,1)S(1)} collective-permute-done((bf16[512,256]{1,0:T(8,128)(2,1)S(1)}, bf16[512,256]{1,0:T(8,128)(2,1)S(1)}, u32[]{:S(2)}, u32[]{:S(2)}) %collective-permute-start.2) | collective-permute-done | bytes 262176 | tf_op jit(solution)/shard_map/ppermute | solution.py:26
  28.5 0.0 collective-permute-done.1
  28.5 0.1 pad_maximum_fusion
  28.6 1.0 collective-permute-start.4
  29.6 1.8 %collective-permute-start.7 = (bf16[2048,256]{1,0:T(8,128)(2,1)S(1)}, bf16[2048,256]{1,0:T(8,128)(2,1)}, u32[]{:S(2)}, u32[]{:S(2)}) collective-permute-start(bf16[2048,256]{1,0:T(8,128)(2,1)S(1)} %pad_maximum_fusion), channel_id=1, source_target_pairs={{0,192},{1,49},{2,194},{3,51},{4,196},{5,53},{6,198},{7,55},{8,200... | collective-permute-start | bytes 3145736 | tf_op jit(solution)/shard_map/ppermute | solution.py:31
  31.3 1.3 collective-permute-start.6
  32.6 0.2 collective-permute-start.5
  32.8 11.1 %collective-permute-done.4 = bf16[2048,256]{1,0:T(8,128)(2,1)S(1)} collective-permute-done((bf16[2048,256]{1,0:T(8,128)(2,1)S(1)}, bf16[2048,256]{1,0:T(8,128)(2,1)S(1)}, u32[]{:S(2)}, u32[]{:S(2)}) %collective-permute-start.4) | collective-permute-done | bytes 1048608 | tf_op jit(solution)/shard_map/ppermute | solution.py:31
  43.9 0.0 collective-permute-start.8
  43.9 0.0 collective-permute-done.7
  43.9 2.7 %collective-permute-start.9 = (bf16[2048,256]{1,0:T(8,128)(2,1)}, bf16[2048,256]{1,0:T(8,128)(2,1)}, u32[]{:S(2)}, u32[]{:S(2)}) collective-permute-start(bf16[2048,256]{1,0:T(8,128)(2,1)} %collective-permute-done.7), channel_id=1, source_target_pairs={{0,192},{1,49},{2,194},{3,51},{4,196},{5,53},{6,198},{7,55},{8,200... | collective-permute-start | bytes 3145736 | tf_op jit(solution)/shard_map/ppermute | solution.py:31
  46.6 0.1 stack.75.table
  46.7 8.2 %collective-permute-done.6 = bf16[2048,256]{1,0:T(8,128)(2,1)} collective-permute-done((bf16[2048,256]{1,0:T(8,128)(2,1)S(1)}, bf16[2048,256]{1,0:T(8,128)(2,1)}, u32[]{:S(2)}, u32[]{:S(2)}) %collective-permute-start.6) | collective-permute-done | bytes 1048608 | tf_op jit(solution)/shard_map/ppermute | solution.py:31
  54.8 0.3 collective-permute-done.5
  55.1 11.2 %collective-permute-done.8 = bf16[2048,256]{1,0:T(8,128)(2,1)} collective-permute-done((bf16[2048,256]{1,0:T(8,128)(2,1)S(1)}, bf16[2048,256]{1,0:T(8,128)(2,1)}, u32[]{:S(2)}, u32[]{:S(2)}) %collective-permute-start.8) | collective-permute-done | bytes 1048608 | tf_op jit(solution)/shard_map/ppermute | solution.py:31
  66.4 0.0 collective-permute-done.9
  66.4 3.7 %all-gather.3.cloned.1.call-done = bf16[16384,256]{1,0:T(8,128)(2,1)} async-done(((bf16[1024,256]{1,0:T(8,128)(2,1)}), bf16[16384,256]{1,0:T(8,128)(2,1)}) %all-gather.3.cloned.1.call-update) | async-done | bytes 8388624 | tf_op jit(solution)/shard_map/all_gather | solution.py:211
  70.0 0.0 copy-done.1
  70.0 8.7 %attend.1 = (f32[16,72,128]{2,1,0:T(8,128)S(1)}, bf16[16,256,256]{2,1,0:T(8,128)(2,1)S(1)}) custom-call(s32[18]{0:T(128)S(1)} %stack.75.table, bf16[16,1024,256]{2,1,0:T(8,128)(2,1)} %bitcast.36, bf16[2,4,256,256]{3,2,1,0:T(8,128)(2,1)S(1)} %bitcast.32, bf16[2,4,256,256]{3,2,1,0:T(8,128)(2,1)S(1)} %bitcast.31, bf16[2,4,256,256]{3,2,1,0:T(8,128)(2,1)S(1)} %bitcast.33, ...), custom_call_target="tpu_custom_call" | custom-call | tf_op jit(solution)/shard_map/attend/pallas_call | solution.py:216
  78.7 0.0 copy-start
  78.7 18.0 %all_to_all.20.parts = f32[16,72,128]{2,1,0:T(8,128)S(1)} all-to-all(f32[16,72,128]{2,1,0:T(8,128)S(1)} %get-tuple-element.10), channel_id=1, replica_groups=mesh['agent'=16,'tensor'=16] {'agent'}, dimensions={0} | all-to-all | bytes 1179648 | tf_op jit(solution)/shard_map/all_to_all | solution.py:234
  96.7 0.0 copy-start.2
  96.7 0.4 combine.1
  97.1 11.7 %all_to_all.21.mine = bf16[8,32,256]{2,1,0:T(8,128)(2,1)S(1)} all-to-all(bf16[8,32,256]{2,1,0:T(8,128)(2,1)S(1)} %combine.1), channel_id=1, replica_groups={{0,2,4,6,8,10,12,14},{1,3,5,7,9,11,13,15},{16,18,20,22,24,26,28,30},{17..., dimensions={0} | all-to-all | bytes 262144 | tf_op jit(solution)/shard_map/all_to_all | solution.py:244
  108.8 3.1 %collective-permute-start.10 = (bf16[8,32,256]{2,1,0:T(8,128)(2,1)S(1)}, bf16[8,32,256]{2,1,0:T(8,128)(2,1)S(1)}, u32[]{:S(2)}, u32[]{:S(2)}) collective-permute-start(bf16[8,32,256]{2,1,0:T(8,128)(2,1)S(1)} %all_to_all.21.mine), channel_id=1, source_target_pairs={{0,1},{1,0},{2,3},{3,2},{4,5},{5,4},{6,7},{7,6},{8,9},{9,8},{10,11... | collective-permute-start | bytes 393224 | tf_op jit(solution)/shard_map/ppermute | solution.py:36
  112.0 1.0 collective-permute-done.10.theirs
  112.9 0.0 copy-done
  112.9 1.3 project.1
  114.3 10.6 %all_to_all.22.refs_0_ = f32[16,8,128]{2,1,0:T(8,128)S(1)} all-to-all(f32[16,8,128]{2,1,0:T(8,128)S(1)} %get-tuple-element.12), channel_id=1, replica_groups=mesh['agent'=16,'tensor'=16] {'tensor'}, dimensions={0} | all-to-all | bytes 131072 | tf_op jit(solution)/shard_map/all_to_all | solution.py:259
  124.9 0.0 copy-done.2
  124.9 0.2 finish.1
  125.1 13.8 %all_to_all.23 = bf16[16,2,32,256]{3,2,1,0:T(8,128)(2,1)S(1)} all-to-all(bf16[16,2,32,256]{3,2,1,0:T(8,128)(2,1)S(1)} %finish.1), channel_id=1, replica_groups=mesh['agent'=16,'tensor'=16] {'agent'}, dimensions={0} | all-to-all | bytes 1048576 | tf_op jit(solution)/shard_map/all_to_all | solution.py:268
  138.8 0.8 fusion
  (5 shorter events, 0.1 us)
Async XLA Ops:
  7.2 9.4 %copy-start.5 = (bf16[256,256]{1,0:T(8,128)(2,1)S(1)}, bf16[256,256]{1,0:T(8,128)(2,1)}, u32[]{:S(2)}) copy-start(bf16[256,256]{1,0:T(8,128)(2,1)} %param.11) | copy-start | bytes 393220
  7.2 9.4 %copy-start.6 = (bf16[256,256]{1,0:T(8,128)(2,1)S(1)}, bf16[256,256]{1,0:T(8,128)(2,1)}, u32[]{:S(2)}) copy-start(bf16[256,256]{1,0:T(8,128)(2,1)} %param.12) | copy-start | bytes 393220
  7.2 3.9 %copy-start.3 = (bf16[256,256]{1,0:T(8,128)(2,1)S(1)}, bf16[256,256]{1,0:T(8,128)(2,1)}, u32[]{:S(2)}) copy-start(bf16[256,256]{1,0:T(8,128)(2,1)} %param.13) | copy-start | bytes 393220
  7.2 4.0 %copy-start.4 = (bf16[256,256]{1,0:T(8,128)(2,1)S(1)}, bf16[256,256]{1,0:T(8,128)(2,1)}, u32[]{:S(2)}) copy-start(bf16[256,256]{1,0:T(8,128)(2,1)} %param.14) | copy-start | bytes 393220
  7.2 62.8 %all-gather.3.cloned.1.call-start = ((), (), s32[]{:S(2)}) async-start(), calls=%async_computation.4 | async-start | bytes 8912896 | tf_op jit(solution)/shard_map/all_gather | solution.py:211
  11.2 10.5 %collective-permute-start = (bf16[1024,256]{1,0:T(8,128)(2,1)S(1)}, bf16[1024,256]{1,0:T(8,128)(2,1)S(1)}, u32[]{:S(2)}, u32[]{:S(2)}) collective-permute-start(bf16[1024,256]{1,0:T(8,128)(2,1)S(1)} %get-tuple-element.16), channel_id=1, source_target_pairs={{0,16},{1,65},{2,18},{3,67},{4,20},{5,69},{6,22},{7,71},{8,24},{9,... | collective-permute-start | bytes 1572872 | tf_op jit(solution)/shard_map/ppermute | solution.py:26
  13.4 15.1 %collective-permute-start.1 = (bf16[1024,256]{1,0:T(8,128)(2,1)S(1)}, bf16[1024,256]{1,0:T(8,128)(2,1)S(1)}, u32[]{:S(2)}, u32[]{:S(2)}) collective-permute-start(bf16[1024,256]{1,0:T(8,128)(2,1)S(1)} %get-tuple-element.16), channel_id=1, source_target_pairs={{0,48},{1,193},{2,50},{3,195},{4,52},{5,197},{6,54},{7,199},{8,56}... | collective-permute-start | bytes 1572872 | tf_op jit(solution)/shard_map/ppermute | solution.py:26
  14.9 10.7 %collective-permute-start.3 = (bf16[512,256]{1,0:T(8,128)(2,1)S(1)}, bf16[512,256]{1,0:T(8,128)(2,1)S(1)}, u32[]{:S(2)}, u32[]{:S(2)}) collective-permute-start(bf16[512,256]{1,0:T(8,128)(2,1)S(1)} %pad_maximum_fusion.3), channel_id=1, source_target_pairs={{0,32},{1,129},{2,34},{3,131},{4,36},{5,133},{6,38},{7,135},{8,40}... | collective-permute-start | bytes 786440 | tf_op jit(solution)/shard_map/ppermute | solution.py:26
  16.6 53.4 %copy-start.1 = (s32[512]{0:T(512)S(1)}, s32[512]{0:T(512)}, u32[]{:S(2)}) copy-start(s32[512]{0:T(512)} %param.9) | copy-start | bytes 6148
  16.6 11.9 %collective-permute-start.2 = (bf16[512,256]{1,0:T(8,128)(2,1)S(1)}, bf16[512,256]{1,0:T(8,128)(2,1)S(1)}, u32[]{:S(2)}, u32[]{:S(2)}) collective-permute-start(bf16[512,256]{1,0:T(8,128)(2,1)S(1)} %pad_maximum_fusion.2), channel_id=1, source_target_pairs={{0,32},{1,129},{2,34},{3,131},{4,36},{5,133},{6,38},{7,135},{8,40}... | collective-permute-start | bytes 786440 | tf_op jit(solution)/shard_map/ppermute | solution.py:26
  28.6 15.3 %collective-permute-start.4 = (bf16[2048,256]{1,0:T(8,128)(2,1)S(1)}, bf16[2048,256]{1,0:T(8,128)(2,1)S(1)}, u32[]{:S(2)}, u32[]{:S(2)}) collective-permute-start(bf16[2048,256]{1,0:T(8,128)(2,1)S(1)} %constant_dynamic-update-slice_fusion.4), channel_id=1, source_target_pairs={{0,64},{1,17},{2,66},{3,19},{4,68},{5,21},{6,70},{7,23},{8,72},{9,... | collective-permute-start | bytes 3145736 | tf_op jit(solution)/shard_map/ppermute | solution.py:31
  29.6 14.3 %collective-permute-start.7 = (bf16[2048,256]{1,0:T(8,128)(2,1)S(1)}, bf16[2048,256]{1,0:T(8,128)(2,1)}, u32[]{:S(2)}, u32[]{:S(2)}) collective-permute-start(bf16[2048,256]{1,0:T(8,128)(2,1)S(1)} %pad_maximum_fusion), channel_id=1, source_target_pairs={{0,192},{1,49},{2,194},{3,51},{4,196},{5,53},{6,198},{7,55},{8,200... | collective-permute-start | bytes 3145736 | tf_op jit(solution)/shard_map/ppermute | solution.py:31
  31.3 23.5 %collective-permute-start.6 = (bf16[2048,256]{1,0:T(8,128)(2,1)S(1)}, bf16[2048,256]{1,0:T(8,128)(2,1)}, u32[]{:S(2)}, u32[]{:S(2)}) collective-permute-start(bf16[2048,256]{1,0:T(8,128)(2,1)S(1)} %constant_dynamic-update-slice_fusion.4), channel_id=1, source_target_pairs={{0,192},{1,49},{2,194},{3,51},{4,196},{5,53},{6,198},{7,55},{8,200... | collective-permute-start | bytes 3145736 | tf_op jit(solution)/shard_map/ppermute | solution.py:31
  32.6 22.5 %collective-permute-start.5 = (bf16[2048,256]{1,0:T(8,128)(2,1)S(1)}, bf16[2048,256]{1,0:T(8,128)(2,1)}, u32[]{:S(2)}, u32[]{:S(2)}) collective-permute-start(bf16[2048,256]{1,0:T(8,128)(2,1)S(1)} %pad_maximum_fusion), channel_id=1, source_target_pairs={{0,64},{1,17},{2,66},{3,19},{4,68},{5,21},{6,70},{7,23},{8,72},{9,... | collective-permute-start | bytes 3145736 | tf_op jit(solution)/shard_map/ppermute | solution.py:31
  43.9 22.5 %collective-permute-start.8 = (bf16[2048,256]{1,0:T(8,128)(2,1)S(1)}, bf16[2048,256]{1,0:T(8,128)(2,1)}, u32[]{:S(2)}, u32[]{:S(2)}) collective-permute-start(bf16[2048,256]{1,0:T(8,128)(2,1)S(1)} %collective-permute-done.4), channel_id=1, source_target_pairs={{0,64},{1,17},{2,66},{3,19},{4,68},{5,21},{6,70},{7,23},{8,72},{9,... | collective-permute-start | bytes 3145736 | tf_op jit(solution)/shard_map/ppermute | solution.py:31
  43.9 22.5 %collective-permute-start.9 = (bf16[2048,256]{1,0:T(8,128)(2,1)}, bf16[2048,256]{1,0:T(8,128)(2,1)}, u32[]{:S(2)}, u32[]{:S(2)}) collective-permute-start(bf16[2048,256]{1,0:T(8,128)(2,1)} %collective-permute-done.7), channel_id=1, source_target_pairs={{0,192},{1,49},{2,194},{3,51},{4,196},{5,53},{6,198},{7,55},{8,200... | collective-permute-start | bytes 3145736 | tf_op jit(solution)/shard_map/ppermute | solution.py:31
  78.7 34.2 %copy-start = (bf16[512,256]{1,0:T(8,128)(2,1)S(1)}, bf16[512,256]{1,0:T(8,128)(2,1)}, u32[]{:S(2)}) copy-start(bf16[512,256]{1,0:T(8,128)(2,1)} %latents.1) | copy-start | bytes 786436
  96.7 28.2 %copy-start.2 = (f32[256]{0:T(256)S(1)}, f32[256]{0:T(256)}, u32[]{:S(2)}) copy-start(f32[256]{0:T(256)} %param.15) | copy-start | bytes 3076
  108.8 4.1 %collective-permute-start.10 = (bf16[8,32,256]{2,1,0:T(8,128)(2,1)S(1)}, bf16[8,32,256]{2,1,0:T(8,128)(2,1)S(1)}, u32[]{:S(2)}, u32[]{:S(2)}) collective-permute-start(bf16[8,32,256]{2,1,0:T(8,128)(2,1)S(1)} %all_to_all.21.mine), channel_id=1, source_target_pairs={{0,1},{1,0},{2,3},{3,2},{4,5},{5,4},{6,7},{7,6},{8,9},{9,8},{10,11... | collective-permute-start | bytes 393224 | tf_op jit(solution)/shard_map/ppermute | solution.py:36
Sparse Core Ops, SparseCore 0:
  9.9 60.1 all-gather.2

commit v8 on v7

--- a/solution.py
+++ b/solution.py
@@ -189,14 +189,14 @@
 
 def finish_kernel(width, squares, upd, gain, out):
     total = jnp.sum(squares[...], axis=0)
-    chunk = upd.shape[0]
+    chunk, depth = upd.shape
     mean_sq = jnp.concatenate([total[:, n:n + 1] for n in range(chunk // 8)], axis=0) / width
     u = upd[...]
     normed = (gain[...] * u * lax.rsqrt(mean_sq + 1e-05)).astype(BF16)
     u = u.astype(BF16)
     for a in range(GROUP):
-        out[a, 0] = u
-        out[a, 1] = normed
+        out[a, :, pl.ds(0, depth)] = u
+        out[a, :, pl.ds(depth, depth)] = normed
 
 
 def whole(count):
@@ -259,14 +259,14 @@
     squares = lax.all_to_all(squares, "tensor", 0, 0)
     out = pl.pallas_call(
         lambda *refs: finish_kernel(width, *refs),
-        out_shape=jax.ShapeDtypeStruct((GROUP, 2, chunk, depth), BF16),
+        out_shape=jax.ShapeDtypeStruct((GROUP, chunk, 2 * depth), BF16),
         in_specs=whole(3),
         out_specs=whole(1)[0],
         compiler_params=pltpu.CompilerParams(vmem_limit_bytes=4 * 2**20),
         name="finish",
     )(squares, upd, gain.reshape(1, depth))
     out = lax.all_to_all(out, "agent", 0, 0)
-    return out[:, 0].reshape(-1, depth), out[:, 1].reshape(-1, depth)
+    return out[:, :, :depth].reshape(-1, depth), out[:, :, depth:].reshape(-1, depth)
 
 
 def solution(mesh):

time: 147 us -> 147 us (level)
  no operation moved by 1% of the time
where the time goes in v8:
time: 147 us
  blocking collectives  54.1 us (37%)
  waiting for transfers between devices  45.8 us (31%)
  starting transfers between devices  16.9 us (11%)
  between operations  14.2 us (10%)
  Pallas kernels  10.6 us (7%)
  local copies, waits for them, and re-layouts  2.91 us (2%)
  other arithmetic  2.08 us (1%)
    ppermute x6, waiting for transfers between devices, second(): lax.ppermute(array, ('agent', 'tensor'), pairs(lambda y, x, core: (y + by...  30.8 us
    all_to_all x1, blocking collectives, body(): partial = lax.all_to_all(partial, 'agent', 0, 0)  18 us
    all_to_all x1, blocking collectives, body(): out = lax.all_to_all(out, 'agent', 0, 0)  13.8 us
    all_to_all x1, blocking collectives, body(): lax.all_to_all(attended, 'tensor', 0, 0, axis_index_groups=same_core)  11.7 us
    all_to_all x1, blocking collectives, body(): squares = lax.all_to_all(squares, 'tensor', 0, 0)  10.6 us
    ppermute x4, waiting for transfers between devices, first(): lax.ppermute(array, ('agent', 'tensor'), pairs(lambda y, x, core: (y, x +...  10.3 us
    pallas_call x1, Pallas kernels, body(): pl.pallas_call(attend_kernel, out_shape=(jax.ShapeDtypeStruct((GROUP, 2 *...  8.68 us
    ppermute x6, starting transfers between devices, second(): lax.ppermute(array, ('agent', 'tensor'), pairs(lambda y, x, core: (y + by...  6.9 us
  transfers between devices with their start and end apart: 12, of which 9 were waited for; matrix products, arithmetic and copies ran while one was open for 1% of the time, Pallas kernels for 0%

profile of v8, /device:TPU:1, one launch (start us, length us, event | category | flops | bytes accessed | tf_op | source)
XLA Modules:
  0.0 146.6 jit_solution(8916114176073485430)
XLA Ops:
  7.2 0.0 copy-start.5
  7.2 0.0 copy-start.6
  7.2 0.0 copy-start.3
  7.2 0.0 copy-start.4
  7.2 0.0 all-gather.3.cloned.1.call-start
  7.3 2.0 %pad_maximum_fusion.1 = bf16[1024,256]{1,0:T(8,128)(2,1)} fusion(bf16[512,256]{1,0:T(8,128)(2,1)} %latents.1, bf16[512,256]{1,0:T(8,128)(2,1)} %param.8), kind=kLoop, calls=%fused_computation.1 | loop fusion | flops 1048576 | bytes 1048576 | tf_op jit(solution)/shard_map/concatenate | solution.py:210
  9.2 0.0 all-gather.3.cloned.1.call-update
  9.3 0.9 constant_dynamic-update-slice_fusion.3
  10.2 0.9 constant_dynamic-update-slice_fusion.2
  11.1 0.0 copy-done.3
  11.2 0.0 copy-done.4
  11.2 2.2 %collective-permute-start = (bf16[1024,256]{1,0:T(8,128)(2,1)S(1)}, bf16[1024,256]{1,0:T(8,128)(2,1)S(1)}, u32[]{:S(2)}, u32[]{:S(2)}) collective-permute-start(bf16[1024,256]{1,0:T(8,128)(2,1)S(1)} %get-tuple-element.16), channel_id=1, source_target_pairs={{0,16},{1,65},{2,18},{3,67},{4,20},{5,69},{6,22},{7,71},{8,24},{9,... | collective-permute-start | bytes 1572872 | tf_op jit(solution)/shard_map/ppermute | solution.py:26
  13.4 1.5 %collective-permute-start.1 = (bf16[1024,256]{1,0:T(8,128)(2,1)S(1)}, bf16[1024,256]{1,0:T(8,128)(2,1)S(1)}, u32[]{:S(2)}, u32[]{:S(2)}) collective-permute-start(bf16[1024,256]{1,0:T(8,128)(2,1)S(1)} %get-tuple-element.16), channel_id=1, source_target_pairs={{0,48},{1,193},{2,50},{3,195},{4,52},{5,197},{6,54},{7,199},{8,56}... | collective-permute-start | bytes 1572872 | tf_op jit(solution)/shard_map/ppermute | solution.py:26
  14.9 1.6 %collective-permute-start.3 = (bf16[512,256]{1,0:T(8,128)(2,1)S(1)}, bf16[512,256]{1,0:T(8,128)(2,1)S(1)}, u32[]{:S(2)}, u32[]{:S(2)}) collective-permute-start(bf16[512,256]{1,0:T(8,128)(2,1)S(1)} %pad_maximum_fusion.3), channel_id=1, source_target_pairs={{0,32},{1,129},{2,34},{3,131},{4,36},{5,133},{6,38},{7,135},{8,40}... | collective-permute-start | bytes 786440 | tf_op jit(solution)/shard_map/ppermute | solution.py:26
  16.6 0.0 copy-done.5
  16.6 0.0 copy-done.6
  16.6 0.0 copy-start.1
  16.6 1.5 %collective-permute-start.2 = (bf16[512,256]{1,0:T(8,128)(2,1)S(1)}, bf16[512,256]{1,0:T(8,128)(2,1)S(1)}, u32[]{:S(2)}, u32[]{:S(2)}) collective-permute-start(bf16[512,256]{1,0:T(8,128)(2,1)S(1)} %pad_maximum_fusion.2), channel_id=1, source_target_pairs={{0,32},{1,129},{2,34},{3,131},{4,36},{5,133},{6,38},{7,135},{8,40}... | collective-permute-start | bytes 786440 | tf_op jit(solution)/shard_map/ppermute | solution.py:26
  18.1 3.6 %collective-permute-done = bf16[1024,256]{1,0:T(8,128)(2,1)S(1)} collective-permute-done((bf16[1024,256]{1,0:T(8,128)(2,1)S(1)}, bf16[1024,256]{1,0:T(8,128)(2,1)S(1)}, u32[]{:S(2)}, u32[]{:S(2)}) %collective-permute-start) | collective-permute-done | bytes 524320 | tf_op jit(solution)/shard_map/ppermute | solution.py:26
  21.7 3.9 %collective-permute-done.3 = bf16[512,256]{1,0:T(8,128)(2,1)S(1)} collective-permute-done((bf16[512,256]{1,0:T(8,128)(2,1)S(1)}, bf16[512,256]{1,0:T(8,128)(2,1)S(1)}, u32[]{:S(2)}, u32[]{:S(2)}) %collective-permute-start.3) | collective-permute-done | bytes 262176 | tf_op jit(solution)/shard_map/ppermute | solution.py:26
  25.7 2.8 %collective-permute-done.2 = bf16[512,256]{1,0:T(8,128)(2,1)S(1)} collective-permute-done((bf16[512,256]{1,0:T(8,128)(2,1)S(1)}, bf16[512,256]{1,0:T(8,128)(2,1)S(1)}, u32[]{:S(2)}, u32[]{:S(2)}) %collective-permute-start.2) | collective-permute-done | bytes 262176 | tf_op jit(solution)/shard_map/ppermute | solution.py:26
  28.5 0.0 collective-permute-done.1
  28.5 0.1 pad_maximum_fusion
  28.6 1.0 collective-permute-start.4
  29.6 1.8 %collective-permute-start.7 = (bf16[2048,256]{1,0:T(8,128)(2,1)S(1)}, bf16[2048,256]{1,0:T(8,128)(2,1)}, u32[]{:S(2)}, u32[]{:S(2)}) collective-permute-start(bf16[2048,256]{1,0:T(8,128)(2,1)S(1)} %pad_maximum_fusion), channel_id=1, source_target_pairs={{0,192},{1,49},{2,194},{3,51},{4,196},{5,53},{6,198},{7,55},{8,200... | collective-permute-start | bytes 3145736 | tf_op jit(solution)/shard_map/ppermute | solution.py:31
  31.3 1.3 collective-permute-start.6
  32.6 0.2 collective-permute-start.5
  32.8 11.1 %collective-permute-done.4 = bf16[2048,256]{1,0:T(8,128)(2,1)S(1)} collective-permute-done((bf16[2048,256]{1,0:T(8,128)(2,1)S(1)}, bf16[2048,256]{1,0:T(8,128)(2,1)S(1)}, u32[]{:S(2)}, u32[]{:S(2)}) %collective-permute-start.4) | collective-permute-done | bytes 1048608 | tf_op jit(solution)/shard_map/ppermute | solution.py:31
  43.9 0.0 collective-permute-start.8
  43.9 0.0 collective-permute-done.7
  43.9 2.7 %collective-permute-start.9 = (bf16[2048,256]{1,0:T(8,128)(2,1)}, bf16[2048,256]{1,0:T(8,128)(2,1)}, u32[]{:S(2)}, u32[]{:S(2)}) collective-permute-start(bf16[2048,256]{1,0:T(8,128)(2,1)} %collective-permute-done.7), channel_id=1, source_target_pairs={{0,192},{1,49},{2,194},{3,51},{4,196},{5,53},{6,198},{7,55},{8,200... | collective-permute-start | bytes 3145736 | tf_op jit(solution)/shard_map/ppermute | solution.py:31
  46.6 0.1 stack.75.table
  46.7 8.2 %collective-permute-done.6 = bf16[2048,256]{1,0:T(8,128)(2,1)} collective-permute-done((bf16[2048,256]{1,0:T(8,128)(2,1)S(1)}, bf16[2048,256]{1,0:T(8,128)(2,1)}, u32[]{:S(2)}, u32[]{:S(2)}) %collective-permute-start.6) | collective-permute-done | bytes 1048608 | tf_op jit(solution)/shard_map/ppermute | solution.py:31
  54.8 0.3 collective-permute-done.5
  55.1 11.2 %collective-permute-done.8 = bf16[2048,256]{1,0:T(8,128)(2,1)} collective-permute-done((bf16[2048,256]{1,0:T(8,128)(2,1)S(1)}, bf16[2048,256]{1,0:T(8,128)(2,1)}, u32[]{:S(2)}, u32[]{:S(2)}) %collective-permute-start.8) | collective-permute-done | bytes 1048608 | tf_op jit(solution)/shard_map/ppermute | solution.py:31
  66.4 0.0 collective-permute-done.9
  66.4 3.7 %all-gather.3.cloned.1.call-done = bf16[16384,256]{1,0:T(8,128)(2,1)} async-done(((bf16[1024,256]{1,0:T(8,128)(2,1)}), bf16[16384,256]{1,0:T(8,128)(2,1)}) %all-gather.3.cloned.1.call-update) | async-done | bytes 8388624 | tf_op jit(solution)/shard_map/all_gather | solution.py:211
  70.0 0.0 copy-done.1
  70.0 8.7 %attend.1 = (f32[16,72,128]{2,1,0:T(8,128)S(1)}, bf16[16,256,256]{2,1,0:T(8,128)(2,1)S(1)}) custom-call(s32[18]{0:T(128)S(1)} %stack.75.table, bf16[16,1024,256]{2,1,0:T(8,128)(2,1)} %bitcast.36, bf16[2,4,256,256]{3,2,1,0:T(8,128)(2,1)S(1)} %bitcast.32, bf16[2,4,256,256]{3,2,1,0:T(8,128)(2,1)S(1)} %bitcast.31, bf16[2,4,256,256]{3,2,1,0:T(8,128)(2,1)S(1)} %bitcast.33, ...), custom_call_target="tpu_custom_call" | custom-call | tf_op jit(solution)/shard_map/attend/pallas_call | solution.py:216
  78.7 0.0 copy-start
  78.7 18.0 %all_to_all.20.parts = f32[16,72,128]{2,1,0:T(8,128)S(1)} all-to-all(f32[16,72,128]{2,1,0:T(8,128)S(1)} %get-tuple-element.10), channel_id=1, replica_groups=mesh['agent'=16,'tensor'=16] {'agent'}, dimensions={0} | all-to-all | bytes 1179648 | tf_op jit(solution)/shard_map/all_to_all | solution.py:234
  96.7 0.0 copy-start.2
  96.7 0.4 combine.1
  97.1 11.7 %all_to_all.21.mine = bf16[8,32,256]{2,1,0:T(8,128)(2,1)S(1)} all-to-all(bf16[8,32,256]{2,1,0:T(8,128)(2,1)S(1)} %combine.1), channel_id=1, replica_groups={{0,2,4,6,8,10,12,14},{1,3,5,7,9,11,13,15},{16,18,20,22,24,26,28,30},{17..., dimensions={0} | all-to-all | bytes 262144 | tf_op jit(solution)/shard_map/all_to_all | solution.py:244
  108.8 3.1 %collective-permute-start.10 = (bf16[8,32,256]{2,1,0:T(8,128)(2,1)S(1)}, bf16[8,32,256]{2,1,0:T(8,128)(2,1)S(1)}, u32[]{:S(2)}, u32[]{:S(2)}) collective-permute-start(bf16[8,32,256]{2,1,0:T(8,128)(2,1)S(1)} %all_to_all.21.mine), channel_id=1, source_target_pairs={{0,1},{1,0},{2,3},{3,2},{4,5},{5,4},{6,7},{7,6},{8,9},{9,8},{10,11... | collective-permute-start | bytes 393224 | tf_op jit(solution)/shard_map/ppermute | solution.py:36
  112.0 1.0 collective-permute-done.10.theirs
  112.9 0.0 copy-done
  112.9 1.3 project.1
  114.3 10.6 %all_to_all.22.refs_0_ = f32[16,8,128]{2,1,0:T(8,128)S(1)} all-to-all(f32[16,8,128]{2,1,0:T(8,128)S(1)} %get-tuple-element.12), channel_id=1, replica_groups=mesh['agent'=16,'tensor'=16] {'tensor'}, dimensions={0} | all-to-all | bytes 131072 | tf_op jit(solution)/shard_map/all_to_all | solution.py:259
  124.9 0.0 copy-done.2
  124.9 0.2 finish.1
  125.1 13.8 %all_to_all.23 = bf16[16,32,512]{2,1,0:T(8,128)(2,1)S(1)} all-to-all(bf16[16,32,512]{2,1,0:T(8,128)(2,1)S(1)} %finish.1), channel_id=1, replica_groups=mesh['agent'=16,'tensor'=16] {'agent'}, dimensions={0} | all-to-all | bytes 1048576 | tf_op jit(solution)/shard_map/all_to_all | solution.py:268
  138.8 0.9 fusion
  (5 shorter events, 0.1 us)
Async XLA Ops:
  7.2 9.4 %copy-start.5 = (bf16[256,256]{1,0:T(8,128)(2,1)S(1)}, bf16[256,256]{1,0:T(8,128)(2,1)}, u32[]{:S(2)}) copy-start(bf16[256,256]{1,0:T(8,128)(2,1)} %param.11) | copy-start | bytes 393220
  7.2 9.4 %copy-start.6 = (bf16[256,256]{1,0:T(8,128)(2,1)S(1)}, bf16[256,256]{1,0:T(8,128)(2,1)}, u32[]{:S(2)}) copy-start(bf16[256,256]{1,0:T(8,128)(2,1)} %param.12) | copy-start | bytes 393220
  7.2 3.9 %copy-start.3 = (bf16[256,256]{1,0:T(8,128)(2,1)S(1)}, bf16[256,256]{1,0:T(8,128)(2,1)}, u32[]{:S(2)}) copy-start(bf16[256,256]{1,0:T(8,128)(2,1)} %param.13) | copy-start | bytes 393220
  7.2 4.0 %copy-start.4 = (bf16[256,256]{1,0:T(8,128)(2,1)S(1)}, bf16[256,256]{1,0:T(8,128)(2,1)}, u32[]{:S(2)}) copy-start(bf16[256,256]{1,0:T(8,128)(2,1)} %param.14) | copy-start | bytes 393220
  7.2 62.8 %all-gather.3.cloned.1.call-start = ((), (), s32[]{:S(2)}) async-start(), calls=%async_computation.4 | async-start | bytes 8912896 | tf_op jit(solution)/shard_map/all_gather | solution.py:211
  11.2 10.5 %collective-permute-start = (bf16[1024,256]{1,0:T(8,128)(2,1)S(1)}, bf16[1024,256]{1,0:T(8,128)(2,1)S(1)}, u32[]{:S(2)}, u32[]{:S(2)}) collective-permute-start(bf16[1024,256]{1,0:T(8,128)(2,1)S(1)} %get-tuple-element.16), channel_id=1, source_target_pairs={{0,16},{1,65},{2,18},{3,67},{4,20},{5,69},{6,22},{7,71},{8,24},{9,... | collective-permute-start | bytes 1572872 | tf_op jit(solution)/shard_map/ppermute | solution.py:26
  13.4 15.1 %collective-permute-start.1 = (bf16[1024,256]{1,0:T(8,128)(2,1)S(1)}, bf16[1024,256]{1,0:T(8,128)(2,1)S(1)}, u32[]{:S(2)}, u32[]{:S(2)}) collective-permute-start(bf16[1024,256]{1,0:T(8,128)(2,1)S(1)} %get-tuple-element.16), channel_id=1, source_target_pairs={{0,48},{1,193},{2,50},{3,195},{4,52},{5,197},{6,54},{7,199},{8,56}... | collective-permute-start | bytes 1572872 | tf_op jit(solution)/shard_map/ppermute | solution.py:26
  14.9 10.7 %collective-permute-start.3 = (bf16[512,256]{1,0:T(8,128)(2,1)S(1)}, bf16[512,256]{1,0:T(8,128)(2,1)S(1)}, u32[]{:S(2)}, u32[]{:S(2)}) collective-permute-start(bf16[512,256]{1,0:T(8,128)(2,1)S(1)} %pad_maximum_fusion.3), channel_id=1, source_target_pairs={{0,32},{1,129},{2,34},{3,131},{4,36},{5,133},{6,38},{7,135},{8,40}... | collective-permute-start | bytes 786440 | tf_op jit(solution)/shard_map/ppermute | solution.py:26
  16.6 53.4 %copy-start.1 = (s32[512]{0:T(512)S(1)}, s32[512]{0:T(512)}, u32[]{:S(2)}) copy-start(s32[512]{0:T(512)} %param.9) | copy-start | bytes 6148
  16.6 11.9 %collective-permute-start.2 = (bf16[512,256]{1,0:T(8,128)(2,1)S(1)}, bf16[512,256]{1,0:T(8,128)(2,1)S(1)}, u32[]{:S(2)}, u32[]{:S(2)}) collective-permute-start(bf16[512,256]{1,0:T(8,128)(2,1)S(1)} %pad_maximum_fusion.2), channel_id=1, source_target_pairs={{0,32},{1,129},{2,34},{3,131},{4,36},{5,133},{6,38},{7,135},{8,40}... | collective-permute-start | bytes 786440 | tf_op jit(solution)/shard_map/ppermute | solution.py:26
  28.6 15.3 %collective-permute-start.4 = (bf16[2048,256]{1,0:T(8,128)(2,1)S(1)}, bf16[2048,256]{1,0:T(8,128)(2,1)S(1)}, u32[]{:S(2)}, u32[]{:S(2)}) collective-permute-start(bf16[2048,256]{1,0:T(8,128)(2,1)S(1)} %constant_dynamic-update-slice_fusion.4), channel_id=1, source_target_pairs={{0,64},{1,17},{2,66},{3,19},{4,68},{5,21},{6,70},{7,23},{8,72},{9,... | collective-permute-start | bytes 3145736 | tf_op jit(solution)/shard_map/ppermute | solution.py:31
  29.6 14.3 %collective-permute-start.7 = (bf16[2048,256]{1,0:T(8,128)(2,1)S(1)}, bf16[2048,256]{1,0:T(8,128)(2,1)}, u32[]{:S(2)}, u32[]{:S(2)}) collective-permute-start(bf16[2048,256]{1,0:T(8,128)(2,1)S(1)} %pad_maximum_fusion), channel_id=1, source_target_pairs={{0,192},{1,49},{2,194},{3,51},{4,196},{5,53},{6,198},{7,55},{8,200... | collective-permute-start | bytes 3145736 | tf_op jit(solution)/shard_map/ppermute | solution.py:31
  31.3 23.5 %collective-permute-start.6 = (bf16[2048,256]{1,0:T(8,128)(2,1)S(1)}, bf16[2048,256]{1,0:T(8,128)(2,1)}, u32[]{:S(2)}, u32[]{:S(2)}) collective-permute-start(bf16[2048,256]{1,0:T(8,128)(2,1)S(1)} %constant_dynamic-update-slice_fusion.4), channel_id=1, source_target_pairs={{0,192},{1,49},{2,194},{3,51},{4,196},{5,53},{6,198},{7,55},{8,200... | collective-permute-start | bytes 3145736 | tf_op jit(solution)/shard_map/ppermute | solution.py:31
  32.6 22.5 %collective-permute-start.5 = (bf16[2048,256]{1,0:T(8,128)(2,1)S(1)}, bf16[2048,256]{1,0:T(8,128)(2,1)}, u32[]{:S(2)}, u32[]{:S(2)}) collective-permute-start(bf16[2048,256]{1,0:T(8,128)(2,1)S(1)} %pad_maximum_fusion), channel_id=1, source_target_pairs={{0,64},{1,17},{2,66},{3,19},{4,68},{5,21},{6,70},{7,23},{8,72},{9,... | collective-permute-start | bytes 3145736 | tf_op jit(solution)/shard_map/ppermute | solution.py:31
  43.9 22.5 %collective-permute-start.8 = (bf16[2048,256]{1,0:T(8,128)(2,1)S(1)}, bf16[2048,256]{1,0:T(8,128)(2,1)}, u32[]{:S(2)}, u32[]{:S(2)}) collective-permute-start(bf16[2048,256]{1,0:T(8,128)(2,1)S(1)} %collective-permute-done.4), channel_id=1, source_target_pairs={{0,64},{1,17},{2,66},{3,19},{4,68},{5,21},{6,70},{7,23},{8,72},{9,... | collective-permute-start | bytes 3145736 | tf_op jit(solution)/shard_map/ppermute | solution.py:31
  43.9 22.5 %collective-permute-start.9 = (bf16[2048,256]{1,0:T(8,128)(2,1)}, bf16[2048,256]{1,0:T(8,128)(2,1)}, u32[]{:S(2)}, u32[]{:S(2)}) collective-permute-start(bf16[2048,256]{1,0:T(8,128)(2,1)} %collective-permute-done.7), channel_id=1, source_target_pairs={{0,192},{1,49},{2,194},{3,51},{4,196},{5,53},{6,198},{7,55},{8,200... | collective-permute-start | bytes 3145736 | tf_op jit(solution)/shard_map/ppermute | solution.py:31
  78.7 34.2 %copy-start = (bf16[512,256]{1,0:T(8,128)(2,1)S(1)}, bf16[512,256]{1,0:T(8,128)(2,1)}, u32[]{:S(2)}) copy-start(bf16[512,256]{1,0:T(8,128)(2,1)} %latents.1) | copy-start | bytes 786436
  96.7 28.2 %copy-start.2 = (f32[256]{0:T(256)S(1)}, f32[256]{0:T(256)}, u32[]{:S(2)}) copy-start(f32[256]{0:T(256)} %param.15) | copy-start | bytes 3076
  108.8 4.1 %collective-permute-start.10 = (bf16[8,32,256]{2,1,0:T(8,128)(2,1)S(1)}, bf16[8,32,256]{2,1,0:T(8,128)(2,1)S(1)}, u32[]{:S(2)}, u32[]{:S(2)}) collective-permute-start(bf16[8,32,256]{2,1,0:T(8,128)(2,1)S(1)} %all_to_all.21.mine), channel_id=1, source_target_pairs={{0,1},{1,0},{2,3},{3,2},{4,5},{5,4},{6,7},{7,6},{8,9},{9,8},{10,11... | collective-permute-start | bytes 393224 | tf_op jit(solution)/shard_map/ppermute | solution.py:36
Sparse Core Ops, SparseCore 0:
  9.9 60.1 all-gather.2

commit v9 on v8

--- a/solution.py
+++ b/solution.py
@@ -69,7 +69,7 @@
 
 def attend_kernel(table, feats, *refs):
     w_refs = refs[:8]
-    valid, out, w_out, x_all, w_all, acc, stat, x_sem, w_sem, out_sem = refs[8:]
+    valid, latents, out, w_out, mine, x_all, w_all, acc, stat, x_sem, w_sem, out_sem, mine_sem = refs[8:]
     rows = feats.shape[1] // 2
     depth = feats.shape[2]
     parts = 8
@@ -90,6 +90,9 @@
             w_refs[n].at[:, 3], w_out.at[pl.ds(n * step, step)], out_sem.at[n])
         for n in range(2, parts)
     ]
+    chunk = mine.shape[0]
+    out_copies.append(pltpu.make_async_copy(
+        latents.at[pl.ds(pl.multiple_of(table[GROUP] * chunk, chunk), chunk)], mine, mine_sem))
     for copy in out_copies:
         copy.start()
     for n in range(2):
@@ -163,19 +166,15 @@
         out[t] = attended
 
 
-def project_kernel(table, mine, theirs, w_out, latents, upd, squares, rows, sem):
+def project_kernel(table, mine, theirs, w_out, rows, upd, squares):
     chunk, depth = upd.shape
-    agent, core = table[GROUP], table[GROUP + 1]
-    copy = pltpu.make_async_copy(
-        latents.at[pl.ds(pl.multiple_of(agent * chunk, chunk), chunk)], rows, sem)
-    copy.start()
+    core = table[GROUP + 1]
     lefts = []
     for slot in range(GROUP):
         block = table[slot]
         lefts.append(jnp.where(block % 2 == core, mine[block // 2], theirs[block // 2]))
     total = jnp.dot(jnp.concatenate(lefts, axis=1), w_out[...].reshape(GROUP * depth, depth),
                     preferred_element_type=F32)
-    copy.wait()
     total += rows[...].astype(F32)
     upd[...] = total
     square = jnp.sum(total * total, axis=1, keepdims=True)
@@ -213,12 +212,13 @@
     table = index_table()
     smem = pl.BlockSpec(memory_space=pltpu.SMEM)
     hbm = pl.BlockSpec(memory_space=pltpu.HBM)
-    partial, out_weight = pl.pallas_call(
+    partial, out_weight, share = pl.pallas_call(
         attend_kernel,
         out_shape=(jax.ShapeDtypeStruct((GROUP, 2 * chunk + 8, HEAD_DIM), F32),
-                   jax.ShapeDtypeStruct((GROUP, depth, depth), BF16)),
-        in_specs=[smem, hbm] + whole(2) + [hbm] * 6 + whole(1),
-        out_specs=tuple(whole(2)),
+                   jax.ShapeDtypeStruct((GROUP, depth, depth), BF16),
+                   jax.ShapeDtypeStruct((chunk, depth), BF16)),
+        in_specs=[smem, hbm] + whole(2) + [hbm] * 6 + whole(1) + [hbm],
+        out_specs=tuple(whole(3)),
         scratch_shapes=[
             pltpu.VMEM((2 * rows, GROUP * depth), BF16),
             pltpu.VMEM((3, GROUP, depth, depth), BF16),
@@ -227,10 +227,11 @@
             pltpu.SemaphoreType.DMA((GROUP,)),
             pltpu.SemaphoreType.DMA((3, 8)),
             pltpu.SemaphoreType.DMA((8,)),
+            pltpu.SemaphoreType.DMA,
         ],
         compiler_params=pltpu.CompilerParams(vmem_limit_bytes=40 * 2**20),
         name="attend",
-    )(table, feats, *weights, valid.reshape(1, rows))
+    )(table, feats, *weights, valid.reshape(1, rows), latents)
     partial = lax.all_to_all(partial, "agent", 0, 0)
     attended = pl.pallas_call(
         combine_kernel,
@@ -247,15 +248,11 @@
         project_kernel,
         out_shape=(jax.ShapeDtypeStruct((chunk, depth), F32),
                    jax.ShapeDtypeStruct((GROUP, 8, HEAD_DIM), F32)),
-        in_specs=[smem] + whole(3) + [hbm],
+        in_specs=[smem] + whole(4),
         out_specs=tuple(whole(2)),
-        scratch_shapes=[
-            pltpu.VMEM((chunk, depth), BF16),
-            pltpu.SemaphoreType.DMA,
-        ],
         compiler_params=pltpu.CompilerParams(vmem_limit_bytes=8 * 2**20),
         name="project",
-    )(table, attended, theirs, out_weight, latents)
+    )(table, attended, theirs, out_weight, share)
     squares = lax.all_to_all(squares, "tensor", 0, 0)
     out = pl.pallas_call(
         lambda *refs: finish_kernel(width, *refs),

time: 147 us -> 146 us (level)
  no operation moved by 1% of the time
where the time goes in v9:
time: 146 us
  blocking collectives  53.9 us (37%)
  waiting for transfers between devices  45.8 us (31%)
  starting transfers between devices  16.9 us (12%)
  between operations  14.2 us (10%)
  Pallas kernels  10.4 us (7%)
  local copies, waits for them, and re-layouts  2.91 us (2%)
  other arithmetic  2.08 us (1%)
    ppermute x6, waiting for transfers between devices, second(): lax.ppermute(array, ('agent', 'tensor'), pairs(lambda y, x, core: (y + by...  30.8 us
    all_to_all x1, blocking collectives, body(): partial = lax.all_to_all(partial, 'agent', 0, 0)  17.9 us
    all_to_all x1, blocking collectives, body(): out = lax.all_to_all(out, 'agent', 0, 0)  13.8 us
    all_to_all x1, blocking collectives, body(): lax.all_to_all(attended, 'tensor', 0, 0, axis_index_groups=same_core)  11.7 us
    all_to_all x1, blocking collectives, body(): squares = lax.all_to_all(squares, 'tensor', 0, 0)  10.6 us
    ppermute x4, waiting for transfers between devices, first(): lax.ppermute(array, ('agent', 'tensor'), pairs(lambda y, x, core: (y, x +...  10.3 us
    pallas_call x1, Pallas kernels, body(): pl.pallas_call(attend_kernel, out_shape=(jax.ShapeDtypeStruct((GROUP, 2 *...  8.69 us
    ppermute x6, starting transfers between devices, second(): lax.ppermute(array, ('agent', 'tensor'), pairs(lambda y, x, core: (y + by...  6.9 us
  transfers between devices with their start and end apart: 12, of which 9 were waited for; matrix products, arithmetic and copies ran while one was open for 1% of the time, Pallas kernels for 0%

profile of v9, /device:TPU:1, one launch (start us, length us, event | category | flops | bytes accessed | tf_op | source)
XLA Modules:
  0.0 146.2 jit_solution(4255155029885178529)
XLA Ops:
  7.2 0.0 copy-start.5
  7.2 0.0 copy-start.6
  7.2 0.0 copy-start.3
  7.2 0.0 copy-start.4
  7.2 0.0 all-gather.3.cloned.1.call-start
  7.3 2.0 %pad_maximum_fusion.1 = bf16[1024,256]{1,0:T(8,128)(2,1)} fusion(bf16[512,256]{1,0:T(8,128)(2,1)} %refs_9_.1, bf16[512,256]{1,0:T(8,128)(2,1)} %param.8), kind=kLoop, calls=%fused_computation.1 | loop fusion | flops 1048576 | bytes 1048576 | tf_op jit(solution)/shard_map/concatenate | solution.py:209
  9.2 0.0 all-gather.3.cloned.1.call-update
  9.3 0.9 constant_dynamic-update-slice_fusion.3
  10.2 0.9 constant_dynamic-update-slice_fusion.2
  11.1 0.0 copy-done.3
  11.2 0.0 copy-done.4
  11.2 2.2 %collective-permute-start = (bf16[1024,256]{1,0:T(8,128)(2,1)S(1)}, bf16[1024,256]{1,0:T(8,128)(2,1)S(1)}, u32[]{:S(2)}, u32[]{:S(2)}) collective-permute-start(bf16[1024,256]{1,0:T(8,128)(2,1)S(1)} %get-tuple-element.18), channel_id=1, source_target_pairs={{0,16},{1,65},{2,18},{3,67},{4,20},{5,69},{6,22},{7,71},{8,24},{9,... | collective-permute-start | bytes 1572872 | tf_op jit(solution)/shard_map/ppermute | solution.py:26
  13.4 1.5 %collective-permute-start.1 = (bf16[1024,256]{1,0:T(8,128)(2,1)S(1)}, bf16[1024,256]{1,0:T(8,128)(2,1)S(1)}, u32[]{:S(2)}, u32[]{:S(2)}) collective-permute-start(bf16[1024,256]{1,0:T(8,128)(2,1)S(1)} %get-tuple-element.18), channel_id=1, source_target_pairs={{0,48},{1,193},{2,50},{3,195},{4,52},{5,197},{6,54},{7,199},{8,56}... | collective-permute-start | bytes 1572872 | tf_op jit(solution)/shard_map/ppermute | solution.py:26
  14.9 1.6 %collective-permute-start.3 = (bf16[512,256]{1,0:T(8,128)(2,1)S(1)}, bf16[512,256]{1,0:T(8,128)(2,1)S(1)}, u32[]{:S(2)}, u32[]{:S(2)}) collective-permute-start(bf16[512,256]{1,0:T(8,128)(2,1)S(1)} %pad_maximum_fusion.3), channel_id=1, source_target_pairs={{0,32},{1,129},{2,34},{3,131},{4,36},{5,133},{6,38},{7,135},{8,40}... | collective-permute-start | bytes 786440 | tf_op jit(solution)/shard_map/ppermute | solution.py:26
  16.6 0.0 copy-done.5
  16.6 0.0 copy-done.6
  16.6 0.0 copy-start
  16.6 0.0 copy-start.1
  16.6 1.5 %collective-permute-start.2 = (bf16[512,256]{1,0:T(8,128)(2,1)S(1)}, bf16[512,256]{1,0:T(8,128)(2,1)S(1)}, u32[]{:S(2)}, u32[]{:S(2)}) collective-permute-start(bf16[512,256]{1,0:T(8,128)(2,1)S(1)} %pad_maximum_fusion.2), channel_id=1, source_target_pairs={{0,32},{1,129},{2,34},{3,131},{4,36},{5,133},{6,38},{7,135},{8,40}... | collective-permute-start | bytes 786440 | tf_op jit(solution)/shard_map/ppermute | solution.py:26
  18.1 3.6 %collective-permute-done = bf16[1024,256]{1,0:T(8,128)(2,1)S(1)} collective-permute-done((bf16[1024,256]{1,0:T(8,128)(2,1)S(1)}, bf16[1024,256]{1,0:T(8,128)(2,1)S(1)}, u32[]{:S(2)}, u32[]{:S(2)}) %collective-permute-start) | collective-permute-done | bytes 524320 | tf_op jit(solution)/shard_map/ppermute | solution.py:26
  21.7 3.9 %collective-permute-done.3 = bf16[512,256]{1,0:T(8,128)(2,1)S(1)} collective-permute-done((bf16[512,256]{1,0:T(8,128)(2,1)S(1)}, bf16[512,256]{1,0:T(8,128)(2,1)S(1)}, u32[]{:S(2)}, u32[]{:S(2)}) %collective-permute-start.3) | collective-permute-done | bytes 262176 | tf_op jit(solution)/shard_map/ppermute | solution.py:26
  25.7 2.8 %collective-permute-done.2 = bf16[512,256]{1,0:T(8,128)(2,1)S(1)} collective-permute-done((bf16[512,256]{1,0:T(8,128)(2,1)S(1)}, bf16[512,256]{1,0:T(8,128)(2,1)S(1)}, u32[]{:S(2)}, u32[]{:S(2)}) %collective-permute-start.2) | collective-permute-done | bytes 262176 | tf_op jit(solution)/shard_map/ppermute | solution.py:26
  28.5 0.0 collective-permute-done.1
  28.5 0.1 pad_maximum_fusion
  28.6 1.0 collective-permute-start.4
  29.6 1.8 %collective-permute-start.7 = (bf16[2048,256]{1,0:T(8,128)(2,1)S(1)}, bf16[2048,256]{1,0:T(8,128)(2,1)}, u32[]{:S(2)}, u32[]{:S(2)}) collective-permute-start(bf16[2048,256]{1,0:T(8,128)(2,1)S(1)} %pad_maximum_fusion), channel_id=1, source_target_pairs={{0,192},{1,49},{2,194},{3,51},{4,196},{5,53},{6,198},{7,55},{8,200... | collective-permute-start | bytes 3145736 | tf_op jit(solution)/shard_map/ppermute | solution.py:31
  31.3 1.3 collective-permute-start.6
  32.6 0.2 collective-permute-start.5
  32.8 11.1 %collective-permute-done.4 = bf16[2048,256]{1,0:T(8,128)(2,1)S(1)} collective-permute-done((bf16[2048,256]{1,0:T(8,128)(2,1)S(1)}, bf16[2048,256]{1,0:T(8,128)(2,1)S(1)}, u32[]{:S(2)}, u32[]{:S(2)}) %collective-permute-start.4) | collective-permute-done | bytes 1048608 | tf_op jit(solution)/shard_map/ppermute | solution.py:31
  43.9 0.0 collective-permute-start.8
  43.9 0.0 collective-permute-done.7
  43.9 2.7 %collective-permute-start.9 = (bf16[2048,256]{1,0:T(8,128)(2,1)}, bf16[2048,256]{1,0:T(8,128)(2,1)}, u32[]{:S(2)}, u32[]{:S(2)}) collective-permute-start(bf16[2048,256]{1,0:T(8,128)(2,1)} %collective-permute-done.7), channel_id=1, source_target_pairs={{0,192},{1,49},{2,194},{3,51},{4,196},{5,53},{6,198},{7,55},{8,200... | collective-permute-start | bytes 3145736 | tf_op jit(solution)/shard_map/ppermute | solution.py:31
  46.6 0.1 stack.75.table
  46.7 8.2 %collective-permute-done.6 = bf16[2048,256]{1,0:T(8,128)(2,1)} collective-permute-done((bf16[2048,256]{1,0:T(8,128)(2,1)S(1)}, bf16[2048,256]{1,0:T(8,128)(2,1)}, u32[]{:S(2)}, u32[]{:S(2)}) %collective-permute-start.6) | collective-permute-done | bytes 1048608 | tf_op jit(solution)/shard_map/ppermute | solution.py:31
  54.8 0.3 collective-permute-done.5
  55.1 11.2 %collective-permute-done.8 = bf16[2048,256]{1,0:T(8,128)(2,1)} collective-permute-done((bf16[2048,256]{1,0:T(8,128)(2,1)S(1)}, bf16[2048,256]{1,0:T(8,128)(2,1)}, u32[]{:S(2)}, u32[]{:S(2)}) %collective-permute-start.8) | collective-permute-done | bytes 1048608 | tf_op jit(solution)/shard_map/ppermute | solution.py:31
  66.4 0.0 collective-permute-done.9
  66.4 3.7 %all-gather.3.cloned.1.call-done = bf16[16384,256]{1,0:T(8,128)(2,1)} async-done(((bf16[1024,256]{1,0:T(8,128)(2,1)}), bf16[16384,256]{1,0:T(8,128)(2,1)}) %all-gather.3.cloned.1.call-update) | async-done | bytes 8388624 | tf_op jit(solution)/shard_map/all_gather | solution.py:210
  70.0 0.0 copy-done
  70.0 0.0 copy-done.1
  70.0 8.7 %attend.1 = (f32[16,72,128]{2,1,0:T(8,128)S(1)}, bf16[16,256,256]{2,1,0:T(8,128)(2,1)S(1)}, bf16[32,256]{1,0:T(8,128)(2,1)S(1)}) custom-call(s32[18]{0:T(128)S(1)} %stack.75.table, bf16[16,1024,256]{2,1,0:T(8,128)(2,1)} %bitcast.36, bf16[2,4,256,256]{3,2,1,0:T(8,128)(2,1)S(1)} %bitcast.32, bf16[2,4,256,256]{3,2,1,0:T(8,128)(2,1)S(1)} %bitcast.31, ...), custom_call_target="tpu_custom_call" | custom-call | tf_op jit(solution)/shard_map/attend/pallas_call | solution.py:215
  78.7 0.0 copy-start.2
  78.7 17.9 %all_to_all.20.parts = f32[16,72,128]{2,1,0:T(8,128)S(1)} all-to-all(f32[16,72,128]{2,1,0:T(8,128)S(1)} %get-tuple-element.11), channel_id=1, replica_groups=mesh['agent'=16,'tensor'=16] {'agent'}, dimensions={0} | all-to-all | bytes 1179648 | tf_op jit(solution)/shard_map/all_to_all | solution.py:235
  96.6 0.4 combine.1
  97.0 11.7 %all_to_all.21.mine = bf16[8,32,256]{2,1,0:T(8,128)(2,1)S(1)} all-to-all(bf16[8,32,256]{2,1,0:T(8,128)(2,1)S(1)} %combine.1), channel_id=1, replica_groups={{0,2,4,6,8,10,12,14},{1,3,5,7,9,11,13,15},{16,18,20,22,24,26,28,30},{17..., dimensions={0} | all-to-all | bytes 262144 | tf_op jit(solution)/shard_map/all_to_all | solution.py:245
  108.7 3.1 %collective-permute-start.10 = (bf16[8,32,256]{2,1,0:T(8,128)(2,1)S(1)}, bf16[8,32,256]{2,1,0:T(8,128)(2,1)S(1)}, u32[]{:S(2)}, u32[]{:S(2)}) collective-permute-start(bf16[8,32,256]{2,1,0:T(8,128)(2,1)S(1)} %all_to_all.21.mine), channel_id=1, source_target_pairs={{0,1},{1,0},{2,3},{3,2},{4,5},{5,4},{6,7},{7,6},{8,9},{9,8},{10,11... | collective-permute-start | bytes 393224 | tf_op jit(solution)/shard_map/ppermute | solution.py:36
  111.8 1.0 collective-permute-done.10.theirs
  112.8 1.1 project.1
  113.9 10.6 %all_to_all.22.refs_0_ = f32[16,8,128]{2,1,0:T(8,128)S(1)} all-to-all(f32[16,8,128]{2,1,0:T(8,128)S(1)} %get-tuple-element.14), channel_id=1, replica_groups=mesh['agent'=16,'tensor'=16] {'tensor'}, dimensions={0} | all-to-all | bytes 131072 | tf_op jit(solution)/shard_map/all_to_all | solution.py:256
  124.5 0.0 copy-done.2
  124.5 0.2 finish.1
  124.7 13.8 %all_to_all.23 = bf16[16,32,512]{2,1,0:T(8,128)(2,1)S(1)} all-to-all(bf16[16,32,512]{2,1,0:T(8,128)(2,1)S(1)} %finish.1), channel_id=1, replica_groups=mesh['agent'=16,'tensor'=16] {'agent'}, dimensions={0} | all-to-all | bytes 1048576 | tf_op jit(solution)/shard_map/all_to_all | solution.py:265
  138.5 0.9 fusion
  (5 shorter events, 0.1 us)
Async XLA Ops:
  7.2 9.4 %copy-start.5 = (bf16[256,256]{1,0:T(8,128)(2,1)S(1)}, bf16[256,256]{1,0:T(8,128)(2,1)}, u32[]{:S(2)}) copy-start(bf16[256,256]{1,0:T(8,128)(2,1)} %param.11) | copy-start | bytes 393220
  7.2 9.4 %copy-start.6 = (bf16[256,256]{1,0:T(8,128)(2,1)S(1)}, bf16[256,256]{1,0:T(8,128)(2,1)}, u32[]{:S(2)}) copy-start(bf16[256,256]{1,0:T(8,128)(2,1)} %param.12) | copy-start | bytes 393220
  7.2 3.9 %copy-start.3 = (bf16[256,256]{1,0:T(8,128)(2,1)S(1)}, bf16[256,256]{1,0:T(8,128)(2,1)}, u32[]{:S(2)}) copy-start(bf16[256,256]{1,0:T(8,128)(2,1)} %param.13) | copy-start | bytes 393220
  7.2 4.0 %copy-start.4 = (bf16[256,256]{1,0:T(8,128)(2,1)S(1)}, bf16[256,256]{1,0:T(8,128)(2,1)}, u32[]{:S(2)}) copy-start(bf16[256,256]{1,0:T(8,128)(2,1)} %param.14) | copy-start | bytes 393220
  7.2 62.8 %all-gather.3.cloned.1.call-start = ((), (), s32[]{:S(2)}) async-start(), calls=%async_computation.4 | async-start | bytes 8912896 | tf_op jit(solution)/shard_map/all_gather | solution.py:210
  11.2 10.5 %collective-permute-start = (bf16[1024,256]{1,0:T(8,128)(2,1)S(1)}, bf16[1024,256]{1,0:T(8,128)(2,1)S(1)}, u32[]{:S(2)}, u32[]{:S(2)}) collective-permute-start(bf16[1024,256]{1,0:T(8,128)(2,1)S(1)} %get-tuple-element.18), channel_id=1, source_target_pairs={{0,16},{1,65},{2,18},{3,67},{4,20},{5,69},{6,22},{7,71},{8,24},{9,... | collective-permute-start | bytes 1572872 | tf_op jit(solution)/shard_map/ppermute | solution.py:26
  13.4 15.1 %collective-permute-start.1 = (bf16[1024,256]{1,0:T(8,128)(2,1)S(1)}, bf16[1024,256]{1,0:T(8,128)(2,1)S(1)}, u32[]{:S(2)}, u32[]{:S(2)}) collective-permute-start(bf16[1024,256]{1,0:T(8,128)(2,1)S(1)} %get-tuple-element.18), channel_id=1, source_target_pairs={{0,48},{1,193},{2,50},{3,195},{4,52},{5,197},{6,54},{7,199},{8,56}... | collective-permute-start | bytes 1572872 | tf_op jit(solution)/shard_map/ppermute | solution.py:26
  14.9 10.7 %collective-permute-start.3 = (bf16[512,256]{1,0:T(8,128)(2,1)S(1)}, bf16[512,256]{1,0:T(8,128)(2,1)S(1)}, u32[]{:S(2)}, u32[]{:S(2)}) collective-permute-start(bf16[512,256]{1,0:T(8,128)(2,1)S(1)} %pad_maximum_fusion.3), channel_id=1, source_target_pairs={{0,32},{1,129},{2,34},{3,131},{4,36},{5,133},{6,38},{7,135},{8,40}... | collective-permute-start | bytes 786440 | tf_op jit(solution)/shard_map/ppermute | solution.py:26
  16.6 53.4 %copy-start = (bf16[512,256]{1,0:T(8,128)(2,1)S(1)}, bf16[512,256]{1,0:T(8,128)(2,1)}, u32[]{:S(2)}) copy-start(bf16[512,256]{1,0:T(8,128)(2,1)} %refs_9_.1) | copy-start | bytes 786436
  16.6 53.4 %copy-start.1 = (s32[512]{0:T(512)S(1)}, s32[512]{0:T(512)}, u32[]{:S(2)}) copy-start(s32[512]{0:T(512)} %param.9) | copy-start | bytes 6148
  16.6 11.9 %collective-permute-start.2 = (bf16[512,256]{1,0:T(8,128)(2,1)S(1)}, bf16[512,256]{1,0:T(8,128)(2,1)S(1)}, u32[]{:S(2)}, u32[]{:S(2)}) collective-permute-start(bf16[512,256]{1,0:T(8,128)(2,1)S(1)} %pad_maximum_fusion.2), channel_id=1, source_target_pairs={{0,32},{1,129},{2,34},{3,131},{4,36},{5,133},{6,38},{7,135},{8,40}... | collective-permute-start | bytes 786440 | tf_op jit(solution)/shard_map/ppermute | solution.py:26
  28.6 15.3 %collective-permute-start.4 = (bf16[2048,256]{1,0:T(8,128)(2,1)S(1)}, bf16[2048,256]{1,0:T(8,128)(2,1)S(1)}, u32[]{:S(2)}, u32[]{:S(2)}) collective-permute-start(bf16[2048,256]{1,0:T(8,128)(2,1)S(1)} %constant_dynamic-update-slice_fusion.4), channel_id=1, source_target_pairs={{0,64},{1,17},{2,66},{3,19},{4,68},{5,21},{6,70},{7,23},{8,72},{9,... | collective-permute-start | bytes 3145736 | tf_op jit(solution)/shard_map/ppermute | solution.py:31
  29.6 14.3 %collective-permute-start.7 = (bf16[2048,256]{1,0:T(8,128)(2,1)S(1)}, bf16[2048,256]{1,0:T(8,128)(2,1)}, u32[]{:S(2)}, u32[]{:S(2)}) collective-permute-start(bf16[2048,256]{1,0:T(8,128)(2,1)S(1)} %pad_maximum_fusion), channel_id=1, source_target_pairs={{0,192},{1,49},{2,194},{3,51},{4,196},{5,53},{6,198},{7,55},{8,200... | collective-permute-start | bytes 3145736 | tf_op jit(solution)/shard_map/ppermute | solution.py:31
  31.3 23.5 %collective-permute-start.6 = (bf16[2048,256]{1,0:T(8,128)(2,1)S(1)}, bf16[2048,256]{1,0:T(8,128)(2,1)}, u32[]{:S(2)}, u32[]{:S(2)}) collective-permute-start(bf16[2048,256]{1,0:T(8,128)(2,1)S(1)} %constant_dynamic-update-slice_fusion.4), channel_id=1, source_target_pairs={{0,192},{1,49},{2,194},{3,51},{4,196},{5,53},{6,198},{7,55},{8,200... | collective-permute-start | bytes 3145736 | tf_op jit(solution)/shard_map/ppermute | solution.py:31
  32.6 22.5 %collective-permute-start.5 = (bf16[2048,256]{1,0:T(8,128)(2,1)S(1)}, bf16[2048,256]{1,0:T(8,128)(2,1)}, u32[]{:S(2)}, u32[]{:S(2)}) collective-permute-start(bf16[2048,256]{1,0:T(8,128)(2,1)S(1)} %pad_maximum_fusion), channel_id=1, source_target_pairs={{0,64},{1,17},{2,66},{3,19},{4,68},{5,21},{6,70},{7,23},{8,72},{9,... | collective-permute-start | bytes 3145736 | tf_op jit(solution)/shard_map/ppermute | solution.py:31
  43.9 22.5 %collective-permute-start.8 = (bf16[2048,256]{1,0:T(8,128)(2,1)S(1)}, bf16[2048,256]{1,0:T(8,128)(2,1)}, u32[]{:S(2)}, u32[]{:S(2)}) collective-permute-start(bf16[2048,256]{1,0:T(8,128)(2,1)S(1)} %collective-permute-done.4), channel_id=1, source_target_pairs={{0,64},{1,17},{2,66},{3,19},{4,68},{5,21},{6,70},{7,23},{8,72},{9,... | collective-permute-start | bytes 3145736 | tf_op jit(solution)/shard_map/ppermute | solution.py:31
  43.9 22.5 %collective-permute-start.9 = (bf16[2048,256]{1,0:T(8,128)(2,1)}, bf16[2048,256]{1,0:T(8,128)(2,1)}, u32[]{:S(2)}, u32[]{:S(2)}) collective-permute-start(bf16[2048,256]{1,0:T(8,128)(2,1)} %collective-permute-done.7), channel_id=1, source_target_pairs={{0,192},{1,49},{2,194},{3,51},{4,196},{5,53},{6,198},{7,55},{8,200... | collective-permute-start | bytes 3145736 | tf_op jit(solution)/shard_map/ppermute | solution.py:31
  78.7 45.8 %copy-start.2 = (f32[256]{0:T(256)S(1)}, f32[256]{0:T(256)}, u32[]{:S(2)}) copy-start(f32[256]{0:T(256)} %param.15) | copy-start | bytes 3076
  108.7 4.1 %collective-permute-start.10 = (bf16[8,32,256]{2,1,0:T(8,128)(2,1)S(1)}, bf16[8,32,256]{2,1,0:T(8,128)(2,1)S(1)}, u32[]{:S(2)}, u32[]{:S(2)}) collective-permute-start(bf16[8,32,256]{2,1,0:T(8,128)(2,1)S(1)} %all_to_all.21.mine), channel_id=1, source_target_pairs={{0,1},{1,0},{2,3},{3,2},{4,5},{5,4},{6,7},{7,6},{8,9},{9,8},{10,11... | collective-permute-start | bytes 393224 | tf_op jit(solution)/shard_map/ppermute | solution.py:36
Sparse Core Ops, SparseCore 0:
  9.9 60.1 all-gather.2
